TPU v7x, 32 devices: a whole 2x2x4 slice. The times are simulated.
32 devices in a mesh: kt: 8 (over y, x, core), en: 4 (over z).
Axes of the slice: x: 2, y: 2, z: 4, core: 2. Of those that a mesh axis runs over, the one named last changes fastest.
Arguments:
- counts: int32 [8], P('kt'), may hold values from 1 to 4, 16 in all
- contact_slabs: int32 [2], replicated, may hold values from 0 to 15
- onsite: float32 [16, 384], P('en'), may hold values from -0.5 to 0.5
- hopping: float32 [16, 384], P('en'), may hold values from 0.1 to 0.5
- potential_in: float32 [16, 384], P('en'), may hold values from -2 to 2
- couple_base: bfloat16 [16, 384, 384], P('en'), may hold values from -0.25 to 0.25
- couple_wave: bfloat16 [16, 384, 384], P('en'), may hold values from -0.25 to 0.25
- doping: float32 [16, 384], P('en'), may hold values from 0 to 2
- poisson_inverse: float32 [384, 384], replicated, may hold values from -0.3125 to 0.3125
Outputs:
- electron_populace: float32 [16, 384], P('en')
- potential_out: float32 [16, 384], P('en')
Inputs may be any that keep to these rules, and one draw needn't show every extreme that they name: counts sum to 16 and the largest is 4.
All inputs are finite; a program needn't handle non-finite values. No bound on the sum of `counts` on one device may be relied on, other than what follows from the above.
Results may differ from a plain program's by a relative error of at most 0.00045.
Values may be sent and summed in bfloat16 or wider, within the bound.
No kernel may reach another device: no remote copies, remote signals or barrier semaphores. Data moves between devices by JAX's collectives and lax.ppermute only.
A program may use at most 64 MiB of HBM per device.

v0:
```python
import jax
import jax.numpy as jnp
from jax import lax
from jax.sharding import PartitionSpec as P

EMAX = 4


bottom_sample_mark = -1.0
sample_gap = 0.25
electrode_filling = -0.5
boltzmann_spread = 0.1
broadening = 1.0
contact_width = 0.5


def from_behind(block, axis, distance):
    devices = range(lax.axis_size(axis))
    route = [(i - distance, i) for i in devices if i - distance in devices]
    return lax.ppermute(block, axis, route)


def entry_amounts(transverse_impulse, eigen_height, impulse_count):
    wave_vector_number = jnp.pi * (transverse_impulse.astype(jnp.float32) + 0.5) / impulse_count
    angular_projection = jnp.cos(wave_vector_number)
    occupancy_mark = bottom_sample_mark + sample_gap * eigen_height.astype(jnp.float32)
    summation_multiplier = (
        sample_gap
        / (1.0 + jnp.exp((occupancy_mark - electrode_filling) / boltzmann_spread))
        / jnp.pi
    )
    return (angular_projection, occupancy_mark, summation_multiplier)


def slab_step(carried, couple_base, couple_wave, angular_projection, diag_real, diag_imag):
    coupled = (
        couple_base.astype(jnp.float32) + angular_projection * couple_wave.astype(jnp.float32)
    ).astype(jnp.bfloat16)
    left_part = jnp.einsum(
        "rm,pmn->prn", coupled, carried, preferred_element_type=jnp.float32
    ).astype(jnp.bfloat16)
    self_energy = jnp.einsum("prn,cn->prc", left_part, coupled, preferred_element_type=jnp.float32)
    magnitude = diag_real * diag_real + diag_imag * diag_imag
    inv_real = diag_real / magnitude
    inv_imag = -diag_imag / magnitude
    half_real = inv_real[:, None] * self_energy[0] - inv_imag[:, None] * self_energy[1]
    half_imag = inv_real[:, None] * self_energy[1] + inv_imag[:, None] * self_energy[0]
    identity = jnp.eye(diag_real.shape[0], dtype=jnp.float32)
    green_real = (
        half_real * inv_real[None, :] - half_imag * inv_imag[None, :] + identity * inv_real[None, :]
    )
    green_imag = (
        half_real * inv_imag[None, :] + half_imag * inv_real[None, :] + identity * inv_imag[None, :]
    )
    return (jnp.stack([green_real, green_imag]).astype(jnp.bfloat16), -jnp.diagonal(green_imag))


def slab_chain(carried, item_cos, item_energy, item_weight, tables):

    def one_slab(blocks, slab_row):
        couple_one, wave_one, real_row, hop_row, imag_value = slab_row
        diag_real = item_energy + real_row - item_cos * hop_row
        imag_row = jnp.full(real_row.shape, 1.0, jnp.float32) * imag_value
        blocks, diag_part = slab_step(blocks, couple_one, wave_one, item_cos, diag_real, imag_row)
        return (blocks, item_weight * diag_part)

    return lax.scan(one_slab, carried, tables)


def body(
    counts,
    contact_slabs,
    onsite,
    hopping,
    potential_in,
    couple_base,
    couple_wave,
    doping,
    poisson_inverse,
):
    kt_size = lax.axis_size("kt")
    en_size = lax.axis_size("en")
    position = lax.axis_index("en")
    mom_dev = counts.shape[0]
    impulse_count = mom_dev * kt_size
    slab_dev = onsite.shape[0]
    orbitals = onsite.shape[1]
    slot_index = jnp.arange(mom_dev * EMAX, dtype=jnp.int32)
    slot_momentum = slot_index // EMAX
    eigen_height = slot_index % EMAX
    transverse_impulse = lax.axis_index("kt") * mom_dev + slot_momentum
    selector = (jnp.arange(mom_dev, dtype=jnp.int32)[None, :] == slot_momentum[:, None]).astype(
        jnp.int32
    )
    live_count = jnp.sum(selector * counts[None, :], axis=1)
    live_mask = (eigen_height < live_count).astype(jnp.float32)
    angular_projection, occupancy_mark, summation_multiplier = entry_amounts(
        transverse_impulse, eigen_height, impulse_count
    )
    summation_multiplier = summation_multiplier * live_mask
    item_total = angular_projection.shape[0]
    real_base = -onsite - potential_in
    slab_ids = position * slab_dev + jnp.arange(slab_dev, dtype=jnp.int32)
    contact_flag = jnp.any(slab_ids[:, None] == contact_slabs[None, :], axis=1).astype(jnp.float32)
    diag_imag = broadening + contact_width * contact_flag
    tables = (couple_base, couple_wave, real_base, hopping, diag_imag)
    group_count = item_total // item_total
    section_count = group_count + en_size - 1

    def step_forward(injected_from_lead, first_item):

        def each_entry_share(values):
            carried, item_cos, item_energy, item_weight = values
            return slab_chain(carried, item_cos, item_energy, item_weight, tables)

        emitted_flux, parts = lax.map(
            each_entry_share,
            (injected_from_lead, angular_projection, occupancy_mark, summation_multiplier),
        )
        return (emitted_flux, jnp.sum(parts, axis=0))

    def stand_still(injected_from_lead, first_item):
        return (jnp.zeros_like(injected_from_lead), jnp.zeros((slab_dev, orbitals), jnp.float32))

    def section_body(section, carry):
        injected_from_lead, density_now = carry
        group_turn = section - position
        active = jnp.logical_and(group_turn >= 0, group_turn < group_count)
        first_item = jnp.clip(group_turn, 0, group_count - 1) * item_total
        emitted_flux, density_part = lax.cond(
            active, step_forward, stand_still, injected_from_lead, first_item
        )
        injected_from_lead = from_behind(emitted_flux, "en", 1)
        return (injected_from_lead, density_now + density_part)

    start_blocks = jnp.zeros((item_total, 2, orbitals, orbitals), jnp.bfloat16)
    start_density = jnp.zeros((slab_dev, orbitals), jnp.float32)
    last_blocks, electron_populace = lax.fori_loop(
        0, section_count, section_body, (start_blocks, start_density)
    )
    summed = lax.psum(electron_populace, "kt")
    potential_out = jnp.dot(summed - doping, poisson_inverse.T, precision=lax.Precision.HIGHEST)
    return (summed, potential_out)


def solution(mesh):
    return jax.shard_map(
        body,
        mesh=mesh,
        in_specs=(
            P("kt"),
            P(),
            P("en", None),
            P("en", None),
            P("en", None),
            P("en", None, None),
            P("en", None, None),
            P("en", None),
            P(),
        ),
        out_specs=(P("en", None), P("en", None)),
        check_vma=False,
    )
```

profile of v0, /device:TPU:24, one launch (start us, length us, event | category | flops | bytes accessed | tf_op | source)
XLA Modules:
  0.0 1077.9 jit_solution(15134780117669656087)
XLA Ops:
  3.9 1060.8 %while.42 = (s32[]{:T(128)}, bf16[4,2,384,384]{3,2,1,0:T(8,128)(2,1)}, f32[4,384]{1,0:T(4,128)S(1)}, s32[]{:T(128)}, f32[4,384]{1,0:T(4,128)S(1)}, /*index=5*/f3...) while((s32[]{:T(128)}, ...), condition=%wide.region_9.10_spmd.clone, body=%wide.region_1.9_spmd.clone.sunk | while | flops 459634752 | bytes 19570456 | solution.py:138
  6.9 53.9 %collective-permute-done = bf16[4,2,384,384]{3,2,1,0:T(8,128)(2,1)} collective-permute-done((bf16[4,2,384,384]{3,2,1,0:T(8,128)(2,1)}, bf16[4,2,384,384]{3,2,1,0:T(8,128)(2,1)}, u32[]{:S(2)}, u32[]{:S(2)}) %collective-permute-start) | collective-permute-done | bytes 2359328 | tf_op jit(solution)/shard_map/while/body/eval_jaxpr/ppermute | solution.py:20
  63.7 53.0 %collective-permute-done = bf16[4,2,384,384]{3,2,1,0:T(8,128)(2,1)} collective-permute-done((bf16[4,2,384,384]{3,2,1,0:T(8,128)(2,1)}, bf16[4,2,384,384]{3,2,1,0:T(8,128)(2,1)}, u32[]{:S(2)}, u32[]{:S(2)}) %collective-permute-start) | collective-permute-done | bytes 2359328 | tf_op jit(solution)/shard_map/while/body/eval_jaxpr/ppermute | solution.py:20
  119.7 679.2 %collective-permute-done = bf16[4,2,384,384]{3,2,1,0:T(8,128)(2,1)} collective-permute-done((bf16[4,2,384,384]{3,2,1,0:T(8,128)(2,1)}, bf16[4,2,384,384]{3,2,1,0:T(8,128)(2,1)}, u32[]{:S(2)}, u32[]{:S(2)}) %collective-permute-start) | collective-permute-done | bytes 2359328 | tf_op jit(solution)/shard_map/while/body/eval_jaxpr/ppermute | solution.py:20
  798.9 211.7 %conditional.3 = (bf16[4,2,384,384]{3,2,1,0:T(8,128)(2,1)}, f32[4,384]{1,0:T(4,128)S(1)}) conditional(s32[]{:T(128)} %convert_element_type.89, () %tuple.154, (bf16[4,2,384,384]{3,2,1,0:T(8,128)(2,1)}, f32[4]{0:T(128)S(1)}, f32[4]{0:T(128)S(1)}, s32[4]{0:T(128)S(1)}, f32[4,384]{1,0:T(4,128)S(1)}, /*index=5*/f32[4,384]{1,0:T(4,128)}, ...), branch_computations={%region_2.2_spmd, %region_3.8_spmd.clone} | conditional | flops 459631552 | bytes 10114378 | solution.py:130
  799.7 210.9 %while.41 = (s32[]{:T(128)}, bf16[4,2,384,384]{3,2,1,0:T(8,128)(2,1)}, f32[4,4,384]{2,1,0:T(4,128)S(1)}, bf16[4,2,384,384]{3,2,1,0:T(8,128)(2,1)}, f32[4]{0:T(12...) while((s32[]{:T(128)}, ...), condition=%wide.region_7.6_spmd, body=%wide.region_4.5_spmd.sunk | while | flops 459626880 | bytes 10083334 | solution.py:116
  802.7 48.8 %while.43 = (s32[]{:T(128)}, bf16[2,384,384]{2,1,0:T(8,128)(2,1)S(1)}, f32[4,384]{1,0:T(4,128)S(1)}, f32[]{:T(128)}, f32[4,384]{1,0:T(4,128)S(1)}, /*index=5*/f3...) while((s32[]{:T(128)}, ...), condition=%wide.region_6.4_spmd, body=%wide.region_5.3_spmd.sunk | while | flops 459626880 | bytes 7711433 | solution.py:67
  807.4 2.6 fusion.47
  810.6 3.4 gather_fusion
  817.6 2.0 fusion.46
  819.6 2.6 fusion.47
  822.8 3.4 gather_fusion
  831.8 2.6 fusion.47
  835.1 3.4 gather_fusion
  844.0 2.6 fusion.47
  847.3 3.4 gather_fusion
  855.4 48.8 %while.43 = (s32[]{:T(128)}, bf16[2,384,384]{2,1,0:T(8,128)(2,1)S(1)}, f32[4,384]{1,0:T(4,128)S(1)}, f32[]{:T(128)}, f32[4,384]{1,0:T(4,128)S(1)}, /*index=5*/f3...) while((s32[]{:T(128)}, ...), condition=%wide.region_6.4_spmd, body=%wide.region_5.3_spmd.sunk | while | flops 459626880 | bytes 7711433 | solution.py:67
  858.1 2.0 fusion.46
  860.1 2.6 fusion.47
  863.4 3.4 gather_fusion
  870.3 2.0 fusion.46
  872.3 2.6 fusion.47
  875.6 3.4 gather_fusion
  882.5 2.0 fusion.46
  884.5 2.6 fusion.47
  887.8 3.4 gather_fusion
  896.7 2.6 fusion.47
  900.0 3.4 gather_fusion
  908.1 48.8 %while.43 = (s32[]{:T(128)}, bf16[2,384,384]{2,1,0:T(8,128)(2,1)S(1)}, f32[4,384]{1,0:T(4,128)S(1)}, f32[]{:T(128)}, f32[4,384]{1,0:T(4,128)S(1)}, /*index=5*/f3...) while((s32[]{:T(128)}, ...), condition=%wide.region_6.4_spmd, body=%wide.region_5.3_spmd.sunk | while | flops 459626880 | bytes 7711433 | solution.py:67
  912.8 2.6 fusion.47
  916.1 3.4 gather_fusion
  925.0 2.6 fusion.47
  928.3 3.4 gather_fusion
  937.2 2.6 fusion.47
  940.5 3.4 gather_fusion
  949.4 2.6 fusion.47
  952.7 3.4 gather_fusion
  960.8 48.8 %while.43 = (s32[]{:T(128)}, bf16[2,384,384]{2,1,0:T(8,128)(2,1)S(1)}, f32[4,384]{1,0:T(4,128)S(1)}, f32[]{:T(128)}, f32[4,384]{1,0:T(4,128)S(1)}, /*index=5*/f3...) while((s32[]{:T(128)}, ...), condition=%wide.region_6.4_spmd, body=%wide.region_5.3_spmd.sunk | while | flops 459626880 | bytes 7711433 | solution.py:67
  965.5 2.6 fusion.47
  968.8 3.4 gather_fusion
  977.8 2.6 fusion.47
  981.0 3.4 gather_fusion
  990.0 2.6 fusion.47
  993.2 3.4 gather_fusion
  1002.2 2.6 fusion.47
  1005.4 3.4 gather_fusion
  1011.9 52.8 %collective-permute-done = bf16[4,2,384,384]{3,2,1,0:T(8,128)(2,1)} collective-permute-done((bf16[4,2,384,384]{3,2,1,0:T(8,128)(2,1)}, bf16[4,2,384,384]{3,2,1,0:T(8,128)(2,1)}, u32[]{:S(2)}, u32[]{:S(2)}) %collective-permute-start) | collective-permute-done | bytes 2359328 | tf_op jit(solution)/shard_map/while/body/eval_jaxpr/ppermute | solution.py:20
  1064.7 12.0 %psum.7 = f32[4,384]{1,0:T(4,128)S(1)} all-reduce(f32[4,384]{1,0:T(4,128)S(1)} %get-tuple-element.351), channel_id=1, replica_groups=mesh['kt'=8,'en'=4] {'kt'}, use_global_device_ids=true, to_apply=%region_10.11 | all-reduce | flops 1536 | bytes 12288 | tf_op jit(solution)/shard_map/psum | solution.py:141
  (239 shorter events, 92.3 us)
Async XLA Ops:
  0.6 1076.0 %copy-start = (f32[384,384]{1,0:T(8,128)S(1)}, f32[384,384]{1,0:T(8,128)}, u32[]{:S(2)}) copy-start(f32[384,384]{1,0:T(8,128)} %param.25) | copy-start | bytes 1769476
  3.9 1072.8 %copy-start.2 = (f32[4,384]{1,0:T(4,128)S(1)}, f32[4,384]{1,0:T(4,128)}, u32[]{:S(2)}) copy-start(f32[4,384]{1,0:T(4,128)} %param.24) | copy-start | bytes 18436
  5.6 55.2 %collective-permute-start = (bf16[4,2,384,384]{3,2,1,0:T(8,128)(2,1)}, bf16[4,2,384,384]{3,2,1,0:T(8,128)(2,1)}, u32[]{:S(2)}, u32[]{:S(2)}) collective-permute-start(bf16[4,2,384,384]{3,2,1,0:T(8,128)(2,1)} %get-tuple-element.768), channel_id=1, source_target_pairs={{0,1},{1,2},{2,3},{4,5},{5,6},{6,7},{8,9},{9,10},{10,11},{12,13},{... | collective-permute-start | bytes 7077896 | tf_op jit(solution)/shard_map/while/body/eval_jaxpr/ppermute | solution.py:20
  62.4 54.3 %collective-permute-start = (bf16[4,2,384,384]{3,2,1,0:T(8,128)(2,1)}, bf16[4,2,384,384]{3,2,1,0:T(8,128)(2,1)}, u32[]{:S(2)}, u32[]{:S(2)}) collective-permute-start(bf16[4,2,384,384]{3,2,1,0:T(8,128)(2,1)} %get-tuple-element.768), channel_id=1, source_target_pairs={{0,1},{1,2},{2,3},{4,5},{5,6},{6,7},{8,9},{9,10},{10,11},{12,13},{... | collective-permute-start | bytes 7077896 | tf_op jit(solution)/shard_map/while/body/eval_jaxpr/ppermute | solution.py:20
  118.4 680.5 %collective-permute-start = (bf16[4,2,384,384]{3,2,1,0:T(8,128)(2,1)}, bf16[4,2,384,384]{3,2,1,0:T(8,128)(2,1)}, u32[]{:S(2)}, u32[]{:S(2)}) collective-permute-start(bf16[4,2,384,384]{3,2,1,0:T(8,128)(2,1)} %get-tuple-element.768), channel_id=1, source_target_pairs={{0,1},{1,2},{2,3},{4,5},{5,6},{6,7},{8,9},{9,10},{10,11},{12,13},{... | collective-permute-start | bytes 7077896 | tf_op jit(solution)/shard_map/while/body/eval_jaxpr/ppermute | solution.py:20
  1010.6 54.1 %collective-permute-start = (bf16[4,2,384,384]{3,2,1,0:T(8,128)(2,1)}, bf16[4,2,384,384]{3,2,1,0:T(8,128)(2,1)}, u32[]{:S(2)}, u32[]{:S(2)}) collective-permute-start(bf16[4,2,384,384]{3,2,1,0:T(8,128)(2,1)} %get-tuple-element.768), channel_id=1, source_target_pairs={{0,1},{1,2},{2,3},{4,5},{5,6},{6,7},{8,9},{9,10},{10,11},{12,13},{... | collective-permute-start | bytes 7077896 | tf_op jit(solution)/shard_map/while/body/eval_jaxpr/ppermute | solution.py:20
  1076.7 1.2 copy-start.1
where the time goes:
time: 1080 us
  waiting for transfers between devices  839 us (78%)
  local copies, waits for them, and re-layouts  88.4 us (8%)
  other arithmetic  55.6 us (5%)
  matrix products  43.2 us (4%)
  loops' own time  34.1 us (3%)
  blocking collectives  12 us (1%)
    ppermute x4, waiting for transfers between devices, from_behind(): return lax.ppermute(block, axis, route)  839 us
    gather x16, local copies, waits for them, and re-layouts, slab_step(): jnp.diagonal(green_imag)  55.1 us
    dot_general x16, matrix products, slab_step(): jnp.einsum('prn,cn->prc', left_part, coupled, preferred_element_type=jnp....  41.9 us
    another operation x4, loops' own time, slab_chain(): return lax.scan(one_slab, carried, tables)  33.8 us
    sub x16, other arithmetic, one_slab(): diag_real = item_energy + real_row - item_cos * hop_row  31.3 us
  transfers between devices with their start and end apart: 4, of which 4 were waited for; matrix products, arithmetic and copies ran while one was open for 0% of the time, Pallas kernels for 0%

commit v1 on v0

v1 whole, which is shorter than its diff:
```python
import functools

import jax
import jax.numpy as jnp
import numpy as np
from jax import lax
from jax.experimental import pallas as pl
from jax.experimental.pallas import tpu as pltpu
from jax.sharding import PartitionSpec as P

EMAX = 4
LANE = 128
F32 = jnp.float32
BF16 = jnp.bfloat16

bottom_sample_mark = -1.0
sample_gap = 0.25
electrode_filling = -0.5
boltzmann_spread = 0.1
broadening = 1.0
contact_width = 0.5


def item_constants(impulse_count):
    wave = np.float32(np.pi) * (np.arange(impulse_count, dtype=np.float32) + np.float32(0.5))
    cosine = np.cos(wave / np.float32(impulse_count))
    energy = bottom_sample_mark + sample_gap * np.arange(EMAX)
    weight = sample_gap / (1.0 + np.exp((energy - electrode_filling) / boltzmann_spread)) / np.pi
    return np.concatenate([cosine, weight]).astype(np.float32)


def span(k):
    return slice(k * LANE, (k + 1) * LANE)


def place(parts, half, c):
    if c == parts - 1:
        return parts - 1 + half
    return c if half == 0 else parts + 1 + c


def blocks_on_or_below(parts):
    return [(r, c) for r in range(parts) for c in range(r + 1)]


def packed_rows(orbitals):
    parts = orbitals // LANE
    return parts * parts * LANE + 16


def pairs_below(parts):
    return [(r, c) for r in range(parts) for c in range(r)]


def pair_slot(parts, r, c, half):
    return 2 * pairs_below(parts).index((r, c)) + half


def middle_slot(parts, r):
    return parts * (parts - 1) + r


def tile_indices():
    rows = lax.broadcasted_iota(jnp.int32, (LANE, LANE), 0)
    cols = lax.broadcasted_iota(jnp.int32, (LANE, LANE), 1)
    return rows, cols


def unpack_blocks(packed, g, parts):
    rows, cols = tile_indices()
    for r, c in pairs_below(parts):
        for half in range(2):
            block = packed[span(pair_slot(parts, r, c, half)), :]
            g[span(r), span(place(parts, half, c))] = block
            g[span(c), span(place(parts, half, r))] = block.T
    at = parts * parts * LANE
    for r in range(parts):
        block = packed[span(middle_slot(parts, r)), :]
        turned = block.T
        middle = packed[at : at + 16, :][r : r + 1, :]
        g[span(r), span(place(parts, 0, r))] = jnp.where(rows <= cols, block, turned)
        g[span(r), span(place(parts, 1, r))] = jnp.where(
            rows > cols, block, jnp.where(rows == cols, middle, turned)
        )


def extra_item(counts, mine):
    def one(k, state):
        momentum, before = state
        extra = counts[k] - 1
        take = jnp.logical_and(momentum == k, before + extra <= mine)
        return (jnp.where(take, k + 1, momentum), jnp.where(take, before + extra, before))

    momentum, before = lax.fori_loop(0, counts.shape[0], one, (jnp.int32(0), jnp.int32(0)))
    momentum = jnp.minimum(momentum, counts.shape[0] - 1)
    return momentum, jnp.clip(1 + mine - before, 0, EMAX - 1)


def entry_amounts(constants, impulse_count, momentum, level):
    energy = bottom_sample_mark + sample_gap * level.astype(F32)
    return constants[momentum], energy, constants[impulse_count + level]


def inverse_diagonal(position, cosine, energy, contact, onsite, hopping, potential):
    slabs, orbitals = onsite.shape
    diag_real = energy + (-onsite[...] - potential[...]) - cosine * hopping[...]
    slab_in = lax.broadcasted_iota(jnp.int32, (slabs, orbitals), 0) + position * slabs
    at_contact = jnp.logical_or(slab_in == contact[0], slab_in == contact[1])
    diag_imag = broadening + contact_width * at_contact.astype(F32)
    magnitude = diag_real * diag_real + diag_imag * diag_imag
    inv_real = diag_real / magnitude
    inv_imag = -diag_imag / magnitude
    return inv_real, inv_imag


def scale_rows(parts):
    return 2 * len(blocks_on_or_below(parts)) * LANE


def form_scales(slabs_wanted, inv_real, inv_imag, scales, parts):
    slabs = inv_real.shape[0]
    down = jnp.concatenate([inv_real, inv_imag], axis=0).T
    for s in slabs_wanted:
        for k, (r, c) in enumerate(blocks_on_or_below(parts)):
            real_col = down[span(r), s : s + 1]
            imag_col = down[span(r), slabs + s : slabs + s + 1]
            rr = inv_real[s : s + 1, span(c)]
            ri = inv_imag[s : s + 1, span(c)]
            scales[s, span(2 * k), :] = real_col * rr - imag_col * ri
            scales[s, span(2 * k + 1), :] = real_col * ri + imag_col * rr


def store_left(left, piece, half, c, parts):
    last = (parts - 1) * LANE
    left[half * last : (half + 1) * last, span(c)] = piece[:last]
    bottom = 2 * last + half * LANE
    left[bottom : bottom + LANE, span(c)] = piece[last:]


def times_carried(coupled, g, left, parts):
    last = (parts - 1) * LANE
    for begin, width in ((last, 2 * LANE), (0, last), (last + 2 * LANE, last)):
        product = jnp.dot(
            coupled, g[:, begin : begin + width], preferred_element_type=F32
        ).astype(BF16)
        for k in range(width // LANE):
            column = begin // LANE + k
            half, c = (
                (0, column)
                if column < parts
                else (1, parts - 1 if column == parts else column - parts - 1)
            )
            store_left(left, product[:, span(k)], half, c, parts)


def finish_slab(s, times_turned, left, g, packed, inv_real, inv_imag, scales, weight, density, parts):
    last = (parts - 1) * LANE
    rows, cols = tile_indices()
    diagonal = rows == cols
    numbers = {block: k for k, block in enumerate(blocks_on_or_below(parts))}
    middles = {}

    def finish(r, c, sr, si):
        k = numbers[r, c]
        scale_real = scales[s, span(2 * k), :]
        scale_imag = scales[s, span(2 * k + 1), :]
        green_real = scale_real * sr - scale_imag * si
        green_imag = scale_real * si + scale_imag * sr
        if r == c:
            green_real = green_real + jnp.where(diagonal, inv_real[s : s + 1, span(c)], 0.0)
            green_imag = green_imag + jnp.where(diagonal, inv_imag[s : s + 1, span(c)], 0.0)
            middles[r] = jnp.sum(jnp.where(diagonal, green_imag, 0.0), axis=0, keepdims=True)
            density[s : s + 1, span(r)] += -weight * middles[r]
        if packed is not None:
            if r == c:
                packed[span(middle_slot(parts, r)), :] = jnp.where(
                    rows <= cols, green_real, green_imag
                ).astype(BF16)
            else:
                packed[span(pair_slot(parts, r, c, 0)), :] = green_real.astype(BF16)
                packed[span(pair_slot(parts, r, c, 1)), :] = green_imag.astype(BF16)
            return
        if g is None:
            return
        for half, green in ((0, green_real), (1, green_imag)):
            rounded = green.astype(BF16)
            g[span(r), span(place(parts, half, c))] = rounded
            if r != c:
                g[span(c), span(place(parts, half, r))] = rounded.T

    far = times_turned(left[2 * last :, :], last + LANE)
    near = times_turned(left[: 2 * last, :], last)
    for c in range(parts):
        finish(parts - 1, c, far[:LANE, span(c)], far[LANE:, span(c)])
    for r in range(parts - 1):
        for c in range(r + 1):
            finish(r, c, near[span(r), span(c)], near[last:, :][span(r), span(c)])
    if packed is not None:
        rest = jnp.zeros((16 - parts, LANE), F32)
        at = parts * parts * LANE
        packed[at : at + 16, :] = jnp.concatenate(
            [middles[r] for r in range(parts)] + [rest], axis=0
        ).astype(BF16)


def coupling_of(base, wave, cosine):
    return (base.astype(F32) + cosine * wave.astype(F32)).astype(BF16)


def first_segment(coupled_of, inv_real, inv_imag, scales, weight, g, left, sent, density):
    slabs, orbitals = inv_real.shape
    parts = orbitals // LANE
    density[0:1, :] = -weight * inv_imag[0:1, :]
    for s in range(1, slabs):
        coupled = coupled_of(s)
        if s == 1:
            wide = coupled.astype(F32)
            for half, inv in ((0, inv_real), (1, inv_imag)):
                piece = (wide * inv[0:1, :].astype(BF16).astype(F32)).astype(BF16)
                for c in range(parts):
                    store_left(left, piece[:, span(c)], half, c, parts)
        else:
            times_carried(coupled, g, left, parts)

        def times_turned(rows, upto):
            return lax.dot_general(
                rows, coupled[:upto], (((1,), (1,)), ((), ())), preferred_element_type=F32
            )

        finish_slab(
            s, times_turned, left, g, sent if s == slabs - 1 else None,
            inv_real, inv_imag, scales, weight, density, parts,
        )


def own_kernel(
    impulse_count,
    constants_hbm, contact_hbm, onsite_hbm, hopping_hbm, potential_hbm, base_hbm, wave_hbm,
    sent, density,
    constants, contact, tables, base, wave, scales, g, left, small_sem, table_sem, couple_sem,
):
    slabs, orbitals = onsite_hbm.shape
    parts = orbitals // LANE
    position = lax.axis_index("en")
    density[...] = jnp.zeros_like(density)

    @pl.when(position == 0)
    def _():
        small_copies = [
            pltpu.make_async_copy(source, target, small_sem.at[k])
            for k, (source, target) in enumerate(
                ((constants_hbm, constants), (contact_hbm, contact))
            )
        ] + [
            pltpu.make_async_copy(source, tables.at[k], table_sem.at[k])
            for k, source in enumerate((onsite_hbm, hopping_hbm, potential_hbm))
        ]
        couple_copies = {
            s: (
                pltpu.make_async_copy(base_hbm.at[s], base.at[s], couple_sem.at[0, s]),
                pltpu.make_async_copy(wave_hbm.at[s], wave.at[s], couple_sem.at[1, s]),
            )
            for s in range(1, slabs)
        }
        for copy in small_copies:
            copy.start()
        for s in range(1, slabs):
            for copy in couple_copies[s]:
                copy.start()
        for copy in small_copies:
            copy.wait()
        cosine, energy, weight = entry_amounts(
            constants, impulse_count, lax.axis_index("kt"), jnp.int32(0)
        )
        inv_real, inv_imag = inverse_diagonal(
            position, cosine, energy, contact, tables.at[0], tables.at[1], tables.at[2]
        )
        form_scales(range(1, slabs), inv_real, inv_imag, scales, parts)

        def coupled_of(s):
            for copy in couple_copies[s]:
                copy.wait()
            return coupling_of(base[s], wave[s], cosine)

        first_segment(coupled_of, inv_real, inv_imag, scales, weight, g, left, sent, density)


def extra_kernel(
    impulse_count,
    constants, contact, counts, onsite, hopping, potential, base, wave, so_far,
    sent, density,
    couple_own, turned_own, scales_own, entry_own,
    couple_extra, turned_extra, scales_extra, entry_extra,
    scales, g, left,
):
    slabs, orbitals = onsite.shape
    parts = orbitals // LANE
    position = lax.axis_index("en")
    mine = lax.axis_index("kt")
    density[...] = so_far[...]
    momentum, level = extra_item(counts, mine)
    cosine, energy, weight = entry_amounts(constants, impulse_count, momentum, level)
    inv_real, inv_imag = inverse_diagonal(
        position, cosine, energy, contact, onsite, hopping, potential
    )

    @pl.when(position == 0)
    def _():
        form_scales(range(1, slabs), inv_real, inv_imag, scales, parts)
        first = jnp.zeros_like(density)
        kept = density[...]
        density[...] = first

        def coupled_of(s):
            return coupling_of(base[s], wave[s], cosine)

        first_segment(coupled_of, inv_real, inv_imag, scales, weight, g, left, sent, density)
        density[...] += kept

    def prepare(cosine, weight, inv_real, inv_imag, couple, turned, scales_out, entry):
        form_scales(range(slabs), inv_real, inv_imag, scales_out, parts)
        entry[:slabs, :] = inv_real
        entry[slabs : 2 * slabs, :] = inv_imag
        entry[2 * slabs :, :] = jnp.full((slabs, orbitals), weight, F32)
        for s in range(slabs):
            coupled = coupling_of(base[s], wave[s], cosine)
            couple[s] = coupled
            for r in range(parts):
                for c in range(parts):
                    turned[s, span(c), span(r)] = coupled[span(r), span(c)].T

    @pl.when(position > 0)
    def _():
        own_cosine, own_energy, own_weight = entry_amounts(
            constants, impulse_count, mine, jnp.int32(0)
        )
        own_real, own_imag = inverse_diagonal(
            position, own_cosine, own_energy, contact, onsite, hopping, potential
        )
        prepare(
            own_cosine, own_weight, own_real, own_imag,
            couple_own, turned_own, scales_own, entry_own,
        )
        prepare(
            cosine, weight, inv_real, inv_imag,
            couple_extra, turned_extra, scales_extra, entry_extra,
        )


def stage_kernel(stage, last_stage, couple, turned, scales, entry, arrived, so_far, *refs):
    if last_stage:
        density, g, left = refs
        sent = None
    else:
        sent, density, g, left = refs
    slabs, orbitals = so_far.shape
    parts = orbitals // LANE
    density[...] = so_far[...]

    @pl.when(lax.axis_index("en") == stage)
    def _():
        inv_real = entry[:slabs, :]
        inv_imag = entry[slabs : 2 * slabs, :]
        weight = entry[2 * slabs : 2 * slabs + 1, :LANE]
        unpack_blocks(arrived, g, parts)
        for s in range(slabs):
            times_carried(couple[s], g, left, parts)

            def times_turned(rows, upto):
                return jnp.dot(rows, turned[s, :, :upto], preferred_element_type=F32)

            final = s == slabs - 1
            finish_slab(
                s, times_turned, left, None if final else g, sent if final else None,
                inv_real, inv_imag, scales, weight, density, parts,
            )


def vmem_call(kernel, outs, operands, in_specs, scratch, name, flops, **more):
    vmem = pl.BlockSpec(memory_space=pltpu.VMEM)
    return pl.pallas_call(
        kernel,
        out_shape=tuple(outs),
        in_specs=in_specs,
        out_specs=(vmem,) * len(outs),
        scratch_shapes=scratch,
        compiler_params=pltpu.CompilerParams(vmem_limit_bytes=24 * 2**20),
        cost_estimate=pl.CostEstimate(flops=flops, bytes_accessed=2**21, transcendentals=0),
        name=name,
        **more,
    )(*operands)


def last_kernel(gathered, doping, inverse, summed, potential):
    total = jnp.sum(gathered[...], axis=0)
    summed[...] = total
    potential[...] = lax.dot_general(
        total - doping[...],
        inverse[...],
        (((1,), (1,)), ((), ())),
        preferred_element_type=F32,
        precision=lax.Precision.HIGHEST,
    )


def gather_over(values, axis):
    copies = jnp.broadcast_to(values[None], (lax.axis_size(axis),) + values.shape)
    return lax.all_to_all(copies, axis, 0, 0)


def body(
    counts,
    contact_slabs,
    onsite,
    hopping,
    potential_in,
    couple_base,
    couple_wave,
    doping,
    poisson_inverse,
):
    kt_size = lax.axis_size("kt")
    en_size = lax.axis_size("en")
    slabs, orbitals = onsite.shape
    parts = orbitals // LANE
    position = lax.axis_index("en")
    impulse_count = counts.shape[0] * kt_size
    constants = jnp.asarray(item_constants(impulse_count))
    smem = pl.BlockSpec(memory_space=pltpu.SMEM)
    hbm = pl.BlockSpec(memory_space=pltpu.HBM)
    vmem = pl.BlockSpec(memory_space=pltpu.VMEM)
    flops = 2 * slabs * orbitals**3

    def forward(block, stage):
        return lax.ppermute(block, "en", [(stage, stage + 1)])

    block_shape = jax.ShapeDtypeStruct((packed_rows(orbitals), LANE), BF16)
    density_shape = jax.ShapeDtypeStruct((slabs, orbitals), F32)
    couple_shape = jax.ShapeDtypeStruct((slabs, orbitals, orbitals), BF16)
    scales_shape = jax.ShapeDtypeStruct((slabs, scale_rows(parts), LANE), F32)
    entry_shape = jax.ShapeDtypeStruct((3 * slabs, orbitals), F32)
    scales_scratch = pltpu.VMEM(scales_shape.shape, F32)
    work = [
        pltpu.VMEM((orbitals, 2 * orbitals), BF16),
        pltpu.VMEM((2 * orbitals, orbitals), BF16),
    ]

    half = en_size // 2
    counts_here = lax.cond(
        position >= half,
        lambda c: lax.all_gather(c, "kt", tiled=True),
        lambda c: jnp.zeros((impulse_count,), jnp.int32),
        counts,
    )
    pinned, counts_here = lax.optimization_barrier(
        (
            (constants, contact_slabs, onsite, hopping, potential_in, couple_base, couple_wave),
            counts_here,
        )
    )
    pinned = [pltpu.with_memory_space_constraint(t, pltpu.HBM) for t in pinned]
    block, density = vmem_call(
        functools.partial(own_kernel, impulse_count),
        (block_shape, density_shape),
        pinned,
        [hbm] * len(pinned),
        [
            pltpu.SMEM(constants.shape, F32),
            pltpu.SMEM(contact_slabs.shape, jnp.int32),
            pltpu.VMEM((3, slabs, orbitals), F32),
            pltpu.VMEM((slabs, orbitals, orbitals), BF16),
            pltpu.VMEM((slabs, orbitals, orbitals), BF16),
            scales_scratch,
        ]
        + work
        + [
            pltpu.SemaphoreType.DMA((2,)),
            pltpu.SemaphoreType.DMA((3,)),
            pltpu.SemaphoreType.DMA((2, slabs)),
        ],
        "first_own",
        3 * flops,
    )
    arrived_own = forward(block, 0)
    counts_all = counts_here + lax.ppermute(
        counts_here, "en", [(p + half, p) for p in range(half)]
    )
    held, density, *made = vmem_call(
        functools.partial(extra_kernel, impulse_count),
        (block_shape, density_shape) + (couple_shape, couple_shape, scales_shape, entry_shape) * 2,
        (
            constants, contact_slabs, counts_all,
            onsite, hopping, potential_in, couple_base, couple_wave, density,
        ),
        [smem] * 3 + [vmem] * 6,
        [scales_scratch] + work,
        "first_extra",
        3 * flops,
        input_output_aliases={8: 1},
    )
    made_own, made_extra = made[:4], made[4:]

    def run_stage(stage, made, arrived, density, name):
        last_stage = stage == en_size - 1
        results = vmem_call(
            functools.partial(stage_kernel, stage, last_stage),
            (density_shape,) if last_stage else (block_shape, density_shape),
            (*made, arrived, density),
            [vmem] * 6,
            work,
            f"stage_{stage}_{name}",
            4 * flops,
            input_output_aliases={5: 0 if last_stage else 1},
        )
        return (None, *results) if last_stage else results

    for stage in range(1, en_size):
        arrived_own, held = lax.optimization_barrier((arrived_own, held))
        arrived_extra = forward(held, stage - 1)
        block, density = run_stage(stage, made_own, arrived_own, density, "own")
        if stage < en_size - 1:
            arrived_own = forward(block, stage)
        held, density = run_stage(stage, made_extra, arrived_extra, density, "extra")
    return pl.pallas_call(
        last_kernel,
        out_shape=(density_shape, density_shape),
        in_specs=[vmem] * 3,
        out_specs=(vmem, vmem),
        name="last",
    )(gather_over(density, "kt"), doping, poisson_inverse)


def solution(mesh):
    return jax.shard_map(
        body,
        mesh=mesh,
        in_specs=(
            P("kt"),
            P(),
            P("en", None),
            P("en", None),
            P("en", None),
            P("en", None, None),
            P("en", None, None),
            P("en", None),
            P(),
        ),
        out_specs=(P("en", None), P("en", None)),
        check_vma=False,
    )
```

time: 1080 us -> 68.2 us (0.06)
  waiting for transfers between devices: 839 us -> 27.5 us
  local copies, waits for them, and re-layouts: 88.4 us -> 2.69 us
  other arithmetic: 55.6 us -> 0.01 us
  matrix products: 43.2 us -> 0 us
  loops' own time: 34.1 us -> 0.03 us
  Pallas kernels: 0 us -> 14.1 us
    ppermute x4 -> x7, waiting for transfers between devices: 839 us -> 27.5 us  [the longest x6 26.2 us: forward(): return lax.ppermute(block, 'en', [(stage, stage + 1)])]
    gather x16 -> x0, local copies, waits for them, and re-layouts: 55.1 us -> none  [slab_step(): jnp.diagonal(green_imag)]
    dot_general x17 -> x0, matrix products: 43.2 us -> none  [the longest x16 41.9 us: slab_step(): jnp.einsum('prn,cn->prc', left_part, coupled, preferred_element_type=jnp....]
    another operation x10 -> x1, loops' own time: 34.1 us -> 0.03 us  [body(): lax.cond(position >= half, lambda c: lax.all_gather(c, 'kt', tiled=True),...]
    sub x17 -> x0, other arithmetic: 32 us -> none  [the longest x16 31.3 us: one_slab(): diag_real = item_energy + real_row - item_cos * hop_row]
    dynamic_slice x28 -> x0, local copies, waits for them, and re-layouts: 17.9 us -> none  [step_forward(): lax.map(each_entry_share, (injected_from_lead, angular_projection, occupa...]
    pallas_call x0 -> x9, Pallas kernels: none -> 14.1 us  [the longest x8 11.8 us: vmem_call(): pl.pallas_call(kernel, out_shape=tuple(outs), in_specs=in_specs, out_spec...]
    psum x1 -> x0, blocking collectives: 12 us -> none  [body(): summed = lax.psum(electron_populace, 'kt')]
  transfers between devices with their start and end apart: 4 -> 7, of which waited for: 4 -> 3; matrix products, arithmetic and copies ran while one was open for 0% -> 0% of each run, Pallas kernels for 0% -> 11%
where the time goes in v1:
time: 68.2 us; the launch traced here: 67.9 us
  waiting for transfers between devices  27.5 us (40%)
  blocking collectives  16 us (23%)
  Pallas kernels  14.1 us (21%)
  starting transfers between devices  6.71 us (10%)
  local copies, waits for them, and re-layouts  2.69 us (4%)
  between operations  0.86 us (1%)
    ppermute x6, waiting for transfers between devices, forward(): return lax.ppermute(block, 'en', [(stage, stage + 1)])  26.2 us
    pallas_call x8, Pallas kernels, vmem_call(): pl.pallas_call(kernel, out_shape=tuple(outs), in_specs=in_specs, out_spec...  11.8 us
    cond x1, blocking collectives  8.01 us
    all_to_all x1, blocking collectives, gather_over(): return lax.all_to_all(copies, axis, 0, 0)  7.99 us
    ppermute x6, starting transfers between devices, forward(): return lax.ppermute(block, 'en', [(stage, stage + 1)])  5.42 us
    cond x3, local copies, waits for them, and re-layouts  2.65 us
    pallas_call x1, Pallas kernels, body(): pl.pallas_call(last_kernel, out_shape=(density_shape, density_shape), in_...  2.33 us
  transfers between devices with their start and end apart: 7, of which 3 were waited for; matrix products, arithmetic and copies ran while one was open for 0% of the time, Pallas kernels for 11%

profile of v1, /device:TPU:24, one launch (start us, length us, event | category | flops | bytes accessed | tf_op | source)
XLA Modules:
  0.0 67.9 jit_solution(5644448077044465273)
XLA Ops:
  0.6 10.7 %conditional.1 = (s32[8]{0:T(128)S(1)}) conditional(s32[]{:T(128)} %convert_element_type.3, () %tuple.17, (s32[1]{0:T(128)}) %tuple.22), branch_computations={%region_0.0_spmd, %region_1.0_spmd} | conditional | flops 10 | bytes 156 | solution.py:449
  0.7 1.2 %dynamic-slice = u32[1]{0:T(128)} dynamic-slice(u32[32]{0:T(128)} %constant.14, u32[]{:T(128)S(6)} %add.4), dynamic_slice_sizes={1} | dynamic-slice | bytes 12 | tf_op jit(solution)/shard_map/cond
  1.9 1.4 %dynamic-update-slice = s32[8]{0:T(128)S(1)} dynamic-update-slice(s32[8]{0:T(128)S(1)} %broadcast.4, s32[1]{0:T(128)} %get-tuple-element.75, u32[]{:T(128)} %bitcast) | dynamic-update-slice | bytes 12 | tf_op jit(solution)/shard_map/cond
  3.3 8.0 %all-reduce = s32[8]{0:T(128)S(1)} all-reduce(s32[8]{0:T(128)S(1)} %dynamic-update-slice), channel_id=1, replica_groups=mesh['kt'=8,'en'=4] {'kt'}, use_global_device_ids=true, to_apply=%add | all-reduce | flops 8 | bytes 64 | tf_op jit(solution)/shard_map/cond
  11.3 0.0 copy-start
  11.3 0.0 copy-start.1
  11.3 0.0 copy-start.2
  11.3 0.0 copy-start.3
  11.3 0.0 copy-start.4
  11.3 0.0 copy-start.5
  11.4 0.0 copy-start.6
  11.4 0.1 first_own.1
  11.5 0.8 %collective-permute-start.1 = (bf16[1168,128]{1,0:T(8,128)(2,1)S(1)}, bf16[1168,128]{1,0:T(8,128)(2,1)S(1)}, u32[]{:S(2)}, u32[]{:S(2)}) collective-permute-start(bf16[1168,128]{1,0:T(8,128)(2,1)S(1)} %get-tuple-element.57), channel_id=1, source_target_pairs={{0,1},{4,5},{8,9},{12,13},{16,17},{20,21},{24,25},{28,29}} | collective-permute-start | bytes 897032 | tf_op jit(solution)/shard_map/ppermute | solution.py:435
  12.3 1.3 %collective-permute-start = (s32[8]{0:T(128)S(1)}, s32[8]{0:T(128)S(1)}, u32[]{:S(2)}, u32[]{:S(2)}) collective-permute-start(s32[8]{0:T(128)S(1)} %get-tuple-element.76), channel_id=1, source_target_pairs={{2,0},{3,1},{6,4},{7,5},{10,8},{11,9},{14,12},{15,13},{18,16},{19,... | collective-permute-start | bytes 104 | tf_op jit(solution)/shard_map/ppermute | solution.py:485
  13.6 1.3 %collective-permute-done = s32[8]{0:T(128)S(1)} collective-permute-done((s32[8]{0:T(128)S(1)}, s32[8]{0:T(128)S(1)}, u32[]{:S(2)}, u32[]{:S(2)}) %collective-permute-start) | collective-permute-done | bytes 64 | tf_op jit(solution)/shard_map/ppermute | solution.py:485
  14.9 0.0 copy-done
  14.9 0.0 copy-done.1
  14.9 0.0 copy-done.2
  14.9 0.0 copy-done.3
  14.9 0.0 copy-done.4
  14.9 0.0 copy-done.5
  15.0 0.0 copy-done.6
  15.0 2.9 %first_extra.1 = (bf16[1168,128]{1,0:T(8,128)(2,1)S(1)}, f32[4,384]{1,0:T(4,128)S(1)}, bf16[4,384,384]{2,1,0:T(8,128)(2,1)S(1)}, bf16[4,384,384]{2,1,0:T(8,128)(...) custom-call(f32[12]{0:T(128)S(1)} %copy-done.6, ...), custom_call_target="tpu_custom_call", output_to_operand_aliasing={{1}: (8, {})} | custom-call | flops 1358954496 | bytes 2097152 | tf_op jit(solution)/shard_map/first_extra/pallas_call | solution.py:381
  17.9 0.0 collective-permute-done.1.arrived
  17.9 0.7 %collective-permute-start.3 = (bf16[1168,128]{1,0:T(8,128)(2,1)S(1)}, bf16[1168,128]{1,0:T(8,128)(2,1)S(1)}, u32[]{:S(2)}, u32[]{:S(2)}) collective-permute-start(bf16[1168,128]{1,0:T(8,128)(2,1)S(1)} %get-tuple-element.62), channel_id=1, source_target_pairs={{0,1},{4,5},{8,9},{12,13},{16,17},{20,21},{24,25},{28,29}} | collective-permute-start | bytes 897032 | tf_op jit(solution)/shard_map/ppermute | solution.py:435
  18.6 0.7 %collective-permute-start.2 = (bf16[1168,128]{1,0:T(8,128)(2,1)S(1)}, bf16[1168,128]{1,0:T(8,128)(2,1)S(1)}, u32[]{:S(2)}, u32[]{:S(2)}) collective-permute-start(bf16[1168,128]{1,0:T(8,128)(2,1)S(1)} %get-tuple-element.61), channel_id=1, source_target_pairs={{1,2},{5,6},{9,10},{13,14},{17,18},{21,22},{25,26},{29,30}} | collective-permute-start | bytes 897032 | tf_op jit(solution)/shard_map/ppermute | solution.py:435
  19.3 0.0 collective-permute-done.3.arrived
  19.3 0.2 stage_1_extra.1
  19.5 0.0 collective-permute-done.2.arrived
  19.6 0.7 %collective-permute-start.5 = (bf16[1168,128]{1,0:T(8,128)(2,1)S(1)}, bf16[1168,128]{1,0:T(8,128)(2,1)S(1)}, u32[]{:S(2)}, u32[]{:S(2)}) collective-permute-start(bf16[1168,128]{1,0:T(8,128)(2,1)S(1)} %get-tuple-element.68), channel_id=1, source_target_pairs={{1,2},{5,6},{9,10},{13,14},{17,18},{21,22},{25,26},{29,30}} | collective-permute-start | bytes 897032 | tf_op jit(solution)/shard_map/ppermute | solution.py:435
  20.3 1.3 %collective-permute-start.4 = (bf16[1168,128]{1,0:T(8,128)(2,1)S(1)}, bf16[1168,128]{1,0:T(8,128)(2,1)S(1)}, u32[]{:S(2)}, u32[]{:S(2)}) collective-permute-start(bf16[1168,128]{1,0:T(8,128)(2,1)S(1)} %get-tuple-element.67), channel_id=1, source_target_pairs={{2,3},{6,7},{10,11},{14,15},{18,19},{22,23},{26,27},{30,31}} | collective-permute-start | bytes 897032 | tf_op jit(solution)/shard_map/ppermute | solution.py:435
  21.6 0.0 collective-permute-done.5.arrived
  21.6 23.2 %collective-permute-done.4.arrived = bf16[1168,128]{1,0:T(8,128)(2,1)S(1)} collective-permute-done((bf16[1168,128]{1,0:T(8,128)(2,1)S(1)}, bf16[1168,128]{1,0:T(8,128)(2,1)S(1)}, u32[]{:S(2)}, u32[]{:S(2)}) %collective-permute-start.4) | collective-permute-done | bytes 299040 | tf_op jit(solution)/shard_map/ppermute | solution.py:435
  44.8 1.3 %collective-permute-start.6 = (bf16[1168,128]{1,0:T(8,128)(2,1)S(1)}, bf16[1168,128]{1,0:T(8,128)(2,1)S(1)}, u32[]{:S(2)}, u32[]{:S(2)}) collective-permute-start(bf16[1168,128]{1,0:T(8,128)(2,1)S(1)} %get-tuple-element.71), channel_id=1, source_target_pairs={{2,3},{6,7},{10,11},{14,15},{18,19},{22,23},{26,27},{30,31}} | collective-permute-start | bytes 897032 | tf_op jit(solution)/shard_map/ppermute | solution.py:435
  46.0 4.3 %stage_3_own.1.so_far = f32[4,384]{1,0:T(4,128)S(1)} custom-call(bf16[4,384,384]{2,1,0:T(8,128)(2,1)S(1)} %get-tuple-element.53.couple, bf16[4,384,384]{2,1,0:T(8,128)(2,1)S(1)} %get-tuple-element.54.turned, f32[4,1536,128]{2,1,0:T(8,128)S(1)} %get-tuple-element.55.scales, f32[12,384]{1,0:T(8,128)S(1)} %get-tuple-element.56.entry, ...), custom_call_target="tpu_custom_call", output_to_operand_aliasing={{}: (5, {})} | custom-call | flops 1811939328 | bytes 2097152 | tf_op jit(solution)/shard_map/stage_3_own/pallas_call | solution.py:381
  50.4 3.0 %collective-permute-done.6.arrived = bf16[1168,128]{1,0:T(8,128)(2,1)S(1)} collective-permute-done((bf16[1168,128]{1,0:T(8,128)(2,1)S(1)}, bf16[1168,128]{1,0:T(8,128)(2,1)S(1)}, u32[]{:S(2)}, u32[]{:S(2)}) %collective-permute-start.6) | collective-permute-done | bytes 299040 | tf_op jit(solution)/shard_map/ppermute | solution.py:435
  53.4 4.1 %stage_3_extra.1 = f32[4,384]{1,0:T(4,128)S(1)} custom-call(bf16[4,384,384]{2,1,0:T(8,128)(2,1)S(1)} %get-tuple-element.49.couple, bf16[4,384,384]{2,1,0:T(8,128)(2,1)S(1)} %get-tuple-element.50.turned, f32[4,1536,128]{2,1,0:T(8,128)S(1)} %get-tuple-element.51.scales, f32[12,384]{1,0:T(8,128)S(1)} %get-tuple-element.52.entry, ...), custom_call_target="tpu_custom_call", output_to_operand_aliasing={{}: (5, {})} | custom-call | flops 1811939328 | bytes 2097152 | tf_op jit(solution)/shard_map/stage_3_extra/pallas_call | solution.py:381
  57.6 8.0 %all_to_all.5.gathered = f32[8,4,384]{2,1,0:T(4,128)} all-to-all(f32[8,4,384]{2,1,0:T(4,128)S(1)} %broadcast_in_dim.2), channel_id=1, replica_groups=mesh['kt'=8,'en'=4] {'kt'}, dimensions={0} | all-to-all | bytes 98304 | tf_op jit(solution)/shard_map/all_to_all | solution.py:408
  65.5 2.3 %last.1 = (f32[4,384]{1,0:T(4,128)}, f32[4,384]{1,0:T(4,128)}) custom-call(f32[8,4,384]{2,1,0:T(4,128)} %all_to_all.5.gathered, f32[4,384]{1,0:T(4,128)} %doping.1, f32[384,384]{1,0:T(8,128)} %inverse.1), custom_call_target="tpu_custom_call" | custom-call | tf_op jit(solution)/shard_map/last/pallas_call | solution.py:524
  (6 shorter events, 0.1 us)
Async XLA Ops:
  11.3 3.6 %copy-start = (bf16[4,384,384]{2,1,0:T(8,128)(2,1)S(1)}, bf16[4,384,384]{2,1,0:T(8,128)(2,1)}, u32[]{:S(2)}) copy-start(bf16[4,384,384]{2,1,0:T(8,128)(2,1)} %base.1) | copy-start | bytes 3538948
  11.3 3.6 %copy-start.1 = (bf16[4,384,384]{2,1,0:T(8,128)(2,1)S(1)}, bf16[4,384,384]{2,1,0:T(8,128)(2,1)}, u32[]{:S(2)}) copy-start(bf16[4,384,384]{2,1,0:T(8,128)(2,1)} %wave.1) | copy-start | bytes 3538948
  11.3 3.6 %copy-start.2 = (f32[4,384]{1,0:T(4,128)S(1)}, f32[4,384]{1,0:T(4,128)}, u32[]{:S(2)}) copy-start(f32[4,384]{1,0:T(4,128)} %onsite.1) | copy-start | bytes 18436
  11.3 3.6 %copy-start.3 = (f32[4,384]{1,0:T(4,128)S(1)}, f32[4,384]{1,0:T(4,128)}, u32[]{:S(2)}) copy-start(f32[4,384]{1,0:T(4,128)} %hopping.1) | copy-start | bytes 18436
  11.3 3.6 %copy-start.4 = (f32[4,384]{1,0:T(4,128)S(1)}, f32[4,384]{1,0:T(4,128)}, u32[]{:S(2)}) copy-start(f32[4,384]{1,0:T(4,128)} %potential.1) | copy-start | bytes 18436
  11.3 3.6 %copy-start.5 = (s32[2]{0:T(128)S(1)}, s32[2]{0:T(128)}, u32[]{:S(2)}) copy-start(s32[2]{0:T(128)} %contact.1) | copy-start | bytes 28
  11.4 3.6 %copy-start.6 = (f32[12]{0:T(128)S(1)}, f32[12]{0:T(128)}, u32[]{:S(2)}) copy-start(f32[12]{0:T(128)} %constant.10.clone.constants_hbm.constants) | copy-start | bytes 148
  11.5 6.4 %collective-permute-start.1 = (bf16[1168,128]{1,0:T(8,128)(2,1)S(1)}, bf16[1168,128]{1,0:T(8,128)(2,1)S(1)}, u32[]{:S(2)}, u32[]{:S(2)}) collective-permute-start(bf16[1168,128]{1,0:T(8,128)(2,1)S(1)} %get-tuple-element.57), channel_id=1, source_target_pairs={{0,1},{4,5},{8,9},{12,13},{16,17},{20,21},{24,25},{28,29}} | collective-permute-start | bytes 897032 | tf_op jit(solution)/shard_map/ppermute | solution.py:435
  12.3 2.6 %collective-permute-start = (s32[8]{0:T(128)S(1)}, s32[8]{0:T(128)S(1)}, u32[]{:S(2)}, u32[]{:S(2)}) collective-permute-start(s32[8]{0:T(128)S(1)} %get-tuple-element.76), channel_id=1, source_target_pairs={{2,0},{3,1},{6,4},{7,5},{10,8},{11,9},{14,12},{15,13},{18,16},{19,... | collective-permute-start | bytes 104 | tf_op jit(solution)/shard_map/ppermute | solution.py:485
  17.9 1.4 %collective-permute-start.3 = (bf16[1168,128]{1,0:T(8,128)(2,1)S(1)}, bf16[1168,128]{1,0:T(8,128)(2,1)S(1)}, u32[]{:S(2)}, u32[]{:S(2)}) collective-permute-start(bf16[1168,128]{1,0:T(8,128)(2,1)S(1)} %get-tuple-element.62), channel_id=1, source_target_pairs={{0,1},{4,5},{8,9},{12,13},{16,17},{20,21},{24,25},{28,29}} | collective-permute-start | bytes 897032 | tf_op jit(solution)/shard_map/ppermute | solution.py:435
  18.6 0.9 %collective-permute-start.2 = (bf16[1168,128]{1,0:T(8,128)(2,1)S(1)}, bf16[1168,128]{1,0:T(8,128)(2,1)S(1)}, u32[]{:S(2)}, u32[]{:S(2)}) collective-permute-start(bf16[1168,128]{1,0:T(8,128)(2,1)S(1)} %get-tuple-element.61), channel_id=1, source_target_pairs={{1,2},{5,6},{9,10},{13,14},{17,18},{21,22},{25,26},{29,30}} | collective-permute-start | bytes 897032 | tf_op jit(solution)/shard_map/ppermute | solution.py:435
  19.6 2.0 %collective-permute-start.5 = (bf16[1168,128]{1,0:T(8,128)(2,1)S(1)}, bf16[1168,128]{1,0:T(8,128)(2,1)S(1)}, u32[]{:S(2)}, u32[]{:S(2)}) collective-permute-start(bf16[1168,128]{1,0:T(8,128)(2,1)S(1)} %get-tuple-element.68), channel_id=1, source_target_pairs={{1,2},{5,6},{9,10},{13,14},{17,18},{21,22},{25,26},{29,30}} | collective-permute-start | bytes 897032 | tf_op jit(solution)/shard_map/ppermute | solution.py:435
  20.3 24.5 %collective-permute-start.4 = (bf16[1168,128]{1,0:T(8,128)(2,1)S(1)}, bf16[1168,128]{1,0:T(8,128)(2,1)S(1)}, u32[]{:S(2)}, u32[]{:S(2)}) collective-permute-start(bf16[1168,128]{1,0:T(8,128)(2,1)S(1)} %get-tuple-element.67), channel_id=1, source_target_pairs={{2,3},{6,7},{10,11},{14,15},{18,19},{22,23},{26,27},{30,31}} | collective-permute-start | bytes 897032 | tf_op jit(solution)/shard_map/ppermute | solution.py:435
  44.8 8.6 %collective-permute-start.6 = (bf16[1168,128]{1,0:T(8,128)(2,1)S(1)}, bf16[1168,128]{1,0:T(8,128)(2,1)S(1)}, u32[]{:S(2)}, u32[]{:S(2)}) collective-permute-start(bf16[1168,128]{1,0:T(8,128)(2,1)S(1)} %get-tuple-element.71), channel_id=1, source_target_pairs={{2,3},{6,7},{10,11},{14,15},{18,19},{22,23},{26,27},{30,31}} | collective-permute-start | bytes 897032 | tf_op jit(solution)/shard_map/ppermute | solution.py:435

commit v2 on v1

--- a/solution.py
+++ b/solution.py
@@ -87,12 +87,12 @@
 def extra_item(counts, mine):
     def one(k, state):
         momentum, before = state
-        extra = counts[k] - 1
+        extra = counts[0, k] - 1
         take = jnp.logical_and(momentum == k, before + extra <= mine)
         return (jnp.where(take, k + 1, momentum), jnp.where(take, before + extra, before))
 
-    momentum, before = lax.fori_loop(0, counts.shape[0], one, (jnp.int32(0), jnp.int32(0)))
-    momentum = jnp.minimum(momentum, counts.shape[0] - 1)
+    momentum, before = lax.fori_loop(0, counts.shape[1], one, (jnp.int32(0), jnp.int32(0)))
+    momentum = jnp.minimum(momentum, counts.shape[1] - 1)
     return momentum, jnp.clip(1 + mine - before, 0, EMAX - 1)
 
 
@@ -138,19 +138,14 @@
 
 
 def times_carried(coupled, g, left, parts):
-    last = (parts - 1) * LANE
-    for begin, width in ((last, 2 * LANE), (0, last), (last + 2 * LANE, last)):
-        product = jnp.dot(
-            coupled, g[:, begin : begin + width], preferred_element_type=F32
-        ).astype(BF16)
-        for k in range(width // LANE):
-            column = begin // LANE + k
-            half, c = (
-                (0, column)
-                if column < parts
-                else (1, parts - 1 if column == parts else column - parts - 1)
-            )
-            store_left(left, product[:, span(k)], half, c, parts)
+    product = jnp.dot(coupled, g[...], preferred_element_type=F32).astype(BF16)
+    for column in range(2 * parts):
+        half, c = (
+            (0, column)
+            if column < parts
+            else (1, parts - 1 if column == parts else column - parts - 1)
+        )
+        store_left(left, product[:, span(column)], half, c, parts)
 
 
 def finish_slab(s, times_turned, left, g, packed, inv_real, inv_imag, scales, weight, density, parts):
@@ -188,8 +183,9 @@
             if r != c:
                 g[span(c), span(place(parts, half, r))] = rounded.T
 
-    far = times_turned(left[2 * last :, :], last + LANE)
-    near = times_turned(left[: 2 * last, :], last)
+    turned = times_turned(left[...])
+    far = turned[2 * last :, :]
+    near = turned[: 2 * last, :]
     for c in range(parts):
         finish(parts - 1, c, far[:LANE, span(c)], far[LANE:, span(c)])
     for r in range(parts - 1):
@@ -210,7 +206,7 @@
 def first_segment(coupled_of, inv_real, inv_imag, scales, weight, g, left, sent, density):
     slabs, orbitals = inv_real.shape
     parts = orbitals // LANE
-    density[0:1, :] = -weight * inv_imag[0:1, :]
+    density[0:1, :] += -weight * inv_imag[0:1, :]
     for s in range(1, slabs):
         coupled = coupled_of(s)
         if s == 1:
@@ -222,9 +218,9 @@
         else:
             times_carried(coupled, g, left, parts)
 
-        def times_turned(rows, upto):
+        def times_turned(rows):
             return lax.dot_general(
-                rows, coupled[:upto], (((1,), (1,)), ((), ())), preferred_element_type=F32
+                rows, coupled, (((1,), (1,)), ((), ())), preferred_element_type=F32
             )
 
         finish_slab(
@@ -235,14 +231,16 @@
 
 def own_kernel(
     impulse_count,
-    constants_hbm, contact_hbm, onsite_hbm, hopping_hbm, potential_hbm, base_hbm, wave_hbm,
-    sent, density,
+    counts, constants_hbm, contact_hbm, onsite_hbm, hopping_hbm, potential_hbm, base_hbm, wave_hbm,
+    sent, density, spread,
     constants, contact, tables, base, wave, scales, g, left, small_sem, table_sem, couple_sem,
 ):
     slabs, orbitals = onsite_hbm.shape
     parts = orbitals // LANE
     position = lax.axis_index("en")
     density[...] = jnp.zeros_like(density)
+    lanes = lax.broadcasted_iota(jnp.int32, spread.shape, 1)
+    spread[...] = jnp.where(lanes == lax.axis_index("kt"), counts[0], 0)
 
     @pl.when(position == 0)
     def _():
@@ -285,20 +283,50 @@
         first_segment(coupled_of, inv_real, inv_imag, scales, weight, g, left, sent, density)
 
 
+def prepare(cosine, weight, inv_real, inv_imag, base, wave, couple, turned, scales, entry):
+    slabs, orbitals = inv_real.shape
+    parts = orbitals // LANE
+    form_scales(range(slabs), inv_real, inv_imag, scales, parts)
+    entry[:slabs, :] = inv_real
+    entry[slabs : 2 * slabs, :] = inv_imag
+    entry[2 * slabs :, :] = jnp.full((slabs, orbitals), weight, F32)
+    for s in range(slabs):
+        coupled = coupling_of(base[s], wave[s], cosine)
+        couple[s] = coupled
+        for r in range(parts):
+            for c in range(parts):
+                turned[s, span(c), span(r)] = coupled[span(r), span(c)].T
+
+
+def prepare_kernel(
+    impulse_count,
+    constants, contact, onsite, hopping, potential, base, wave,
+    couple, turned, scales, entry,
+):
+    position = lax.axis_index("en")
+
+    @pl.when(position > 0)
+    def _():
+        cosine, energy, weight = entry_amounts(
+            constants, impulse_count, lax.axis_index("kt"), jnp.int32(0)
+        )
+        inv_real, inv_imag = inverse_diagonal(
+            position, cosine, energy, contact, onsite, hopping, potential
+        )
+        prepare(cosine, weight, inv_real, inv_imag, base, wave, couple, turned, scales, entry)
+
+
 def extra_kernel(
     impulse_count,
     constants, contact, counts, onsite, hopping, potential, base, wave, so_far,
-    sent, density,
-    couple_own, turned_own, scales_own, entry_own,
-    couple_extra, turned_extra, scales_extra, entry_extra,
-    scales, g, left,
+    sent, density, couple, turned, scales, entry,
+    g, left,
 ):
     slabs, orbitals = onsite.shape
     parts = orbitals // LANE
     position = lax.axis_index("en")
-    mine = lax.axis_index("kt")
     density[...] = so_far[...]
-    momentum, level = extra_item(counts, mine)
+    momentum, level = extra_item(counts, lax.axis_index("kt"))
     cosine, energy, weight = entry_amounts(constants, impulse_count, momentum, level)
     inv_real, inv_imag = inverse_diagonal(
         position, cosine, energy, contact, onsite, hopping, potential
@@ -307,44 +335,15 @@
     @pl.when(position == 0)
     def _():
         form_scales(range(1, slabs), inv_real, inv_imag, scales, parts)
-        first = jnp.zeros_like(density)
-        kept = density[...]
-        density[...] = first
 
         def coupled_of(s):
             return coupling_of(base[s], wave[s], cosine)
 
         first_segment(coupled_of, inv_real, inv_imag, scales, weight, g, left, sent, density)
-        density[...] += kept
-
-    def prepare(cosine, weight, inv_real, inv_imag, couple, turned, scales_out, entry):
-        form_scales(range(slabs), inv_real, inv_imag, scales_out, parts)
-        entry[:slabs, :] = inv_real
-        entry[slabs : 2 * slabs, :] = inv_imag
-        entry[2 * slabs :, :] = jnp.full((slabs, orbitals), weight, F32)
-        for s in range(slabs):
-            coupled = coupling_of(base[s], wave[s], cosine)
-            couple[s] = coupled
-            for r in range(parts):
-                for c in range(parts):
-                    turned[s, span(c), span(r)] = coupled[span(r), span(c)].T
 
     @pl.when(position > 0)
     def _():
-        own_cosine, own_energy, own_weight = entry_amounts(
-            constants, impulse_count, mine, jnp.int32(0)
-        )
-        own_real, own_imag = inverse_diagonal(
-            position, own_cosine, own_energy, contact, onsite, hopping, potential
-        )
-        prepare(
-            own_cosine, own_weight, own_real, own_imag,
-            couple_own, turned_own, scales_own, entry_own,
-        )
-        prepare(
-            cosine, weight, inv_real, inv_imag,
-            couple_extra, turned_extra, scales_extra, entry_extra,
-        )
+        prepare(cosine, weight, inv_real, inv_imag, base, wave, couple, turned, scales, entry)
 
 
 def stage_kernel(stage, last_stage, couple, turned, scales, entry, arrived, so_far, *refs):
@@ -366,8 +365,8 @@
         for s in range(slabs):
             times_carried(couple[s], g, left, parts)
 
-            def times_turned(rows, upto):
-                return jnp.dot(rows, turned[s, :, :upto], preferred_element_type=F32)
+            def times_turned(rows):
+                return jnp.dot(rows, turned[s], preferred_element_type=F32)
 
             final = s == slabs - 1
             finish_slab(
@@ -423,7 +422,6 @@
     en_size = lax.axis_size("en")
     slabs, orbitals = onsite.shape
     parts = orbitals // LANE
-    position = lax.axis_index("en")
     impulse_count = counts.shape[0] * kt_size
     constants = jnp.asarray(item_constants(impulse_count))
     smem = pl.BlockSpec(memory_space=pltpu.SMEM)
@@ -445,25 +443,14 @@
         pltpu.VMEM((2 * orbitals, orbitals), BF16),
     ]
 
-    half = en_size // 2
-    counts_here = lax.cond(
-        position >= half,
-        lambda c: lax.all_gather(c, "kt", tiled=True),
-        lambda c: jnp.zeros((impulse_count,), jnp.int32),
-        counts,
-    )
-    pinned, counts_here = lax.optimization_barrier(
-        (
-            (constants, contact_slabs, onsite, hopping, potential_in, couple_base, couple_wave),
-            counts_here,
-        )
-    )
-    pinned = [pltpu.with_memory_space_constraint(t, pltpu.HBM) for t in pinned]
-    block, density = vmem_call(
+    given = (constants, contact_slabs, onsite, hopping, potential_in, couple_base, couple_wave)
+    pinned = [pltpu.with_memory_space_constraint(t, pltpu.HBM) for t in given]
+    made_shapes = (couple_shape, couple_shape, scales_shape, entry_shape)
+    block, density, spread = vmem_call(
         functools.partial(own_kernel, impulse_count),
-        (block_shape, density_shape),
-        pinned,
-        [hbm] * len(pinned),
+        (block_shape, density_shape, jax.ShapeDtypeStruct((1, impulse_count), jnp.int32)),
+        [counts] + pinned,
+        [smem] + [hbm] * len(pinned),
         [
             pltpu.SMEM(constants.shape, F32),
             pltpu.SMEM(contact_slabs.shape, jnp.int32),
@@ -482,23 +469,27 @@
         3 * flops,
     )
     arrived_own = forward(block, 0)
-    counts_all = counts_here + lax.ppermute(
-        counts_here, "en", [(p + half, p) for p in range(half)]
+    made_own = vmem_call(
+        functools.partial(prepare_kernel, impulse_count),
+        made_shapes,
+        given,
+        [smem] * 2 + [vmem] * 5,
+        [],
+        "prepare_own",
+        flops,
     )
-    held, density, *made = vmem_call(
+    spread, *made_own = lax.optimization_barrier((spread, *made_own))
+    counts_all = lax.psum(spread, "kt")
+    held, density, *made_extra = vmem_call(
         functools.partial(extra_kernel, impulse_count),
-        (block_shape, density_shape) + (couple_shape, couple_shape, scales_shape, entry_shape) * 2,
-        (
-            constants, contact_slabs, counts_all,
-            onsite, hopping, potential_in, couple_base, couple_wave, density,
-        ),
+        (block_shape, density_shape) + made_shapes,
+        given[:2] + (counts_all,) + given[2:] + (density,),
         [smem] * 3 + [vmem] * 6,
-        [scales_scratch] + work,
+        work,
         "first_extra",
         3 * flops,
         input_output_aliases={8: 1},
     )
-    made_own, made_extra = made[:4], made[4:]
 
     def run_stage(stage, made, arrived, density, name):
         last_stage = stage == en_size - 1

time: 68.2 us -> 68.4 us (level)
  local copies, waits for them, and re-layouts: 2.69 us -> 5.59 us
  waiting for transfers between devices: 27.5 us -> 24.9 us
  starting transfers between devices: 6.71 us -> 5.41 us
    cond x1 -> x0, blocking collectives: 8.01 us -> none
    psum x0 -> x1, blocking collectives: none -> 8.01 us  [body(): counts_all = lax.psum(spread, 'kt')]
    unnamed x14 -> x26, local copies, waits for them, and re-layouts: 0.04 us -> 5.58 us
    cond x3 -> x0, local copies, waits for them, and re-layouts: 2.65 us -> none
    ppermute x6, waiting for transfers between devices: 26.2 us -> 24.9 us  [forward(): return lax.ppermute(block, 'en', [(stage, stage + 1)])]
    ppermute x1 -> x0, starting transfers between devices: 1.29 us -> none  [body(): lax.ppermute(counts_here, 'en', [(p + half, p) for p in range(half)])]
    ppermute x1 -> x0, waiting for transfers between devices: 1.28 us -> none  [body(): lax.ppermute(counts_here, 'en', [(p + half, p) for p in range(half)])]
    pallas_call x8 -> x9, Pallas kernels: 11.8 us -> 12.3 us  [vmem_call(): pl.pallas_call(kernel, out_shape=tuple(outs), in_specs=in_specs, out_spec...]
  transfers between devices with their start and end apart: 7 -> 6, of which waited for: 3 -> 2; matrix products, arithmetic and copies ran while one was open for 0% -> 0% of each run, Pallas kernels for 11% -> 12%
where the time goes in v2:
time: 68.4 us; the launch traced here: 68.1 us
  waiting for transfers between devices  24.9 us (36%)
  blocking collectives  16 us (23%)
  Pallas kernels  14.7 us (21%)
  local copies, waits for them, and re-layouts  5.59 us (8%)
  starting transfers between devices  5.41 us (8%)
  between operations  1.53 us (2%)
    ppermute x6, waiting for transfers between devices, forward(): return lax.ppermute(block, 'en', [(stage, stage + 1)])  24.9 us
    pallas_call x9, Pallas kernels, vmem_call(): pl.pallas_call(kernel, out_shape=tuple(outs), in_specs=in_specs, out_spec...  12.3 us
    psum x1, blocking collectives, body(): counts_all = lax.psum(spread, 'kt')  8.01 us
    all_to_all x1, blocking collectives, gather_over(): return lax.all_to_all(copies, axis, 0, 0)  7.98 us
    unnamed x26, local copies, waits for them, and re-layouts  5.58 us
    ppermute x6, starting transfers between devices, forward(): return lax.ppermute(block, 'en', [(stage, stage + 1)])  5.41 us
    pallas_call x1, Pallas kernels, body(): pl.pallas_call(last_kernel, out_shape=(density_shape, density_shape), in_...  2.33 us
  transfers between devices with their start and end apart: 6, of which 2 were waited for; matrix products, arithmetic and copies ran while one was open for 0% of the time, Pallas kernels for 12%

profile of v2, /device:TPU:24, one launch (start us, length us, event | category | flops | bytes accessed | tf_op | source)
XLA Modules:
  0.0 68.1 jit_solution(12955051491408462117)
XLA Ops:
  1.3 0.0 copy-start
  1.3 0.0 copy-start.1
  1.3 0.0 copy-start.2
  1.3 0.0 copy-start.3
  1.3 0.0 copy-start.4
  1.3 0.0 copy-start.5
  1.3 0.0 copy-start.6
  1.3 0.1 first_own.1
  1.5 0.8 %collective-permute-start = (bf16[1168,128]{1,0:T(8,128)(2,1)S(1)}, bf16[1168,128]{1,0:T(8,128)(2,1)S(1)}, u32[]{:S(2)}, u32[]{:S(2)}) collective-permute-start(bf16[1168,128]{1,0:T(8,128)(2,1)S(1)} %get-tuple-element.49), channel_id=1, source_target_pairs={{0,1},{4,5},{8,9},{12,13},{16,17},{20,21},{24,25},{28,29}} | collective-permute-start | bytes 897032 | tf_op jit(solution)/shard_map/ppermute | solution.py:433
  2.3 0.2 copy-done
  2.5 0.4 copy-done.1
  2.9 0.0 copy-done.2
  2.9 0.0 copy-done.3
  2.9 0.0 copy-done.4
  2.9 0.0 copy-done.5
  2.9 0.0 copy-done.6
  2.9 1.7 %prepare_own.1 = (bf16[4,384,384]{2,1,0:T(8,128)(2,1)S(1)}, bf16[4,384,384]{2,1,0:T(8,128)(2,1)S(1)}, f32[4,1536,128]{2,1,0:T(8,128)S(1)}, f32[12,384]{1,0:T(8,128)S(1)}) custom-call(f32[12]{0:T(128)S(1)} %copy-done.6, s32[2]{0:T(128)S(1)} %copy-done.5, f32[4,384]{1,0:T(4,128)S(1)} %copy-done.2, f32[4,384]{1,0:T(4,128)S(1)} %copy-done.3, ...), custom_call_target="tpu_custom_call" | custom-call | flops 452984832 | bytes 2097152 | tf_op jit(solution)/shard_map/prepare_own/pallas_call | solution.py:380
  4.7 0.0 copy-start.7
  4.7 1.6 %copy-done.7 = f32[4,1536,128]{2,1,0:T(8,128)} copy-done((f32[4,1536,128]{2,1,0:T(8,128)}, f32[4,1536,128]{2,1,0:T(8,128)S(1)}, u32[]{:S(2)}) %copy-start.7) | copy-done | bytes 3145752
  6.3 0.0 copy-start.9
  6.3 1.0 %copy-done.9 = bf16[4,384,384]{2,1,0:T(8,128)(2,1)} copy-done((bf16[4,384,384]{2,1,0:T(8,128)(2,1)}, bf16[4,384,384]{2,1,0:T(8,128)(2,1)S(1)}, u32[]{:S(2)}) %copy-start.9) | copy-done | bytes 1179672
  7.3 0.0 copy-start.11
  7.3 1.1 %copy-done.11 = bf16[4,384,384]{2,1,0:T(8,128)(2,1)} copy-done((bf16[4,384,384]{2,1,0:T(8,128)(2,1)}, bf16[4,384,384]{2,1,0:T(8,128)(2,1)S(1)}, u32[]{:S(2)}) %copy-start.11) | copy-done | bytes 1179672
  8.4 8.0 %psum.7.counts = s32[1,8]{1,0:T(1,128)S(1)} all-reduce(s32[1,8]{1,0:T(1,128)S(1)} %get-tuple-element.39), channel_id=1, replica_groups=mesh['kt'=8,'en'=4] {'kt'}, use_global_device_ids=true, to_apply=%region_0.0 | all-reduce | flops 8 | bytes 64 | tf_op jit(solution)/shard_map/psum | solution.py:482
  16.4 0.0 copy-start.8
  16.4 0.0 copy-start.10
  16.4 1.8 %first_extra.1 = (bf16[1168,128]{1,0:T(8,128)(2,1)S(1)}, f32[4,384]{1,0:T(4,128)S(1)}, bf16[4,384,384]{2,1,0:T(8,128)(2,1)S(1)}, bf16[4,384,384]{2,1,0:T(8,128)(...) custom-call(f32[12]{0:T(128)S(1)} %copy-done.6, s32[2]{0:T(128)S(1)} %copy-done.5, ...), custom_call_target="tpu_custom_call", output_to_operand_aliasing={{1}: (8, {})} | custom-call | flops 1358954496 | bytes 2097152 | tf_op jit(solution)/shard_map/first_extra/pallas_call | solution.py:380
  18.2 0.0 collective-permute-done.arrived
  18.2 0.7 collective-permute-start.2
  18.9 0.0 copy-done.8
  18.9 0.0 copy-done.10
  18.9 0.0 copy-start.12
  18.9 1.3 %copy-done.12 = bf16[4,384,384]{2,1,0:T(8,128)(2,1)S(1)} copy-done((bf16[4,384,384]{2,1,0:T(8,128)(2,1)S(1)}, bf16[4,384,384]{2,1,0:T(8,128)(2,1)}, u32[]{:S(2)}) %copy-start.12) | copy-done | bytes 1179672
  20.2 0.7 collective-permute-start.1
  20.9 0.0 collective-permute-done.2.arrived
  20.9 0.2 stage_1_extra.1
  21.1 0.0 collective-permute-done.1.arrived
  21.1 0.7 collective-permute-start.4
  21.8 1.3 %collective-permute-start.3 = (bf16[1168,128]{1,0:T(8,128)(2,1)S(1)}, bf16[1168,128]{1,0:T(8,128)(2,1)S(1)}, u32[]{:S(2)}, u32[]{:S(2)}) collective-permute-start(bf16[1168,128]{1,0:T(8,128)(2,1)S(1)} %get-tuple-element.59), channel_id=1, source_target_pairs={{2,3},{6,7},{10,11},{14,15},{18,19},{22,23},{26,27},{30,31}} | collective-permute-start | bytes 897032 | tf_op jit(solution)/shard_map/ppermute | solution.py:433
  23.1 0.0 collective-permute-done.4.arrived
  23.1 21.9 %collective-permute-done.3.arrived = bf16[1168,128]{1,0:T(8,128)(2,1)S(1)} collective-permute-done((bf16[1168,128]{1,0:T(8,128)(2,1)S(1)}, bf16[1168,128]{1,0:T(8,128)(2,1)S(1)}, u32[]{:S(2)}, u32[]{:S(2)}) %collective-permute-start.3) | collective-permute-done | bytes 299040 | tf_op jit(solution)/shard_map/ppermute | solution.py:433
  45.0 1.3 %collective-permute-start.5 = (bf16[1168,128]{1,0:T(8,128)(2,1)S(1)}, bf16[1168,128]{1,0:T(8,128)(2,1)S(1)}, u32[]{:S(2)}, u32[]{:S(2)}) collective-permute-start(bf16[1168,128]{1,0:T(8,128)(2,1)S(1)} %get-tuple-element.63), channel_id=1, source_target_pairs={{2,3},{6,7},{10,11},{14,15},{18,19},{22,23},{26,27},{30,31}} | collective-permute-start | bytes 897032 | tf_op jit(solution)/shard_map/ppermute | solution.py:433
  46.3 4.3 %stage_3_own.1.so_far = f32[4,384]{1,0:T(4,128)S(1)} custom-call(bf16[4,384,384]{2,1,0:T(8,128)(2,1)S(1)} %copy-done.10, bf16[4,384,384]{2,1,0:T(8,128)(2,1)S(1)} %copy-done.12, f32[4,1536,128]{2,1,0:T(8,128)S(1)} %copy-done.8, f32[12,384]{1,0:T(8,128)S(1)} %get-tuple-element.48.entry, ...), custom_call_target="tpu_custom_call", output_to_operand_aliasing={{}: (5, {})} | custom-call | flops 1811939328 | bytes 2097152 | tf_op jit(solution)/shard_map/stage_3_own/pallas_call | solution.py:380
  50.7 3.0 %collective-permute-done.5.arrived = bf16[1168,128]{1,0:T(8,128)(2,1)S(1)} collective-permute-done((bf16[1168,128]{1,0:T(8,128)(2,1)S(1)}, bf16[1168,128]{1,0:T(8,128)(2,1)S(1)}, u32[]{:S(2)}, u32[]{:S(2)}) %collective-permute-start.5) | collective-permute-done | bytes 299040 | tf_op jit(solution)/shard_map/ppermute | solution.py:433
  53.7 4.1 %stage_3_extra.1 = f32[4,384]{1,0:T(4,128)S(1)} custom-call(bf16[4,384,384]{2,1,0:T(8,128)(2,1)S(1)} %get-tuple-element.41.couple, bf16[4,384,384]{2,1,0:T(8,128)(2,1)S(1)} %get-tuple-element.42.turned, f32[4,1536,128]{2,1,0:T(8,128)S(1)} %get-tuple-element.43.scales, f32[12,384]{1,0:T(8,128)S(1)} %get-tuple-element.44.entry, ...), custom_call_target="tpu_custom_call", output_to_operand_aliasing={{}: (5, {})} | custom-call | flops 1811939328 | bytes 2097152 | tf_op jit(solution)/shard_map/stage_3_extra/pallas_call | solution.py:380
  57.8 8.0 %all_to_all.5.gathered = f32[8,4,384]{2,1,0:T(4,128)} all-to-all(f32[8,4,384]{2,1,0:T(4,128)S(1)} %broadcast_in_dim.2), channel_id=1, replica_groups=mesh['kt'=8,'en'=4] {'kt'}, dimensions={0} | all-to-all | bytes 98304 | tf_op jit(solution)/shard_map/all_to_all | solution.py:407
  65.8 2.3 %last.1 = (f32[4,384]{1,0:T(4,128)}, f32[4,384]{1,0:T(4,128)}) custom-call(f32[8,4,384]{2,1,0:T(4,128)} %all_to_all.5.gathered, f32[4,384]{1,0:T(4,128)} %doping.1, f32[384,384]{1,0:T(8,128)} %inverse.1), custom_call_target="tpu_custom_call" | custom-call | tf_op jit(solution)/shard_map/last/pallas_call | solution.py:515
  (4 shorter events, 0.0 us)
Async XLA Ops:
  1.3 1.3 %copy-start = (bf16[4,384,384]{2,1,0:T(8,128)(2,1)S(1)}, bf16[4,384,384]{2,1,0:T(8,128)(2,1)}, u32[]{:S(2)}) copy-start(bf16[4,384,384]{2,1,0:T(8,128)(2,1)} %base.3) | copy-start | bytes 3538948
  1.3 1.6 %copy-start.1 = (bf16[4,384,384]{2,1,0:T(8,128)(2,1)S(1)}, bf16[4,384,384]{2,1,0:T(8,128)(2,1)}, u32[]{:S(2)}) copy-start(bf16[4,384,384]{2,1,0:T(8,128)(2,1)} %wave.3) | copy-start | bytes 3538948
  1.3 1.6 %copy-start.2 = (f32[4,384]{1,0:T(4,128)S(1)}, f32[4,384]{1,0:T(4,128)}, u32[]{:S(2)}) copy-start(f32[4,384]{1,0:T(4,128)} %onsite.3) | copy-start | bytes 18436
  1.3 1.6 %copy-start.3 = (f32[4,384]{1,0:T(4,128)S(1)}, f32[4,384]{1,0:T(4,128)}, u32[]{:S(2)}) copy-start(f32[4,384]{1,0:T(4,128)} %hopping.3) | copy-start | bytes 18436
  1.3 1.6 %copy-start.4 = (f32[4,384]{1,0:T(4,128)S(1)}, f32[4,384]{1,0:T(4,128)}, u32[]{:S(2)}) copy-start(f32[4,384]{1,0:T(4,128)} %potential.3) | copy-start | bytes 18436
  1.3 1.6 %copy-start.5 = (s32[2]{0:T(128)S(1)}, s32[2]{0:T(128)}, u32[]{:S(2)}) copy-start(s32[2]{0:T(128)} %contact.3) | copy-start | bytes 28
  1.3 1.6 %copy-start.6 = (f32[12]{0:T(128)S(1)}, f32[12]{0:T(128)}, u32[]{:S(2)}) copy-start(f32[12]{0:T(128)} %constant.2.clone.constants_hbm.constants) | copy-start | bytes 148
  1.5 16.7 %collective-permute-start = (bf16[1168,128]{1,0:T(8,128)(2,1)S(1)}, bf16[1168,128]{1,0:T(8,128)(2,1)S(1)}, u32[]{:S(2)}, u32[]{:S(2)}) collective-permute-start(bf16[1168,128]{1,0:T(8,128)(2,1)S(1)} %get-tuple-element.49), channel_id=1, source_target_pairs={{0,1},{4,5},{8,9},{12,13},{16,17},{20,21},{24,25},{28,29}} | collective-permute-start | bytes 897032 | tf_op jit(solution)/shard_map/ppermute | solution.py:433
  4.7 1.6 %copy-start.7 = (f32[4,1536,128]{2,1,0:T(8,128)}, f32[4,1536,128]{2,1,0:T(8,128)S(1)}, u32[]{:S(2)}) copy-start(f32[4,1536,128]{2,1,0:T(8,128)S(1)} %get-tuple-element.47.scales) | copy-start | bytes 9437188
  6.3 1.0 %copy-start.9 = (bf16[4,384,384]{2,1,0:T(8,128)(2,1)}, bf16[4,384,384]{2,1,0:T(8,128)(2,1)S(1)}, u32[]{:S(2)}) copy-start(bf16[4,384,384]{2,1,0:T(8,128)(2,1)S(1)} %get-tuple-element.45.couple) | copy-start | bytes 3538948
  7.3 1.1 %copy-start.11 = (bf16[4,384,384]{2,1,0:T(8,128)(2,1)}, bf16[4,384,384]{2,1,0:T(8,128)(2,1)S(1)}, u32[]{:S(2)}) copy-start(bf16[4,384,384]{2,1,0:T(8,128)(2,1)S(1)} %get-tuple-element.46.turned) | copy-start | bytes 3538948
  16.4 2.5 %copy-start.8 = (f32[4,1536,128]{2,1,0:T(8,128)S(1)}, f32[4,1536,128]{2,1,0:T(8,128)}, u32[]{:S(2)}) copy-start(f32[4,1536,128]{2,1,0:T(8,128)} %copy-done.7) | copy-start | bytes 9437188
  16.4 2.5 %copy-start.10 = (bf16[4,384,384]{2,1,0:T(8,128)(2,1)S(1)}, bf16[4,384,384]{2,1,0:T(8,128)(2,1)}, u32[]{:S(2)}) copy-start(bf16[4,384,384]{2,1,0:T(8,128)(2,1)} %copy-done.9) | copy-start | bytes 3538948
  18.2 2.7 %collective-permute-start.2 = (bf16[1168,128]{1,0:T(8,128)(2,1)S(1)}, bf16[1168,128]{1,0:T(8,128)(2,1)S(1)}, u32[]{:S(2)}, u32[]{:S(2)}) collective-permute-start(bf16[1168,128]{1,0:T(8,128)(2,1)S(1)} %get-tuple-element.54), channel_id=1, source_target_pairs={{0,1},{4,5},{8,9},{12,13},{16,17},{20,21},{24,25},{28,29}} | collective-permute-start | bytes 897032 | tf_op jit(solution)/shard_map/ppermute | solution.py:433
  18.9 1.3 %copy-start.12 = (bf16[4,384,384]{2,1,0:T(8,128)(2,1)S(1)}, bf16[4,384,384]{2,1,0:T(8,128)(2,1)}, u32[]{:S(2)}) copy-start(bf16[4,384,384]{2,1,0:T(8,128)(2,1)} %copy-done.11) | copy-start | bytes 3538948
  20.2 0.9 %collective-permute-start.1 = (bf16[1168,128]{1,0:T(8,128)(2,1)S(1)}, bf16[1168,128]{1,0:T(8,128)(2,1)S(1)}, u32[]{:S(2)}, u32[]{:S(2)}) collective-permute-start(bf16[1168,128]{1,0:T(8,128)(2,1)S(1)} %get-tuple-element.53), channel_id=1, source_target_pairs={{1,2},{5,6},{9,10},{13,14},{17,18},{21,22},{25,26},{29,30}} | collective-permute-start | bytes 897032 | tf_op jit(solution)/shard_map/ppermute | solution.py:433
  21.1 2.0 %collective-permute-start.4 = (bf16[1168,128]{1,0:T(8,128)(2,1)S(1)}, bf16[1168,128]{1,0:T(8,128)(2,1)S(1)}, u32[]{:S(2)}, u32[]{:S(2)}) collective-permute-start(bf16[1168,128]{1,0:T(8,128)(2,1)S(1)} %get-tuple-element.60), channel_id=1, source_target_pairs={{1,2},{5,6},{9,10},{13,14},{17,18},{21,22},{25,26},{29,30}} | collective-permute-start | bytes 897032 | tf_op jit(solution)/shard_map/ppermute | solution.py:433
  21.8 23.2 %collective-permute-start.3 = (bf16[1168,128]{1,0:T(8,128)(2,1)S(1)}, bf16[1168,128]{1,0:T(8,128)(2,1)S(1)}, u32[]{:S(2)}, u32[]{:S(2)}) collective-permute-start(bf16[1168,128]{1,0:T(8,128)(2,1)S(1)} %get-tuple-element.59), channel_id=1, source_target_pairs={{2,3},{6,7},{10,11},{14,15},{18,19},{22,23},{26,27},{30,31}} | collective-permute-start | bytes 897032 | tf_op jit(solution)/shard_map/ppermute | solution.py:433
  45.0 8.6 %collective-permute-start.5 = (bf16[1168,128]{1,0:T(8,128)(2,1)S(1)}, bf16[1168,128]{1,0:T(8,128)(2,1)S(1)}, u32[]{:S(2)}, u32[]{:S(2)}) collective-permute-start(bf16[1168,128]{1,0:T(8,128)(2,1)S(1)} %get-tuple-element.63), channel_id=1, source_target_pairs={{2,3},{6,7},{10,11},{14,15},{18,19},{22,23},{26,27},{30,31}} | collective-permute-start | bytes 897032 | tf_op jit(solution)/shard_map/ppermute | solution.py:433

commit v3 on v2

v3 whole, which is shorter than its diff:
```python
import functools

import jax
import jax.numpy as jnp
import numpy as np
from jax import lax
from jax.experimental import pallas as pl
from jax.experimental.pallas import tpu as pltpu
from jax.sharding import PartitionSpec as P

EMAX = 4
LANE = 128
F32 = jnp.float32
BF16 = jnp.bfloat16

bottom_sample_mark = -1.0
sample_gap = 0.25
electrode_filling = -0.5
boltzmann_spread = 0.1
broadening = 1.0
contact_width = 0.5


def item_constants(impulse_count):
    wave = np.float32(np.pi) * (np.arange(impulse_count, dtype=np.float32) + np.float32(0.5))
    cosine = np.cos(wave / np.float32(impulse_count))
    energy = bottom_sample_mark + sample_gap * np.arange(EMAX)
    weight = sample_gap / (1.0 + np.exp((energy - electrode_filling) / boltzmann_spread)) / np.pi
    return np.concatenate([cosine, weight]).astype(np.float32)


def span(k):
    return slice(k * LANE, (k + 1) * LANE)


def place(parts, half, c):
    if c == parts - 1:
        return parts - 1 + half
    return c if half == 0 else parts + 1 + c


def blocks_on_or_below(parts):
    return [(r, c) for r in range(parts) for c in range(r + 1)]


def packed_rows(orbitals):
    parts = orbitals // LANE
    return parts * parts * LANE + 16


def pairs_below(parts):
    return [(r, c) for r in range(parts) for c in range(r)]


def pair_slot(parts, r, c, half):
    return 2 * pairs_below(parts).index((r, c)) + half


def middle_slot(parts, r):
    return parts * (parts - 1) + r


def tile_indices():
    rows = lax.broadcasted_iota(jnp.int32, (LANE, LANE), 0)
    cols = lax.broadcasted_iota(jnp.int32, (LANE, LANE), 1)
    return rows, cols


def unpack_blocks(packed, put, parts):
    rows, cols = tile_indices()
    for r, c in pairs_below(parts):
        for half in range(2):
            block = packed[span(pair_slot(parts, r, c, half)), :]
            put(half, r, c, block)
            put(half, c, r, block.T)
    at = parts * parts * LANE
    for r in range(parts):
        block = packed[span(middle_slot(parts, r)), :]
        turned = block.T
        middle = packed[at : at + 16, :][r : r + 1, :]
        put(0, r, r, jnp.where(rows <= cols, block, turned))
        put(1, r, r, jnp.where(rows > cols, block, jnp.where(rows == cols, middle, turned)))


def pack_block(packed, r, c, green_real, green_imag, parts):
    rows, cols = tile_indices()
    if r == c:
        packed[span(middle_slot(parts, r)), :] = jnp.where(
            rows <= cols, green_real, green_imag
        ).astype(BF16)
    else:
        packed[span(pair_slot(parts, r, c, 0)), :] = green_real.astype(BF16)
        packed[span(pair_slot(parts, r, c, 1)), :] = green_imag.astype(BF16)


def pack_middles(packed, middles, parts):
    rest = jnp.zeros((16 - parts, LANE), F32)
    at = parts * parts * LANE
    packed[at : at + 16, :] = jnp.concatenate(middles + [rest], axis=0).astype(BF16)


def diagonal_row(block):
    rows, cols = tile_indices()
    return jnp.sum(jnp.where(rows == cols, block, 0.0), axis=0, keepdims=True)


def takes_first_levels():
    return lax.axis_index("kt") % 2 == 1


def first_level_item(slot):
    return lax.axis_index("kt") - 1 + slot, jnp.int32(0)


def item_of(counts, slot):
    wanted = lax.axis_index("kt") + slot

    def one(k, state):
        momentum, before = state
        extra = counts[k] - 1
        take = jnp.logical_and(momentum == k, before + extra <= wanted)
        return (jnp.where(take, k + 1, momentum), jnp.where(take, before + extra, before))

    momentum, before = lax.fori_loop(0, counts.shape[0], one, (jnp.int32(0), jnp.int32(0)))
    momentum = jnp.minimum(momentum, counts.shape[0] - 1)
    level = jnp.clip(1 + wanted - before, 0, EMAX - 1)
    own_momentum, own_level = first_level_item(slot)
    own = takes_first_levels()
    return jnp.where(own, own_momentum, momentum), jnp.where(own, own_level, level)


def entry_amounts(constants, impulse_count, momentum, level):
    energy = bottom_sample_mark + sample_gap * level.astype(F32)
    return constants[momentum], energy, constants[impulse_count + level]


def inverse_diagonal(position, cosine, energy, contact, onsite, hopping, potential):
    slabs, orbitals = onsite.shape
    diag_real = energy + (-onsite[...] - potential[...]) - cosine * hopping[...]
    slab_in = lax.broadcasted_iota(jnp.int32, (slabs, orbitals), 0) + position * slabs
    at_contact = jnp.logical_or(slab_in == contact[0], slab_in == contact[1])
    diag_imag = broadening + contact_width * at_contact.astype(F32)
    magnitude = diag_real * diag_real + diag_imag * diag_imag
    inv_real = diag_real / magnitude
    inv_imag = -diag_imag / magnitude
    return inv_real, inv_imag


def scale_rows(parts):
    return 2 * len(blocks_on_or_below(parts)) * LANE


def form_scales(slabs_wanted, inv_real, inv_imag, scales, parts):
    slabs = inv_real.shape[0]
    down = jnp.concatenate([inv_real, inv_imag], axis=0).T
    for s in slabs_wanted:
        for k, (r, c) in enumerate(blocks_on_or_below(parts)):
            real_col = down[span(r), s : s + 1]
            imag_col = down[span(r), slabs + s : slabs + s + 1]
            rr = inv_real[s : s + 1, span(c)]
            ri = inv_imag[s : s + 1, span(c)]
            scales[s, span(2 * k), :] = real_col * rr - imag_col * ri
            scales[s, span(2 * k + 1), :] = real_col * ri + imag_col * rr


def store_left(left, piece, half, c, parts):
    last = (parts - 1) * LANE
    left[half * last : (half + 1) * last, span(c)] = piece[:last]
    bottom = 2 * last + half * LANE
    left[bottom : bottom + LANE, span(c)] = piece[last:]


def times_carried(coupled, g, left, parts):
    product = jnp.dot(coupled, g[...], preferred_element_type=F32).astype(BF16)
    for column in range(2 * parts):
        half, c = (
            (0, column)
            if column < parts
            else (1, parts - 1 if column == parts else column - parts - 1)
        )
        store_left(left, product[:, span(column)], half, c, parts)


def finish_slab(
    s, times_turned, left, g, packed, real_row, imag_row, scales, note, parts, local=None
):
    last = (parts - 1) * LANE
    rows, cols = tile_indices()
    diagonal = rows == cols
    numbers = {block: k for k, block in enumerate(blocks_on_or_below(parts))}
    middles = {}

    def finish(r, c, sr, si):
        k = numbers[r, c]
        scale_real = scales[s, span(2 * k), :]
        scale_imag = scales[s, span(2 * k + 1), :]
        green_real = scale_real * sr - scale_imag * si
        green_imag = scale_real * si + scale_imag * sr
        if r == c:
            green_real = green_real + jnp.where(diagonal, real_row[:, span(c)], 0.0)
            green_imag = green_imag + jnp.where(diagonal, imag_row[:, span(c)], 0.0)
            if note is not None:
                middles[r] = diagonal_row(green_imag)
                note(r, middles[r])
        if packed is not None:
            pack_block(packed, r, c, green_real, green_imag, parts)
        if local is not None:
            local[span(2 * k), :] = green_real
            local[span(2 * k + 1), :] = green_imag
        if g is None:
            return
        for half, green in ((0, green_real), (1, green_imag)):
            rounded = green.astype(BF16)
            g[span(r), span(place(parts, half, c))] = rounded
            if r != c:
                g[span(c), span(place(parts, half, r))] = rounded.T

    turned = times_turned(left[...])
    far = turned[2 * last :, :]
    near = turned[: 2 * last, :]
    for c in range(parts):
        finish(parts - 1, c, far[:LANE, span(c)], far[LANE:, span(c)])
    for r in range(parts - 1):
        for c in range(r + 1):
            finish(r, c, near[span(r), span(c)], near[last:, :][span(r), span(c)])
    if packed is not None:
        pack_middles(packed, [middles[r] for r in range(parts)], parts)


def coupling_of(base, wave, cosine):
    return (base.astype(F32) + cosine * wave.astype(F32)).astype(BF16)


def first_segment(
    coupled_of, inv_real, inv_imag, scales, weight, g, left, sent, density, local=None
):
    slabs, orbitals = inv_real.shape
    parts = orbitals // LANE
    if density is not None:
        density[0:1, :] += -weight * inv_imag[0:1, :]
    for s in range(1, slabs):
        coupled = coupled_of(s)
        if s == 1:
            wide = coupled.astype(F32)
            for half, inv in ((0, inv_real), (1, inv_imag)):
                piece = (wide * inv[0:1, :].astype(BF16).astype(F32)).astype(BF16)
                for c in range(parts):
                    store_left(left, piece[:, span(c)], half, c, parts)
        else:
            times_carried(coupled, g, left, parts)

        def times_turned(rows):
            return lax.dot_general(
                rows, coupled, (((1,), (1,)), ((), ())), preferred_element_type=F32
            )

        def note(r, middle):
            density[s : s + 1, span(r)] += -weight * middle

        final = s == slabs - 1
        finish_slab(
            s, times_turned, left, None if final else g, sent if final else None,
            inv_real[s : s + 1, :], inv_imag[s : s + 1, :], scales, None if density is None else note, parts,
            local if final else None,
        )


def copies_of_constants(constants_hbm, contact_hbm, constants, contact, sem):
    return [
        pltpu.make_async_copy(constants_hbm, constants, sem.at[0]),
        pltpu.make_async_copy(contact_hbm, contact, sem.at[1]),
    ]


def copies_of_couplings(base_hbm, wave_hbm, base, wave, sem, slabs_wanted):
    return {
        s: (
            pltpu.make_async_copy(base_hbm.at[s], base.at[s], sem.at[0, s]),
            pltpu.make_async_copy(wave_hbm.at[s], wave.at[s], sem.at[1, s]),
        )
        for s in slabs_wanted
    }


def lead_kernel(
    impulse_count,
    constants_hbm, contact_hbm, onsite_hbm, hopping_hbm, potential_hbm, base_hbm, wave_hbm,
    sent, density, base, wave,
    constants, contact, tables, scales, g, left, small_sem, table_sem, couple_sem,
):
    slabs, orbitals = onsite_hbm.shape
    parts = orbitals // LANE
    position = lax.axis_index("en")
    density[...] = jnp.zeros_like(density)

    @pl.when(position == 0)
    def _():
        small_copies = copies_of_constants(
            constants_hbm, contact_hbm, constants, contact, small_sem
        ) + [
            pltpu.make_async_copy(source, tables.at[k], table_sem.at[k])
            for k, source in enumerate((onsite_hbm, hopping_hbm, potential_hbm))
        ]
        couple_copies = copies_of_couplings(
            base_hbm, wave_hbm, base, wave, couple_sem, range(1, slabs)
        )
        for copy in small_copies:
            copy.start()
        for s in couple_copies:
            for copy in couple_copies[s]:
                copy.start()
        for copy in small_copies:
            copy.wait()

        @pl.when(takes_first_levels())
        def _():
            momentum, level = first_level_item(0)
            cosine, energy, weight = entry_amounts(
                constants, impulse_count, momentum, level
            )
            inv_real, inv_imag = inverse_diagonal(
                position, cosine, energy, contact, tables.at[0], tables.at[1], tables.at[2]
            )
            form_scales(range(1, slabs), inv_real, inv_imag, scales, parts)

            def coupled_of(s):
                for copy in couple_copies[s]:
                    copy.wait()
                return coupling_of(base[s], wave[s], cosine)

            first_segment(
                coupled_of, inv_real, inv_imag, scales, weight, g, left, sent, density
            )

        @pl.when(jnp.logical_not(takes_first_levels()))
        def _():
            for s in couple_copies:
                for copy in couple_copies[s]:
                    copy.wait()


    @pl.when(position > 0)
    def _():
        couple_copies = copies_of_couplings(
            base_hbm, wave_hbm, base, wave, couple_sem, range(slabs)
        )
        for s in couple_copies:
            for copy in couple_copies[s]:
                copy.start()
        for s in couple_copies:
            for copy in couple_copies[s]:
                copy.wait()


def begin_kernel(
    impulse_count, slot,
    constants, contact, counts, onsite, hopping, potential, base, wave, so_far, held,
    density, sent,
    scales, g, left,
):
    del held
    slabs, orbitals = onsite.shape
    parts = orbitals // LANE
    position = lax.axis_index("en")
    density[...] = so_far[...]
    active = position == 0
    if slot == 0:
        active = jnp.logical_and(active, jnp.logical_not(takes_first_levels()))

    @pl.when(active)
    def _():
        momentum, level = item_of(counts, slot)
        cosine, energy, weight = entry_amounts(constants, impulse_count, momentum, level)
        inv_real, inv_imag = inverse_diagonal(
            position, cosine, energy, contact, onsite, hopping, potential
        )
        form_scales(range(1, slabs), inv_real, inv_imag, scales, parts)

        def coupled_of(s):
            return coupling_of(base[s], wave[s], cosine)

        first_segment(coupled_of, inv_real, inv_imag, scales, weight, g, left, sent, density)


def prepare(cosine, weight, inv_real, inv_imag, base, wave, couple, turned, scales, entry):
    slabs, orbitals = inv_real.shape
    parts = orbitals // LANE
    form_scales(range(slabs), inv_real, inv_imag, scales, parts)
    for s in range(slabs):
        entry[s] = jnp.broadcast_to(inv_real[s : s + 1, :], entry.shape[1:])
        entry[slabs + s] = jnp.broadcast_to(inv_imag[s : s + 1, :], entry.shape[1:])
    entry[2 * slabs] = jnp.full(entry.shape[1:], weight, F32)

    def one(s, carry):
        coupled = coupling_of(base[s], wave[s], cosine)
        couple[s] = coupled
        for r in range(parts):
            for c in range(parts):
                turned[s, span(c), span(r)] = coupled[span(r), span(c)].T
        return carry

    lax.fori_loop(0, slabs, one, 0)


def prepare_kernel(
    impulse_count,
    constants, contact, counts, onsite, hopping, potential, base, wave,
    couple_0, turned_0, scales_0, entry_0,
    couple_1, turned_1, scales_1, entry_1,
):
    position = lax.axis_index("en")

    @pl.when(position > 0)
    def _():
        for slot, made in (
            (0, (couple_0, turned_0, scales_0, entry_0)),
            (1, (couple_1, turned_1, scales_1, entry_1)),
        ):
            momentum, level = item_of(counts, slot)
            cosine, energy, weight = entry_amounts(constants, impulse_count, momentum, level)
            inv_real, inv_imag = inverse_diagonal(
                position, cosine, energy, contact, onsite, hopping, potential
            )
            prepare(cosine, weight, inv_real, inv_imag, base, wave, *made)


def stage_kernel(stage, last_stage, couple, turned, scales, entry, arrived, so_far, *refs):
    if last_stage:
        density, g, left, noted = refs
        sent = None
    else:
        sent, density, g, left, noted = refs
    slabs, orbitals = so_far.shape
    parts = orbitals // LANE
    density[...] = so_far[...]

    @pl.when(lax.axis_index("en") == stage)
    def _():
        def put(half, r, c, block):
            column = place(parts, half, c)
            g[span(r), span(column)] = block

        unpack_blocks(arrived, put, parts)
        def slab(s, final):
            times_carried(couple[s], g, left, parts)

            def times_turned(rows):
                return jnp.dot(rows, turned[s], preferred_element_type=F32)

            def note(r, middle):
                noted[s, 0:1, span(r)] = middle

            finish_slab(
                s, times_turned, left, None if final else g, sent if final else None,
                entry[s, 0:1, :], entry[slabs + s, 0:1, :], scales, note, parts,
            )

        def inner(s, carry):
            slab(s, False)
            return carry

        lax.fori_loop(0, slabs - 1, inner, 0)
        slab(slabs - 1, True)
        for s in range(slabs):
            density[s : s + 1, :] += -entry[2 * slabs, 0:1, :] * noted[s, 0:1, :]


def operator_kernel(stage, couple, turned, scales, entry, local, carrier, cross, g, left):
    slabs, orbitals, _ = couple.shape
    parts = orbitals // LANE

    @pl.when(lax.axis_index("en") == stage)
    def _():
        inv_real = jnp.concatenate([entry[s, 0:1, :] for s in range(slabs)], axis=0)
        inv_imag = jnp.concatenate([entry[slabs + s, 0:1, :] for s in range(slabs)], axis=0)
        first_segment(
            lambda s: couple[s], inv_real, inv_imag, scales, None, g, left, None, None, local
        )
        down = jnp.concatenate([inv_real, inv_imag], axis=0).T
        for s in range(slabs):
            real_col = down[:, s : s + 1]
            imag_col = down[:, slabs + s : slabs + s + 1]
            if s == 0:
                wide = couple[0].astype(F32)
                real, imag = real_col * wide, imag_col * wide
            else:
                product = jnp.dot(couple[s], carrier[...], preferred_element_type=F32)
                from_real, from_imag = product[:, :orbitals], product[:, orbitals:]
                real = real_col * from_real - imag_col * from_imag
                imag = real_col * from_imag + imag_col * from_real
            carrier[:, :orbitals] = real.astype(BF16)
            carrier[:, orbitals:] = imag.astype(BF16)
        for r in range(parts):
            for c in range(parts):
                real = carrier[span(r), span(c)].T
                imag = carrier[span(r), span(parts + c)].T
                cross[span(c), span(r)] = real
                cross[span(parts + c), span(parts + r)] = real
                cross[span(c), span(parts + r)] = imag
                cross[span(parts + c), span(r)] = -imag


def pass_kernel(stage, local, carrier, cross, arrived, sent, wide, half_way):
    orbitals = carrier.shape[0]
    parts = orbitals // LANE

    @pl.when(lax.axis_index("en") == stage)
    def _():
        def put(half, r, c, block):
            if half == 0:
                wide[span(r), span(c)] = block
                wide[span(parts + r), span(parts + c)] = block
            else:
                wide[span(r), span(parts + c)] = block
                wide[span(parts + r), span(c)] = -block

        unpack_blocks(arrived, put, parts)
        half_way[...] = jnp.dot(carrier[...], wide[...], preferred_element_type=F32).astype(BF16)
        out = jnp.dot(half_way[...], cross[...], preferred_element_type=F32)
        middles = []
        for k, (r, c) in enumerate(blocks_on_or_below(parts)):
            green_real = local[span(2 * k), :] + out[span(r), span(c)]
            green_imag = local[span(2 * k + 1), :] + out[span(r), span(parts + c)]
            pack_block(sent, r, c, green_real, green_imag, parts)
            if r == c:
                middles.append(diagonal_row(green_imag))
        pack_middles(sent, middles, parts)


def vmem_call(kernel, outs, operands, in_specs, scratch, name, flops, **more):
    vmem = pl.BlockSpec(memory_space=pltpu.VMEM)
    return pl.pallas_call(
        kernel,
        out_shape=tuple(outs),
        in_specs=in_specs,
        out_specs=(vmem,) * len(outs),
        scratch_shapes=scratch,
        compiler_params=pltpu.CompilerParams(vmem_limit_bytes=16 * 2**20),
        cost_estimate=pl.CostEstimate(flops=flops, bytes_accessed=2**21, transcendentals=0),
        name=name,
        **more,
    )(*operands)


def split_kernel(inverse, high, middle, low):
    for r in range(inverse.shape[0] // LANE):
        for c in range(inverse.shape[1] // LANE):
            block = inverse[span(r), span(c)].T
            for part in (high, middle, low):
                rounded = block.astype(BF16)
                part[span(c), span(r)] = rounded
                block = block - rounded.astype(F32)


def last_kernel(gathered, doping, high, middle, low, summed, potential):
    total = jnp.sum(gathered[...], axis=0)
    summed[...] = total
    rest = total - doping[...]
    pieces = []
    for _ in range(3):
        pieces.append(rest.astype(BF16).astype(F32))
        rest = rest - pieces[-1]
    rows = total.shape[0]
    answer = jnp.zeros_like(total)
    for count, part in ((1, low), (2, middle), (3, high)):
        padded = -(-3 * rows // 16) * 16 - count * rows
        stacked = jnp.concatenate(
            pieces[:count] + [jnp.zeros((padded, total.shape[1]), F32)], axis=0
        ).astype(BF16)
        product = jnp.dot(stacked, part[...], preferred_element_type=F32)
        for k in reversed(range(count)):
            answer = answer + product[k * rows : (k + 1) * rows]
    potential[...] = answer


def gather_over(values, axis):
    copies = jnp.broadcast_to(values[None], (lax.axis_size(axis),) + values.shape)
    return lax.all_to_all(copies, axis, 0, 0)


def body(
    counts,
    contact_slabs,
    onsite,
    hopping,
    potential_in,
    couple_base,
    couple_wave,
    doping,
    poisson_inverse,
):
    kt_size = lax.axis_size("kt")
    en_size = lax.axis_size("en")
    slabs, orbitals = onsite.shape
    parts = orbitals // LANE
    impulse_count = counts.shape[0] * kt_size
    constants = jnp.asarray(item_constants(impulse_count))
    smem = pl.BlockSpec(memory_space=pltpu.SMEM)
    hbm = pl.BlockSpec(memory_space=pltpu.HBM)
    vmem = pl.BlockSpec(memory_space=pltpu.VMEM)
    flops = 2 * slabs * orbitals**3

    def forward(block, stage):
        return lax.ppermute(block, "en", [(stage, stage + 1)])

    block_shape = jax.ShapeDtypeStruct((packed_rows(orbitals), LANE), BF16)
    density_shape = jax.ShapeDtypeStruct((slabs, orbitals), F32)
    couple_shape = jax.ShapeDtypeStruct((slabs, orbitals, orbitals), BF16)
    scales_shape = jax.ShapeDtypeStruct((slabs, scale_rows(parts), LANE), F32)
    entry_shape = jax.ShapeDtypeStruct((2 * slabs + 1, 8, orbitals), F32)
    scales_scratch = pltpu.VMEM(scales_shape.shape, F32)
    work = [
        pltpu.VMEM((orbitals, 2 * orbitals), BF16),
        pltpu.VMEM((2 * orbitals, orbitals), BF16),
    ]

    counts_all = lax.all_to_all(jnp.tile(counts, kt_size), "kt", 0, 0, tiled=True)
    given = (constants, contact_slabs, onsite, hopping, potential_in, couple_base, couple_wave)
    pinned = [pltpu.with_memory_space_constraint(t, pltpu.HBM) for t in given]
    block, density, *loaded = vmem_call(
        functools.partial(lead_kernel, impulse_count),
        (block_shape, density_shape, couple_shape, couple_shape),
        pinned,
        [hbm] * len(pinned),
        [
            pltpu.SMEM(constants.shape, F32),
            pltpu.SMEM(contact_slabs.shape, jnp.int32),
            pltpu.VMEM((3, slabs, orbitals), F32),
            scales_scratch,
        ]
        + work
        + [
            pltpu.SemaphoreType.DMA((2,)),
            pltpu.SemaphoreType.DMA((3,)),
            pltpu.SemaphoreType.DMA((2, slabs)),
        ],
        "lead",
        3 * flops,
    )
    block, counts_all = lax.optimization_barrier((block, counts_all))
    small = (constants, contact_slabs, counts_all, onsite, hopping, potential_in)

    def begin(slot, density, held):
        return vmem_call(
            functools.partial(begin_kernel, impulse_count, slot),
            (density_shape, block_shape),
            (*small, *loaded, density, held),
            [smem] * 3 + [vmem] * 7,
            [scales_scratch] + work,
            f"begin_{slot}",
            3 * flops,
            input_output_aliases={8: 0, 9: 1},
        )

    density, block = begin(0, density, block)
    arrived = [forward(block, 0)]
    density, block = begin(1, density, jnp.zeros(block_shape.shape, BF16))
    arrived.append(forward(block, 0))
    made = vmem_call(
        functools.partial(prepare_kernel, impulse_count),
        (couple_shape, couple_shape, scales_shape, entry_shape) * 2,
        (*small, *loaded),
        [smem] * 3 + [vmem] * 5,
        [],
        "prepare",
        flops,
    )
    made = (made[:4], made[4:])

    def run_stage(stage, made, arrived, density, name, last_stage):
        results = vmem_call(
            functools.partial(stage_kernel, stage, last_stage),
            (density_shape,) if last_stage else (block_shape, density_shape),
            (*made, arrived, density),
            [vmem] * 6,
            work + [pltpu.VMEM((slabs, 8, orbitals), F32)],
            f"stage_{stage}_{name}",
            4 * flops,
            input_output_aliases={5: 0 if last_stage else 1},
        )
        return (None, *results) if last_stage else results

    def operator_of(stage, slot):
        return vmem_call(
            functools.partial(operator_kernel, stage),
            (
                jax.ShapeDtypeStruct((scale_rows(parts), LANE), F32),
                jax.ShapeDtypeStruct((orbitals, 2 * orbitals), BF16),
                jax.ShapeDtypeStruct((2 * orbitals, 2 * orbitals), BF16),
            ),
            made[slot],
            [vmem] * 4,
            work,
            f"operator_{stage}_{slot}",
            6 * flops,
        )

    def pass_on(stage, slot, operator, block):
        return vmem_call(
            functools.partial(pass_kernel, stage),
            (block_shape,),
            (*operator, block),
            [vmem] * 4,
            [
                pltpu.VMEM((2 * orbitals, 2 * orbitals), BF16),
                pltpu.VMEM((orbitals, 2 * orbitals), BF16),
            ],
            f"pass_{stage}_{slot}",
            2 * flops,
        )[0]

    by_operator = range(2, en_size - 1)
    operators = {
        stage: [operator_of(stage, slot) for slot in range(2)] for stage in by_operator
    }
    waiting = []
    for stage in range(1, en_size):
        for slot in range(2):
            if stage in by_operator:
                waiting.append((stage, slot, arrived[slot]))
                block = pass_on(stage, slot, operators[stage][slot], arrived[slot])
            else:
                block, density = run_stage(
                    stage, made[slot], arrived[slot], density, f"{slot}", stage == en_size - 1
                )
            if stage < en_size - 1:
                arrived[slot] = forward(block, stage)
        if stage == en_size - 2:
            for early, slot, came in waiting:
                _, density = run_stage(early, made[slot], came, density, f"{slot}_density", True)
    part_shape = jax.ShapeDtypeStruct(poisson_inverse.shape, BF16)
    inverse, _ = lax.optimization_barrier((poisson_inverse, made[1][3]))
    split = vmem_call(
        split_kernel, (part_shape,) * 3, (inverse,), [vmem], [], "split_inverse", 2 * flops
    )
    density, *split = lax.optimization_barrier((density, *split))
    return vmem_call(
        last_kernel,
        (density_shape, density_shape),
        (gather_over(density, "kt"), doping, *split),
        [vmem] * 5,
        [],
        "last",
        flops // slabs,
    )


def solution(mesh):
    return jax.shard_map(
        body,
        mesh=mesh,
        in_specs=(
            P("kt"),
            P(),
            P("en", None),
            P("en", None),
            P("en", None),
            P("en", None, None),
            P("en", None, None),
            P("en", None),
            P(),
        ),
        out_specs=(P("en", None), P("en", None)),
        check_vma=False,
    )
```

time: 68.4 us -> 64.7 us (0.946)
  blocking collectives: 16 us -> 7.31 us
  local copies, waits for them, and re-layouts: 5.59 us -> 1.54 us
  starting transfers between devices: 5.41 us -> 9.03 us
  waiting for transfers between devices: 24.9 us -> 28.5 us
  Pallas kernels: 14.7 us -> 16.1 us
    psum x1 -> x0, blocking collectives: 8.01 us -> none  [body(): counts_all = lax.psum(spread, 'kt')]
    unnamed x26 -> x14, local copies, waits for them, and re-layouts: 5.58 us -> 0.89 us
    pallas_call x9 -> x16, Pallas kernels: 12.3 us -> 16.1 us  [vmem_call(): pl.pallas_call(kernel, out_shape=tuple(outs), in_specs=in_specs, out_spec...]
    all_to_all x0 -> x1, starting transfers between devices: none -> 3.72 us  [body(): lax.all_to_all(jnp.tile(counts, kt_size), 'kt', 0, 0, tiled=True)]
    all_to_all x0 -> x1, waiting for transfers between devices: none -> 2.8 us  [body(): lax.all_to_all(jnp.tile(counts, kt_size), 'kt', 0, 0, tiled=True)]
    pallas_call x1 -> x0, Pallas kernels: 2.33 us -> none  [body(): pl.pallas_call(last_kernel, out_shape=(density_shape, density_shape), in_...]
    ppermute x6, waiting for transfers between devices: 24.9 us -> 25.7 us  [forward(): return lax.ppermute(block, 'en', [(stage, stage + 1)])]
  transfers between devices with their start and end apart: 6 -> 7, of which waited for: 2 -> 3; matrix products, arithmetic and copies ran while one was open for 0% -> 0% of each run, Pallas kernels for 12% -> 11%
where the time goes in v3:
time: 64.7 us; the launch traced here: 64.3 us
  waiting for transfers between devices  28.5 us (44%)
  Pallas kernels  16.1 us (25%)
  starting transfers between devices  9.03 us (14%)
  blocking collectives  7.31 us (11%)
  between operations  1.57 us (2%)
  local copies, waits for them, and re-layouts  1.54 us (2%)
    ppermute x6, waiting for transfers between devices, forward(): return lax.ppermute(block, 'en', [(stage, stage + 1)])  25.7 us
    pallas_call x16, Pallas kernels, vmem_call(): pl.pallas_call(kernel, out_shape=tuple(outs), in_specs=in_specs, out_spec...  16.1 us
    all_to_all x1, blocking collectives, gather_over(): return lax.all_to_all(copies, axis, 0, 0)  7.31 us
    ppermute x6, starting transfers between devices, forward(): return lax.ppermute(block, 'en', [(stage, stage + 1)])  5.3 us
    all_to_all x1, starting transfers between devices, body(): lax.all_to_all(jnp.tile(counts, kt_size), 'kt', 0, 0, tiled=True)  3.72 us
    all_to_all x1, waiting for transfers between devices, body(): lax.all_to_all(jnp.tile(counts, kt_size), 'kt', 0, 0, tiled=True)  2.8 us
  transfers between devices with their start and end apart: 7, of which 3 were waited for; matrix products, arithmetic and copies ran while one was open for 0% of the time, Pallas kernels for 11%

profile of v3, /device:TPU:24, one launch (start us, length us, event | category | flops | bytes accessed | tf_op | source)
XLA Modules:
  0.0 64.3 jit_solution(7375179789467818133)
XLA Ops:
  1.3 0.6 tile.10
  1.9 3.7 %all-to-all-start = ((s32[8,1,1]{2,1,0:T(1,128)}), s32[8,1,1]{2,1,0:T(1,128)S(1)}, u32[]{:S(2)}, u32[]{:S(2)}) async-start(s32[8,1,1]{2,1,0:T(1,128)} %tile.10), calls=%async_computation | async-start | bytes 8192 | tf_op jit(solution)/shard_map/all_to_all | solution.py:617
  5.6 0.0 copy-start.1
  5.6 0.0 copy-start.2
  5.6 0.0 copy-start.3
  5.6 0.0 copy-start.4
  5.6 0.0 copy-start.5
  5.6 1.7 %lead.1 = (bf16[1168,128]{1,0:T(8,128)(2,1)S(1)}, f32[4,384]{1,0:T(4,128)S(1)}, bf16[4,384,384]{2,1,0:T(8,128)(2,1)S(1)}, bf16[4,384,384]{2,1,0:T(8,128)(2,1)S(1)}) custom-call(f32[12]{0:T(128)} %constant.4.clone.constants_hbm.constants, s32[2]{0:T(128)} %contact.5, f32[4,384]{1,0:T(4,128)} %onsite.5, f32[4,384]{1,0:T(4,128)} %hopping.5, ...), custom_call_target="tpu_custom_call" | custom-call | flops 1358954496 | bytes 2097152 | tf_op jit(solution)/shard_map/lead/pallas_call | solution.py:532
  7.4 2.8 %all-to-all-done = s32[8,1,1]{2,1,0:T(1,128)S(1)} async-done(((s32[8,1,1]{2,1,0:T(1,128)}), s32[8,1,1]{2,1,0:T(1,128)S(1)}, u32[]{:S(2)}, u32[]{:S(2)}) %all-to-all-start) | async-done | bytes 64 | tf_op jit(solution)/shard_map/all_to_all | solution.py:617
  10.2 0.2 reduce.counts
  10.4 0.0 copy-done.1
  10.4 0.0 copy-done.2
  10.4 0.0 copy-done.3
  10.4 0.0 copy-done.4
  10.4 0.0 copy-done.5
  10.5 3.4 %prepare.1 = (bf16[4,384,384]{2,1,0:T(8,128)(2,1)S(1)}, bf16[4,384,384]{2,1,0:T(8,128)(2,1)S(1)}, f32[4,1536,128]{2,1,0:T(8,128)S(1)}, f32[9,8,384]{2,1,0:T(8,12...) custom-call(f32[12]{0:T(128)S(1)} %copy-done.5, ...), custom_call_target="tpu_custom_call" | custom-call | flops 452984832 | bytes 2097152 | tf_op jit(solution)/shard_map/prepare/pallas_call | solution.py:532
  13.9 0.6 begin_0.1
  14.4 0.7 %collective-permute-start.1 = (bf16[1168,128]{1,0:T(8,128)(2,1)S(1)}, bf16[1168,128]{1,0:T(8,128)(2,1)S(1)}, u32[]{:S(2)}, u32[]{:S(2)}) collective-permute-start(bf16[1168,128]{1,0:T(8,128)(2,1)S(1)} %get-tuple-element.57), channel_id=1, source_target_pairs={{0,1},{4,5},{8,9},{12,13},{16,17},{20,21},{24,25},{28,29}} | collective-permute-start | bytes 897032 | tf_op jit(solution)/shard_map/ppermute | solution.py:604
  15.2 0.6 begin_1.1
  15.7 0.7 %collective-permute-start = (bf16[1168,128]{1,0:T(8,128)(2,1)S(1)}, bf16[1168,128]{1,0:T(8,128)(2,1)S(1)}, u32[]{:S(2)}, u32[]{:S(2)}) collective-permute-start(bf16[1168,128]{1,0:T(8,128)(2,1)S(1)} %get-tuple-element.52), channel_id=1, source_target_pairs={{0,1},{4,5},{8,9},{12,13},{16,17},{20,21},{24,25},{28,29}} | collective-permute-start | bytes 897032 | tf_op jit(solution)/shard_map/ppermute | solution.py:604
  16.4 0.0 copy-start.6
  16.4 0.2 operator_2_0.1
  16.6 0.9 %copy-done.6 = f32[384,384]{1,0:T(8,128)S(1)} copy-done((f32[384,384]{1,0:T(8,128)S(1)}, f32[384,384]{1,0:T(8,128)}, u32[]{:S(2)}) %copy-start.6) | copy-done | bytes 589848
  17.5 0.2 split_inverse.1
  17.7 0.0 collective-permute-done.1.arrived
  17.8 0.7 %collective-permute-start.4 = (bf16[1168,128]{1,0:T(8,128)(2,1)S(1)}, bf16[1168,128]{1,0:T(8,128)(2,1)S(1)}, u32[]{:S(2)}, u32[]{:S(2)}) collective-permute-start(bf16[1168,128]{1,0:T(8,128)(2,1)S(1)} %get-tuple-element.64), channel_id=1, source_target_pairs={{1,2},{5,6},{9,10},{13,14},{17,18},{21,22},{25,26},{29,30}} | collective-permute-start | bytes 897032 | tf_op jit(solution)/shard_map/ppermute | solution.py:604
  18.5 0.0 collective-permute-done.arrived
  18.5 0.7 %collective-permute-start.2 = (bf16[1168,128]{1,0:T(8,128)(2,1)S(1)}, bf16[1168,128]{1,0:T(8,128)(2,1)S(1)}, u32[]{:S(2)}, u32[]{:S(2)}) collective-permute-start(bf16[1168,128]{1,0:T(8,128)(2,1)S(1)} %get-tuple-element.60), channel_id=1, source_target_pairs={{1,2},{5,6},{9,10},{13,14},{17,18},{21,22},{25,26},{29,30}} | collective-permute-start | bytes 897032 | tf_op jit(solution)/shard_map/ppermute | solution.py:604
  19.2 0.0 collective-permute-done.4.arrived
  19.2 0.2 pass_2_0.1
  19.5 1.3 %collective-permute-start.5 = (bf16[1168,128]{1,0:T(8,128)(2,1)S(1)}, bf16[1168,128]{1,0:T(8,128)(2,1)S(1)}, u32[]{:S(2)}, u32[]{:S(2)}) collective-permute-start(bf16[1168,128]{1,0:T(8,128)(2,1)S(1)} %pass_2_0.1), channel_id=1, source_target_pairs={{2,3},{6,7},{10,11},{14,15},{18,19},{22,23},{26,27},{30,31}} | collective-permute-start | bytes 897032 | tf_op jit(solution)/shard_map/ppermute | solution.py:604
  20.8 0.0 collective-permute-done.2.arrived
  20.8 1.3 %collective-permute-start.3 = (bf16[1168,128]{1,0:T(8,128)(2,1)S(1)}, bf16[1168,128]{1,0:T(8,128)(2,1)S(1)}, u32[]{:S(2)}, u32[]{:S(2)}) collective-permute-start(bf16[1168,128]{1,0:T(8,128)(2,1)S(1)} %pass_2_1.1), channel_id=1, source_target_pairs={{2,3},{6,7},{10,11},{14,15},{18,19},{22,23},{26,27},{30,31}} | collective-permute-start | bytes 897032 | tf_op jit(solution)/shard_map/ppermute | solution.py:604
  22.1 23.0 %collective-permute-done.5.arrived = bf16[1168,128]{1,0:T(8,128)(2,1)S(1)} collective-permute-done((bf16[1168,128]{1,0:T(8,128)(2,1)S(1)}, bf16[1168,128]{1,0:T(8,128)(2,1)S(1)}, u32[]{:S(2)}, u32[]{:S(2)}) %collective-permute-start.5) | collective-permute-done | bytes 299040 | tf_op jit(solution)/shard_map/ppermute | solution.py:604
  45.1 4.2 %stage_3_0.1.so_far = f32[4,384]{1,0:T(4,128)S(1)} custom-call(bf16[4,384,384]{2,1,0:T(8,128)(2,1)S(1)} %get-tuple-element.53.couple, bf16[4,384,384]{2,1,0:T(8,128)(2,1)S(1)} %get-tuple-element.54.turned, f32[4,1536,128]{2,1,0:T(8,128)S(1)} %get-tuple-element.55.scales, f32[9,8,384]{2,1,0:T(8,128)S(1)} %get-tuple-element.56.entry, ...), custom_call_target="tpu_custom_call", output_to_operand_aliasing={{}: (5, {})} | custom-call | flops 1811939328 | bytes 2097152 | tf_op jit(solution)/shard_map/stage_3_0/pallas_call | solution.py:532
  49.3 0.0 copy-start
  49.3 2.7 %collective-permute-done.3.arrived = bf16[1168,128]{1,0:T(8,128)(2,1)S(1)} collective-permute-done((bf16[1168,128]{1,0:T(8,128)(2,1)S(1)}, bf16[1168,128]{1,0:T(8,128)(2,1)S(1)}, u32[]{:S(2)}, u32[]{:S(2)}) %collective-permute-start.3) | collective-permute-done | bytes 299040 | tf_op jit(solution)/shard_map/ppermute | solution.py:604
  52.0 4.1 %stage_3_1.1 = f32[4,384]{1,0:T(4,128)S(1)} custom-call(bf16[4,384,384]{2,1,0:T(8,128)(2,1)S(1)} %get-tuple-element.42.couple, bf16[4,384,384]{2,1,0:T(8,128)(2,1)S(1)} %get-tuple-element.43.turned, f32[4,1536,128]{2,1,0:T(8,128)S(1)} %get-tuple-element.44.scales, f32[9,8,384]{2,1,0:T(8,128)S(1)} %get-tuple-element.45.entry, ...), custom_call_target="tpu_custom_call", output_to_operand_aliasing={{}: (5, {})} | custom-call | flops 1811939328 | bytes 2097152 | tf_op jit(solution)/shard_map/stage_3_1/pallas_call | solution.py:532
  56.2 7.3 %all_to_all.14.gathered = f32[8,4,384]{2,1,0:T(4,128)S(1)} all-to-all(f32[8,4,384]{2,1,0:T(4,128)S(1)} %broadcast_in_dim.10), channel_id=1, replica_groups=mesh['kt'=8,'en'=4] {'kt'}, dimensions={0} | all-to-all | bytes 98304 | tf_op jit(solution)/shard_map/all_to_all | solution.py:578
  63.5 0.0 copy-done
  63.5 0.9 %last.1 = (f32[4,384]{1,0:T(4,128)}, f32[4,384]{1,0:T(4,128)}) custom-call(f32[8,4,384]{2,1,0:T(4,128)S(1)} %all_to_all.14.gathered, f32[4,384]{1,0:T(4,128)S(1)} %copy-done, bf16[384,384]{1,0:T(8,128)(2,1)S(1)} %get-tuple-element.71.high, bf16[384,384]{1,0:T(8,128)(2,1)S(1)} %get-tuple-element.72.middle, bf16[384,384]{1,0:T(8,128)(2,1)S(1)} %get-tuple-element.73.low), custom_call_target="tpu_custom_call" | custom-call | flops 113246208 | bytes 2097152 | tf_op jit(solution)/shard_map/last/pallas_call | solution.py:532
  (8 shorter events, 0.1 us)
Async XLA Ops:
  1.9 8.3 %all-to-all-start = ((s32[8,1,1]{2,1,0:T(1,128)}), s32[8,1,1]{2,1,0:T(1,128)S(1)}, u32[]{:S(2)}, u32[]{:S(2)}) async-start(s32[8,1,1]{2,1,0:T(1,128)} %tile.10), calls=%async_computation | async-start | bytes 8192 | tf_op jit(solution)/shard_map/all_to_all | solution.py:617
  5.6 4.8 %copy-start.1 = (f32[4,384]{1,0:T(4,128)S(1)}, f32[4,384]{1,0:T(4,128)}, u32[]{:S(2)}) copy-start(f32[4,384]{1,0:T(4,128)} %onsite.5) | copy-start | bytes 18436
  5.6 4.8 %copy-start.2 = (f32[4,384]{1,0:T(4,128)S(1)}, f32[4,384]{1,0:T(4,128)}, u32[]{:S(2)}) copy-start(f32[4,384]{1,0:T(4,128)} %hopping.5) | copy-start | bytes 18436
  5.6 4.8 %copy-start.3 = (f32[4,384]{1,0:T(4,128)S(1)}, f32[4,384]{1,0:T(4,128)}, u32[]{:S(2)}) copy-start(f32[4,384]{1,0:T(4,128)} %potential.5) | copy-start | bytes 18436
  5.6 4.8 %copy-start.4 = (s32[2]{0:T(128)S(1)}, s32[2]{0:T(128)}, u32[]{:S(2)}) copy-start(s32[2]{0:T(128)} %contact.5) | copy-start | bytes 28
  5.6 4.8 %copy-start.5 = (f32[12]{0:T(128)S(1)}, f32[12]{0:T(128)}, u32[]{:S(2)}) copy-start(f32[12]{0:T(128)} %constant.4.clone.constants_hbm.constants) | copy-start | bytes 148
  14.4 3.3 %collective-permute-start.1 = (bf16[1168,128]{1,0:T(8,128)(2,1)S(1)}, bf16[1168,128]{1,0:T(8,128)(2,1)S(1)}, u32[]{:S(2)}, u32[]{:S(2)}) collective-permute-start(bf16[1168,128]{1,0:T(8,128)(2,1)S(1)} %get-tuple-element.57), channel_id=1, source_target_pairs={{0,1},{4,5},{8,9},{12,13},{16,17},{20,21},{24,25},{28,29}} | collective-permute-start | bytes 897032 | tf_op jit(solution)/shard_map/ppermute | solution.py:604
  15.7 2.7 %collective-permute-start = (bf16[1168,128]{1,0:T(8,128)(2,1)S(1)}, bf16[1168,128]{1,0:T(8,128)(2,1)S(1)}, u32[]{:S(2)}, u32[]{:S(2)}) collective-permute-start(bf16[1168,128]{1,0:T(8,128)(2,1)S(1)} %get-tuple-element.52), channel_id=1, source_target_pairs={{0,1},{4,5},{8,9},{12,13},{16,17},{20,21},{24,25},{28,29}} | collective-permute-start | bytes 897032 | tf_op jit(solution)/shard_map/ppermute | solution.py:604
  16.4 1.1 %copy-start.6 = (f32[384,384]{1,0:T(8,128)S(1)}, f32[384,384]{1,0:T(8,128)}, u32[]{:S(2)}) copy-start(f32[384,384]{1,0:T(8,128)} %inverse) | copy-start | bytes 1769476
  17.8 1.4 %collective-permute-start.4 = (bf16[1168,128]{1,0:T(8,128)(2,1)S(1)}, bf16[1168,128]{1,0:T(8,128)(2,1)S(1)}, u32[]{:S(2)}, u32[]{:S(2)}) collective-permute-start(bf16[1168,128]{1,0:T(8,128)(2,1)S(1)} %get-tuple-element.64), channel_id=1, source_target_pairs={{1,2},{5,6},{9,10},{13,14},{17,18},{21,22},{25,26},{29,30}} | collective-permute-start | bytes 897032 | tf_op jit(solution)/shard_map/ppermute | solution.py:604
  18.5 2.3 %collective-permute-start.2 = (bf16[1168,128]{1,0:T(8,128)(2,1)S(1)}, bf16[1168,128]{1,0:T(8,128)(2,1)S(1)}, u32[]{:S(2)}, u32[]{:S(2)}) collective-permute-start(bf16[1168,128]{1,0:T(8,128)(2,1)S(1)} %get-tuple-element.60), channel_id=1, source_target_pairs={{1,2},{5,6},{9,10},{13,14},{17,18},{21,22},{25,26},{29,30}} | collective-permute-start | bytes 897032 | tf_op jit(solution)/shard_map/ppermute | solution.py:604
  19.5 25.6 %collective-permute-start.5 = (bf16[1168,128]{1,0:T(8,128)(2,1)S(1)}, bf16[1168,128]{1,0:T(8,128)(2,1)S(1)}, u32[]{:S(2)}, u32[]{:S(2)}) collective-permute-start(bf16[1168,128]{1,0:T(8,128)(2,1)S(1)} %pass_2_0.1), channel_id=1, source_target_pairs={{2,3},{6,7},{10,11},{14,15},{18,19},{22,23},{26,27},{30,31}} | collective-permute-start | bytes 897032 | tf_op jit(solution)/shard_map/ppermute | solution.py:604
  20.8 31.2 %collective-permute-start.3 = (bf16[1168,128]{1,0:T(8,128)(2,1)S(1)}, bf16[1168,128]{1,0:T(8,128)(2,1)S(1)}, u32[]{:S(2)}, u32[]{:S(2)}) collective-permute-start(bf16[1168,128]{1,0:T(8,128)(2,1)S(1)} %pass_2_1.1), channel_id=1, source_target_pairs={{2,3},{6,7},{10,11},{14,15},{18,19},{22,23},{26,27},{30,31}} | collective-permute-start | bytes 897032 | tf_op jit(solution)/shard_map/ppermute | solution.py:604
  49.3 14.2 %copy-start = (f32[4,384]{1,0:T(4,128)S(1)}, f32[4,384]{1,0:T(4,128)}, u32[]{:S(2)}) copy-start(f32[4,384]{1,0:T(4,128)} %doping.1) | copy-start | bytes 18436

commit v4 on v3

--- a/solution.py
+++ b/solution.py
@@ -352,11 +352,23 @@
                 copy.wait()
 
 
+def with_scalars(refs, scratch, sem):
+    copies = [
+        pltpu.make_async_copy(source, target, sem.at[k])
+        for k, (source, target) in enumerate(zip(refs, scratch))
+    ]
+    for copy in copies:
+        copy.start()
+    for copy in copies:
+        copy.wait()
+
+
 def begin_kernel(
     impulse_count, slot,
-    constants, contact, counts, onsite, hopping, potential, base, wave, so_far, held,
+    constants_ref, contact_ref, counts_ref,
+    onsite, hopping, potential, base, wave, so_far, held,
     density, sent,
-    scales, g, left,
+    constants, contact, counts, scalar_sem, scales, g, left,
 ):
     del held
     slabs, orbitals = onsite.shape
@@ -369,6 +381,9 @@
 
     @pl.when(active)
     def _():
+        with_scalars(
+            (constants_ref, contact_ref, counts_ref), (constants, contact, counts), scalar_sem
+        )
         momentum, level = item_of(counts, slot)
         cosine, energy, weight = entry_amounts(constants, impulse_count, momentum, level)
         inv_real, inv_imag = inverse_diagonal(
@@ -404,14 +419,18 @@
 
 def prepare_kernel(
     impulse_count,
-    constants, contact, counts, onsite, hopping, potential, base, wave,
+    constants_ref, contact_ref, counts_ref, onsite, hopping, potential, base, wave,
     couple_0, turned_0, scales_0, entry_0,
     couple_1, turned_1, scales_1, entry_1,
+    constants, contact, counts, scalar_sem,
 ):
     position = lax.axis_index("en")
 
     @pl.when(position > 0)
     def _():
+        with_scalars(
+            (constants_ref, contact_ref, counts_ref), (constants, contact, counts), scalar_sem
+        )
         for slot, made in (
             (0, (couple_0, turned_0, scales_0, entry_0)),
             (1, (couple_1, turned_1, scales_1, entry_1)),
@@ -424,23 +443,25 @@
             prepare(cosine, weight, inv_real, inv_imag, base, wave, *made)
 
 
-def stage_kernel(stage, last_stage, couple, turned, scales, entry, arrived, so_far, *refs):
-    if last_stage:
-        density, g, left, noted = refs
-        sent = None
-    else:
-        sent, density, g, left, noted = refs
+def density_kernel(couple, turned, scales, entry, so_far, *refs):
+    arrived, (density, g, left, noted) = refs[:-4], refs[-4:]
     slabs, orbitals = so_far.shape
     parts = orbitals // LANE
+    position = lax.axis_index("en")
     density[...] = so_far[...]
 
-    @pl.when(lax.axis_index("en") == stage)
+    def put(half, r, c, block):
+        column = place(parts, half, c)
+        g[span(r), span(column)] = block
+
+    for stage, block in enumerate(arrived, 1):
+
+        @pl.when(position == stage)
+        def _():
+            unpack_blocks(block, put, parts)
+
+    @pl.when(position > 0)
     def _():
-        def put(half, r, c, block):
-            column = place(parts, half, c)
-            g[span(r), span(column)] = block
-
-        unpack_blocks(arrived, put, parts)
         def slab(s, final):
             times_carried(couple[s], g, left, parts)
 
@@ -451,7 +472,7 @@
                 noted[s, 0:1, span(r)] = middle
 
             finish_slab(
-                s, times_turned, left, None if final else g, sent if final else None,
+                s, times_turned, left, None if final else g, None,
                 entry[s, 0:1, :], entry[slabs + s, 0:1, :], scales, note, parts,
             )
 
@@ -465,11 +486,12 @@
             density[s : s + 1, :] += -entry[2 * slabs, 0:1, :] * noted[s, 0:1, :]
 
 
-def operator_kernel(stage, couple, turned, scales, entry, local, carrier, cross, g, left):
+def operator_kernel(couple, turned, scales, entry, local, carrier, cross, g, left):
     slabs, orbitals, _ = couple.shape
     parts = orbitals // LANE
-
-    @pl.when(lax.axis_index("en") == stage)
+    position = lax.axis_index("en")
+
+    @pl.when(jnp.logical_and(position > 0, position < lax.axis_size("en") - 1))
     def _():
         inv_real = jnp.concatenate([entry[s, 0:1, :] for s in range(slabs)], axis=0)
         inv_imag = jnp.concatenate([entry[slabs + s, 0:1, :] for s in range(slabs)], axis=0)
@@ -640,13 +662,21 @@
     block, counts_all = lax.optimization_barrier((block, counts_all))
     small = (constants, contact_slabs, counts_all, onsite, hopping, potential_in)
 
+    anywhere = pl.BlockSpec(memory_space=pl.ANY)
+    scalar_scratch = [
+        pltpu.SMEM(constants.shape, F32),
+        pltpu.SMEM(contact_slabs.shape, jnp.int32),
+        pltpu.SMEM(counts_all.shape, jnp.int32),
+        pltpu.SemaphoreType.DMA((3,)),
+    ]
+
     def begin(slot, density, held):
         return vmem_call(
             functools.partial(begin_kernel, impulse_count, slot),
             (density_shape, block_shape),
             (*small, *loaded, density, held),
-            [smem] * 3 + [vmem] * 7,
-            [scales_scratch] + work,
+            [anywhere] * 3 + [vmem] * 7,
+            scalar_scratch + [scales_scratch] + work,
             f"begin_{slot}",
             3 * flops,
             input_output_aliases={8: 0, 9: 1},
@@ -656,42 +686,30 @@
     arrived = [forward(block, 0)]
     density, block = begin(1, density, jnp.zeros(block_shape.shape, BF16))
     arrived.append(forward(block, 0))
+    small, _ = lax.optimization_barrier((small, block))
     made = vmem_call(
         functools.partial(prepare_kernel, impulse_count),
         (couple_shape, couple_shape, scales_shape, entry_shape) * 2,
         (*small, *loaded),
-        [smem] * 3 + [vmem] * 5,
-        [],
+        [anywhere] * 3 + [vmem] * 5,
+        scalar_scratch,
         "prepare",
         flops,
     )
-    made = (made[:4], made[4:])
-
-    def run_stage(stage, made, arrived, density, name, last_stage):
-        results = vmem_call(
-            functools.partial(stage_kernel, stage, last_stage),
-            (density_shape,) if last_stage else (block_shape, density_shape),
-            (*made, arrived, density),
-            [vmem] * 6,
-            work + [pltpu.VMEM((slabs, 8, orbitals), F32)],
-            f"stage_{stage}_{name}",
-            4 * flops,
-            input_output_aliases={5: 0 if last_stage else 1},
-        )
-        return (None, *results) if last_stage else results
-
-    def operator_of(stage, slot):
+    made = [made[:4], made[4:]]
+
+    def operator_of(slot, made):
         return vmem_call(
-            functools.partial(operator_kernel, stage),
+            operator_kernel,
             (
                 jax.ShapeDtypeStruct((scale_rows(parts), LANE), F32),
                 jax.ShapeDtypeStruct((orbitals, 2 * orbitals), BF16),
                 jax.ShapeDtypeStruct((2 * orbitals, 2 * orbitals), BF16),
             ),
-            made[slot],
+            made,
             [vmem] * 4,
             work,
-            f"operator_{stage}_{slot}",
+            f"operator_{slot}",
             6 * flops,
         )
 
@@ -709,27 +727,32 @@
             2 * flops,
         )[0]
 
-    by_operator = range(2, en_size - 1)
-    operators = {
-        stage: [operator_of(stage, slot) for slot in range(2)] for stage in by_operator
-    }
-    waiting = []
-    for stage in range(1, en_size):
+    def densities(slot, density, came):
+        return vmem_call(
+            density_kernel,
+            (density_shape,),
+            (*made[slot], density, *came),
+            [vmem] * (5 + len(came)),
+            work + [pltpu.VMEM((slabs, 8, orbitals), F32)],
+            f"density_{slot}",
+            4 * flops,
+            input_output_aliases={4: 0},
+        )[0]
+
+    operators = []
+    came = [[arrived[0]], [arrived[1]]]
+    for stage in range(1, en_size - 1):
         for slot in range(2):
-            if stage in by_operator:
-                waiting.append((stage, slot, arrived[slot]))
-                block = pass_on(stage, slot, operators[stage][slot], arrived[slot])
-            else:
-                block, density = run_stage(
-                    stage, made[slot], arrived[slot], density, f"{slot}", stage == en_size - 1
-                )
-            if stage < en_size - 1:
-                arrived[slot] = forward(block, stage)
-        if stage == en_size - 2:
-            for early, slot, came in waiting:
-                _, density = run_stage(early, made[slot], came, density, f"{slot}_density", True)
+            if stage == 1:
+                if slot == 1:
+                    made[1], _ = lax.optimization_barrier((made[1], block))
+                operators.append(operator_of(slot, made[slot]))
+            block = pass_on(stage, slot, operators[slot], came[slot][-1])
+            came[slot].append(forward(block, stage))
+    for slot in range(2):
+        density = densities(slot, density, came[slot])
     part_shape = jax.ShapeDtypeStruct(poisson_inverse.shape, BF16)
-    inverse, _ = lax.optimization_barrier((poisson_inverse, made[1][3]))
+    inverse, _ = lax.optimization_barrier((poisson_inverse, block))
     split = vmem_call(
         split_kernel, (part_shape,) * 3, (inverse,), [vmem], [], "split_inverse", 2 * flops
     )

time: 64.7 us -> 59.3 us (0.917)
  waiting for transfers between devices: 28.5 us -> 24.9 us
  Pallas kernels: 16.1 us -> 14.8 us
  local copies, waits for them, and re-layouts: 1.54 us -> 0.69 us
    ppermute x6, waiting for transfers between devices: 25.7 us -> 22.1 us  [forward(): return lax.ppermute(block, 'en', [(stage, stage + 1)])]
    pallas_call x16 -> x14, Pallas kernels: 16.1 us -> 14.8 us  [vmem_call(): pl.pallas_call(kernel, out_shape=tuple(outs), in_specs=in_specs, out_spec...]
    unnamed x14, local copies, waits for them, and re-layouts: 0.89 us -> 0.04 us
  transfers between devices with their start and end apart: 7 -> 7, of which waited for: 3 -> 3; matrix products, arithmetic and copies ran while one was open for 0% -> 0% of each run, Pallas kernels for 11% -> 17%
where the time goes in v4:
time: 59.3 us; the launch traced here: 59 us
  waiting for transfers between devices  24.9 us (42%)
  Pallas kernels  14.8 us (25%)
  starting transfers between devices  9.38 us (16%)
  blocking collectives  7.31 us (12%)
  between operations  1.57 us (3%)
  local copies, waits for them, and re-layouts  0.69 us (1%)
    ppermute x6, waiting for transfers between devices, forward(): return lax.ppermute(block, 'en', [(stage, stage + 1)])  22.1 us
    pallas_call x14, Pallas kernels, vmem_call(): pl.pallas_call(kernel, out_shape=tuple(outs), in_specs=in_specs, out_spec...  14.8 us
    all_to_all x1, blocking collectives, gather_over(): return lax.all_to_all(copies, axis, 0, 0)  7.31 us
    ppermute x6, starting transfers between devices, forward(): return lax.ppermute(block, 'en', [(stage, stage + 1)])  5.66 us
    all_to_all x1, starting transfers between devices, body(): lax.all_to_all(jnp.tile(counts, kt_size), 'kt', 0, 0, tiled=True)  3.72 us
    all_to_all x1, waiting for transfers between devices, body(): lax.all_to_all(jnp.tile(counts, kt_size), 'kt', 0, 0, tiled=True)  2.8 us
  transfers between devices with their start and end apart: 7, of which 3 were waited for; matrix products, arithmetic and copies ran while one was open for 0% of the time, Pallas kernels for 17%

profile of v4, /device:TPU:24, one launch (start us, length us, event | category | flops | bytes accessed | tf_op | source)
XLA Modules:
  0.0 59.0 jit_solution(8101079026302155660)
XLA Ops:
  1.3 0.6 %tile.10 = s32[8,1,1]{2,1,0:T(1,128)} broadcast(s32[]{:T(128)} %bitcast.1), dimensions={} | broadcast | bytes 36 | tf_op jit(solution)/shard_map/tile | solution.py:639
  1.9 3.7 %all-to-all-start = ((s32[8,1,1]{2,1,0:T(1,128)}), s32[8,1,1]{2,1,0:T(1,128)S(1)}, u32[]{:S(2)}, u32[]{:S(2)}) async-start(s32[8,1,1]{2,1,0:T(1,128)} %tile.10), calls=%async_computation | async-start | bytes 8192 | tf_op jit(solution)/shard_map/all_to_all | solution.py:639
  5.6 0.0 copy-start.1
  5.6 0.0 copy-start.2
  5.6 0.0 copy-start.3
  5.6 0.0 copy-start.4
  5.6 0.0 copy-start.5
  5.6 1.7 %lead.1 = (bf16[1168,128]{1,0:T(8,128)(2,1)S(1)}, f32[4,384]{1,0:T(4,128)S(1)}, bf16[4,384,384]{2,1,0:T(8,128)(2,1)S(1)}, bf16[4,384,384]{2,1,0:T(8,128)(2,1)S(1)}) custom-call(f32[12]{0:T(128)} %constant.4.clone.constants_hbm.constants_ref, s32[2]{0:T(128)} %contact_ref.4, f32[4,384]{1,0:T(4,128)} %onsite.4, f32[4,384]{1,0:T(4,128)} %hopping.4, ...), custom_call_target="tpu_custom_call" | custom-call | flops 1358954496 | bytes 2097152 | tf_op jit(solution)/shard_map/lead/pallas_call | solution.py:554
  7.4 2.8 %all-to-all-done = s32[8,1,1]{2,1,0:T(1,128)S(1)} async-done(((s32[8,1,1]{2,1,0:T(1,128)}), s32[8,1,1]{2,1,0:T(1,128)S(1)}, u32[]{:S(2)}, u32[]{:S(2)}) %all-to-all-start) | async-done | bytes 64 | tf_op jit(solution)/shard_map/all_to_all | solution.py:639
  10.2 0.2 reduce.counts_ref
  10.4 0.0 copy-done.1
  10.4 0.0 copy-done.2
  10.4 0.0 copy-done.3
  10.4 0.0 copy-done.4
  10.4 0.0 copy-done.5
  10.5 0.7 %collective-permute-start = (bf16[1168,128]{1,0:T(8,128)(2,1)S(1)}, bf16[1168,128]{1,0:T(8,128)(2,1)S(1)}, u32[]{:S(2)}, u32[]{:S(2)}) collective-permute-start(bf16[1168,128]{1,0:T(8,128)(2,1)S(1)} %get-tuple-element.69), channel_id=1, source_target_pairs={{0,1},{4,5},{8,9},{12,13},{16,17},{20,21},{24,25},{28,29}} | collective-permute-start | bytes 897032 | tf_op jit(solution)/shard_map/ppermute | solution.py:626
  11.3 0.7 %collective-permute-start.3 = (bf16[1168,128]{1,0:T(8,128)(2,1)S(1)}, bf16[1168,128]{1,0:T(8,128)(2,1)S(1)}, u32[]{:S(2)}, u32[]{:S(2)}) collective-permute-start(bf16[1168,128]{1,0:T(8,128)(2,1)S(1)} %get-tuple-element.51), channel_id=1, source_target_pairs={{0,1},{4,5},{8,9},{12,13},{16,17},{20,21},{24,25},{28,29}} | collective-permute-start | bytes 897032 | tf_op jit(solution)/shard_map/ppermute | solution.py:626
  12.0 3.4 %prepare.1 = (bf16[4,384,384]{2,1,0:T(8,128)(2,1)S(1)}, bf16[4,384,384]{2,1,0:T(8,128)(2,1)S(1)}, f32[4,1536,128]{2,1,0:T(8,128)S(1)}, f32[9,8,384]{2,1,0:T(8,12...) custom-call(f32[12]{0:T(128)S(1)} %copy-done.5, ...), custom_call_target="tpu_custom_call" | custom-call | flops 452984832 | bytes 2097152 | tf_op jit(solution)/shard_map/prepare/pallas_call | solution.py:554
  15.4 0.2 operator_0.1
  15.6 0.0 collective-permute-done.arrived.refs_0_
  15.7 0.7 %collective-permute-start.1 = (bf16[1168,128]{1,0:T(8,128)(2,1)S(1)}, bf16[1168,128]{1,0:T(8,128)(2,1)S(1)}, u32[]{:S(2)}, u32[]{:S(2)}) collective-permute-start(bf16[1168,128]{1,0:T(8,128)(2,1)S(1)} %pass_1_0.1), channel_id=1, source_target_pairs={{1,2},{5,6},{9,10},{13,14},{17,18},{21,22},{25,26},{29,30}} | collective-permute-start | bytes 897032 | tf_op jit(solution)/shard_map/ppermute | solution.py:626
  16.4 0.0 collective-permute-done.3.arrived.refs_0_
  16.4 0.7 %collective-permute-start.4 = (bf16[1168,128]{1,0:T(8,128)(2,1)S(1)}, bf16[1168,128]{1,0:T(8,128)(2,1)S(1)}, u32[]{:S(2)}, u32[]{:S(2)}) collective-permute-start(bf16[1168,128]{1,0:T(8,128)(2,1)S(1)} %pass_1_1.1), channel_id=1, source_target_pairs={{1,2},{5,6},{9,10},{13,14},{17,18},{21,22},{25,26},{29,30}} | collective-permute-start | bytes 897032 | tf_op jit(solution)/shard_map/ppermute | solution.py:626
  17.1 0.0 collective-permute-done.1.arrived.refs_1_
  17.1 0.0 copy-start.6
  17.1 1.4 %collective-permute-start.2 = (bf16[1168,128]{1,0:T(8,128)(2,1)S(1)}, bf16[1168,128]{1,0:T(8,128)(2,1)S(1)}, u32[]{:S(2)}, u32[]{:S(2)}) collective-permute-start(bf16[1168,128]{1,0:T(8,128)(2,1)S(1)} %pass_2_0.1), channel_id=1, source_target_pairs={{2,3},{6,7},{10,11},{14,15},{18,19},{22,23},{26,27},{30,31}} | collective-permute-start | bytes 897032 | tf_op jit(solution)/shard_map/ppermute | solution.py:626
  18.6 0.0 collective-permute-done.4.arrived.refs_1_
  18.6 1.5 %collective-permute-start.5 = (bf16[1168,128]{1,0:T(8,128)(2,1)S(1)}, bf16[1168,128]{1,0:T(8,128)(2,1)S(1)}, u32[]{:S(2)}, u32[]{:S(2)}) collective-permute-start(bf16[1168,128]{1,0:T(8,128)(2,1)S(1)} %pass_2_1.1), channel_id=1, source_target_pairs={{2,3},{6,7},{10,11},{14,15},{18,19},{22,23},{26,27},{30,31}} | collective-permute-start | bytes 897032 | tf_op jit(solution)/shard_map/ppermute | solution.py:626
  20.1 0.0 copy-done.6
  20.1 0.2 split_inverse.1
  20.4 19.1 %collective-permute-done.2.refs_2_ = bf16[1168,128]{1,0:T(8,128)(2,1)S(1)} collective-permute-done((bf16[1168,128]{1,0:T(8,128)(2,1)S(1)}, bf16[1168,128]{1,0:T(8,128)(2,1)S(1)}, u32[]{:S(2)}, u32[]{:S(2)}) %collective-permute-start.2) | collective-permute-done | bytes 299040 | tf_op jit(solution)/shard_map/ppermute | solution.py:626
  39.5 4.1 %density_0.1.so_far = f32[4,384]{1,0:T(4,128)S(1)} custom-call(bf16[4,384,384]{2,1,0:T(8,128)(2,1)S(1)} %get-tuple-element.62.couple, bf16[4,384,384]{2,1,0:T(8,128)(2,1)S(1)} %get-tuple-element.63.turned, f32[4,1536,128]{2,1,0:T(8,128)S(1)} %get-tuple-element.64.scales, f32[9,8,384]{2,1,0:T(8,128)S(1)} %get-tuple-element.65.entry, ...), custom_call_target="tpu_custom_call", output_to_operand_aliasing={{}: (4, {})} | custom-call | flops 1811939328 | bytes 2097152 | tf_op jit(solution)/shard_map/density_0/pallas_call | solution.py:554
  43.6 0.0 copy-start
  43.6 3.0 %collective-permute-done.5.refs_2_ = bf16[1168,128]{1,0:T(8,128)(2,1)S(1)} collective-permute-done((bf16[1168,128]{1,0:T(8,128)(2,1)S(1)}, bf16[1168,128]{1,0:T(8,128)(2,1)S(1)}, u32[]{:S(2)}, u32[]{:S(2)}) %collective-permute-start.5) | collective-permute-done | bytes 299040 | tf_op jit(solution)/shard_map/ppermute | solution.py:626
  46.7 4.1 %density_1.1 = f32[4,384]{1,0:T(4,128)S(1)} custom-call(bf16[4,384,384]{2,1,0:T(8,128)(2,1)S(1)} %get-tuple-element.70.couple, bf16[4,384,384]{2,1,0:T(8,128)(2,1)S(1)} %get-tuple-element.71.turned, f32[4,1536,128]{2,1,0:T(8,128)S(1)} %get-tuple-element.72.scales, f32[9,8,384]{2,1,0:T(8,128)S(1)} %get-tuple-element.73.entry, ...), custom_call_target="tpu_custom_call", output_to_operand_aliasing={{}: (4, {})} | custom-call | flops 1811939328 | bytes 2097152 | tf_op jit(solution)/shard_map/density_1/pallas_call | solution.py:554
  50.8 7.3 %all_to_all.14.gathered = f32[8,4,384]{2,1,0:T(4,128)S(1)} all-to-all(f32[8,4,384]{2,1,0:T(4,128)S(1)} %broadcast_in_dim.10), channel_id=1, replica_groups=mesh['kt'=8,'en'=4] {'kt'}, dimensions={0} | all-to-all | bytes 98304 | tf_op jit(solution)/shard_map/all_to_all | solution.py:600
  58.1 0.0 copy-done
  58.1 0.9 %last.1 = (f32[4,384]{1,0:T(4,128)}, f32[4,384]{1,0:T(4,128)}) custom-call(f32[8,4,384]{2,1,0:T(4,128)S(1)} %all_to_all.14.gathered, f32[4,384]{1,0:T(4,128)S(1)} %copy-done, bf16[384,384]{1,0:T(8,128)(2,1)S(1)} %get-tuple-element.83.high, bf16[384,384]{1,0:T(8,128)(2,1)S(1)} %get-tuple-element.84.middle, bf16[384,384]{1,0:T(8,128)(2,1)S(1)} %get-tuple-element.85.low), custom_call_target="tpu_custom_call" | custom-call | flops 113246208 | bytes 2097152 | tf_op jit(solution)/shard_map/last/pallas_call | solution.py:554
  (9 shorter events, 0.2 us)
Async XLA Ops:
  1.9 8.3 %all-to-all-start = ((s32[8,1,1]{2,1,0:T(1,128)}), s32[8,1,1]{2,1,0:T(1,128)S(1)}, u32[]{:S(2)}, u32[]{:S(2)}) async-start(s32[8,1,1]{2,1,0:T(1,128)} %tile.10), calls=%async_computation | async-start | bytes 8192 | tf_op jit(solution)/shard_map/all_to_all | solution.py:639
  5.6 4.8 %copy-start.1 = (f32[4,384]{1,0:T(4,128)S(1)}, f32[4,384]{1,0:T(4,128)}, u32[]{:S(2)}) copy-start(f32[4,384]{1,0:T(4,128)} %onsite.4) | copy-start | bytes 18436
  5.6 4.8 %copy-start.2 = (f32[4,384]{1,0:T(4,128)S(1)}, f32[4,384]{1,0:T(4,128)}, u32[]{:S(2)}) copy-start(f32[4,384]{1,0:T(4,128)} %hopping.4) | copy-start | bytes 18436
  5.6 4.8 %copy-start.3 = (f32[4,384]{1,0:T(4,128)S(1)}, f32[4,384]{1,0:T(4,128)}, u32[]{:S(2)}) copy-start(f32[4,384]{1,0:T(4,128)} %potential.4) | copy-start | bytes 18436
  5.6 4.8 %copy-start.4 = (s32[2]{0:T(128)S(1)}, s32[2]{0:T(128)}, u32[]{:S(2)}) copy-start(s32[2]{0:T(128)} %contact_ref.4) | copy-start | bytes 28
  5.6 4.8 %copy-start.5 = (f32[12]{0:T(128)S(1)}, f32[12]{0:T(128)}, u32[]{:S(2)}) copy-start(f32[12]{0:T(128)} %constant.4.clone.constants_hbm.constants_ref) | copy-start | bytes 148
  10.5 5.1 %collective-permute-start = (bf16[1168,128]{1,0:T(8,128)(2,1)S(1)}, bf16[1168,128]{1,0:T(8,128)(2,1)S(1)}, u32[]{:S(2)}, u32[]{:S(2)}) collective-permute-start(bf16[1168,128]{1,0:T(8,128)(2,1)S(1)} %get-tuple-element.69), channel_id=1, source_target_pairs={{0,1},{4,5},{8,9},{12,13},{16,17},{20,21},{24,25},{28,29}} | collective-permute-start | bytes 897032 | tf_op jit(solution)/shard_map/ppermute | solution.py:626
  11.3 5.1 %collective-permute-start.3 = (bf16[1168,128]{1,0:T(8,128)(2,1)S(1)}, bf16[1168,128]{1,0:T(8,128)(2,1)S(1)}, u32[]{:S(2)}, u32[]{:S(2)}) collective-permute-start(bf16[1168,128]{1,0:T(8,128)(2,1)S(1)} %get-tuple-element.51), channel_id=1, source_target_pairs={{0,1},{4,5},{8,9},{12,13},{16,17},{20,21},{24,25},{28,29}} | collective-permute-start | bytes 897032 | tf_op jit(solution)/shard_map/ppermute | solution.py:626
  15.7 1.4 %collective-permute-start.1 = (bf16[1168,128]{1,0:T(8,128)(2,1)S(1)}, bf16[1168,128]{1,0:T(8,128)(2,1)S(1)}, u32[]{:S(2)}, u32[]{:S(2)}) collective-permute-start(bf16[1168,128]{1,0:T(8,128)(2,1)S(1)} %pass_1_0.1), channel_id=1, source_target_pairs={{1,2},{5,6},{9,10},{13,14},{17,18},{21,22},{25,26},{29,30}} | collective-permute-start | bytes 897032 | tf_op jit(solution)/shard_map/ppermute | solution.py:626
  16.4 2.2 %collective-permute-start.4 = (bf16[1168,128]{1,0:T(8,128)(2,1)S(1)}, bf16[1168,128]{1,0:T(8,128)(2,1)S(1)}, u32[]{:S(2)}, u32[]{:S(2)}) collective-permute-start(bf16[1168,128]{1,0:T(8,128)(2,1)S(1)} %pass_1_1.1), channel_id=1, source_target_pairs={{1,2},{5,6},{9,10},{13,14},{17,18},{21,22},{25,26},{29,30}} | collective-permute-start | bytes 897032 | tf_op jit(solution)/shard_map/ppermute | solution.py:626
  17.1 3.0 %copy-start.6 = (f32[384,384]{1,0:T(8,128)S(1)}, f32[384,384]{1,0:T(8,128)}, u32[]{:S(2)}) copy-start(f32[384,384]{1,0:T(8,128)} %inverse) | copy-start | bytes 1769476
  17.1 22.4 %collective-permute-start.2 = (bf16[1168,128]{1,0:T(8,128)(2,1)S(1)}, bf16[1168,128]{1,0:T(8,128)(2,1)S(1)}, u32[]{:S(2)}, u32[]{:S(2)}) collective-permute-start(bf16[1168,128]{1,0:T(8,128)(2,1)S(1)} %pass_2_0.1), channel_id=1, source_target_pairs={{2,3},{6,7},{10,11},{14,15},{18,19},{22,23},{26,27},{30,31}} | collective-permute-start | bytes 897032 | tf_op jit(solution)/shard_map/ppermute | solution.py:626
  18.6 28.0 %collective-permute-start.5 = (bf16[1168,128]{1,0:T(8,128)(2,1)S(1)}, bf16[1168,128]{1,0:T(8,128)(2,1)S(1)}, u32[]{:S(2)}, u32[]{:S(2)}) collective-permute-start(bf16[1168,128]{1,0:T(8,128)(2,1)S(1)} %pass_2_1.1), channel_id=1, source_target_pairs={{2,3},{6,7},{10,11},{14,15},{18,19},{22,23},{26,27},{30,31}} | collective-permute-start | bytes 897032 | tf_op jit(solution)/shard_map/ppermute | solution.py:626
  43.6 14.5 %copy-start = (f32[4,384]{1,0:T(4,128)S(1)}, f32[4,384]{1,0:T(4,128)}, u32[]{:S(2)}) copy-start(f32[4,384]{1,0:T(4,128)} %doping.1) | copy-start | bytes 18436

commit v5 on v4

--- a/solution.py
+++ b/solution.py
@@ -397,7 +397,7 @@
         first_segment(coupled_of, inv_real, inv_imag, scales, weight, g, left, sent, density)
 
 
-def prepare(cosine, weight, inv_real, inv_imag, base, wave, couple, turned, scales, entry):
+def prepare(cosine, weight, inv_real, inv_imag, base, wave, couple, scales, entry):
     slabs, orbitals = inv_real.shape
     parts = orbitals // LANE
     form_scales(range(slabs), inv_real, inv_imag, scales, parts)
@@ -407,11 +407,7 @@
     entry[2 * slabs] = jnp.full(entry.shape[1:], weight, F32)
 
     def one(s, carry):
-        coupled = coupling_of(base[s], wave[s], cosine)
-        couple[s] = coupled
-        for r in range(parts):
-            for c in range(parts):
-                turned[s, span(c), span(r)] = coupled[span(r), span(c)].T
+        couple[s] = coupling_of(base[s], wave[s], cosine)
         return carry
 
     lax.fori_loop(0, slabs, one, 0)
@@ -420,8 +416,8 @@
 def prepare_kernel(
     impulse_count,
     constants_ref, contact_ref, counts_ref, onsite, hopping, potential, base, wave,
-    couple_0, turned_0, scales_0, entry_0,
-    couple_1, turned_1, scales_1, entry_1,
+    couple_0, scales_0, entry_0,
+    couple_1, scales_1, entry_1,
     constants, contact, counts, scalar_sem,
 ):
     position = lax.axis_index("en")
@@ -432,8 +428,8 @@
             (constants_ref, contact_ref, counts_ref), (constants, contact, counts), scalar_sem
         )
         for slot, made in (
-            (0, (couple_0, turned_0, scales_0, entry_0)),
-            (1, (couple_1, turned_1, scales_1, entry_1)),
+            (0, (couple_0, scales_0, entry_0)),
+            (1, (couple_1, scales_1, entry_1)),
         ):
             momentum, level = item_of(counts, slot)
             cosine, energy, weight = entry_amounts(constants, impulse_count, momentum, level)
@@ -443,87 +439,60 @@
             prepare(cosine, weight, inv_real, inv_imag, base, wave, *made)
 
 
-def density_kernel(couple, turned, scales, entry, so_far, *refs):
-    arrived, (density, g, left, noted) = refs[:-4], refs[-4:]
-    slabs, orbitals = so_far.shape
-    parts = orbitals // LANE
-    position = lax.axis_index("en")
-    density[...] = so_far[...]
-
-    def put(half, r, c, block):
-        column = place(parts, half, c)
-        g[span(r), span(column)] = block
-
-    for stage, block in enumerate(arrived, 1):
-
-        @pl.when(position == stage)
-        def _():
-            unpack_blocks(block, put, parts)
-
-    @pl.when(position > 0)
-    def _():
-        def slab(s, final):
-            times_carried(couple[s], g, left, parts)
-
-            def times_turned(rows):
-                return jnp.dot(rows, turned[s], preferred_element_type=F32)
-
-            def note(r, middle):
-                noted[s, 0:1, span(r)] = middle
-
-            finish_slab(
-                s, times_turned, left, None if final else g, None,
-                entry[s, 0:1, :], entry[slabs + s, 0:1, :], scales, note, parts,
-            )
-
-        def inner(s, carry):
-            slab(s, False)
-            return carry
-
-        lax.fori_loop(0, slabs - 1, inner, 0)
-        slab(slabs - 1, True)
-        for s in range(slabs):
-            density[s : s + 1, :] += -entry[2 * slabs, 0:1, :] * noted[s, 0:1, :]
-
-
-def operator_kernel(couple, turned, scales, entry, local, carrier, cross, g, left):
+def rows_of_entry(entry, slabs):
+    inv_real = jnp.concatenate([entry[s, 0:1, :] for s in range(slabs)], axis=0)
+    inv_imag = jnp.concatenate([entry[slabs + s, 0:1, :] for s in range(slabs)], axis=0)
+    return inv_real, inv_imag, entry[2 * slabs, 0:1, 0:1]
+
+
+def carrier_kernel(couple, entry, carriers, cross):
     slabs, orbitals, _ = couple.shape
     parts = orbitals // LANE
-    position = lax.axis_index("en")
-
-    @pl.when(jnp.logical_and(position > 0, position < lax.axis_size("en") - 1))
+
+    @pl.when(lax.axis_index("en") > 0)
     def _():
-        inv_real = jnp.concatenate([entry[s, 0:1, :] for s in range(slabs)], axis=0)
-        inv_imag = jnp.concatenate([entry[slabs + s, 0:1, :] for s in range(slabs)], axis=0)
-        first_segment(
-            lambda s: couple[s], inv_real, inv_imag, scales, None, g, left, None, None, local
-        )
+        inv_real, inv_imag, _ = rows_of_entry(entry, slabs)
         down = jnp.concatenate([inv_real, inv_imag], axis=0).T
         for s in range(slabs):
+            here = slice(s * orbitals, (s + 1) * orbitals)
             real_col = down[:, s : s + 1]
             imag_col = down[:, slabs + s : slabs + s + 1]
             if s == 0:
                 wide = couple[0].astype(F32)
                 real, imag = real_col * wide, imag_col * wide
             else:
-                product = jnp.dot(couple[s], carrier[...], preferred_element_type=F32)
+                ahead = slice((s - 1) * orbitals, s * orbitals)
+                product = jnp.dot(couple[s], carriers[ahead, :], preferred_element_type=F32)
                 from_real, from_imag = product[:, :orbitals], product[:, orbitals:]
                 real = real_col * from_real - imag_col * from_imag
                 imag = real_col * from_imag + imag_col * from_real
-            carrier[:, :orbitals] = real.astype(BF16)
-            carrier[:, orbitals:] = imag.astype(BF16)
+            carriers[here, :orbitals] = real.astype(BF16)
+            carriers[here, orbitals:] = imag.astype(BF16)
+        top = (slabs - 1) * parts
         for r in range(parts):
             for c in range(parts):
-                real = carrier[span(r), span(c)].T
-                imag = carrier[span(r), span(parts + c)].T
+                real = carriers[span(top + r), span(c)].T
+                imag = carriers[span(top + r), span(parts + c)].T
                 cross[span(c), span(r)] = real
                 cross[span(parts + c), span(parts + r)] = real
                 cross[span(c), span(parts + r)] = imag
                 cross[span(parts + c), span(r)] = -imag
 
 
-def pass_kernel(stage, local, carrier, cross, arrived, sent, wide, half_way):
-    orbitals = carrier.shape[0]
+def local_kernel(couple, scales, entry, local, densities, g, left):
+    slabs = couple.shape[0]
+
+    @pl.when(lax.axis_index("en") > 0)
+    def _():
+        inv_real, inv_imag, weight = rows_of_entry(entry, slabs)
+        densities[...] = jnp.zeros_like(densities)
+        first_segment(
+            lambda s: couple[s], inv_real, inv_imag, scales, weight, g, left, None, densities, local
+        )
+
+
+def pass_kernel(stage, local, carriers, cross, arrived, sent, wide, half_way):
+    orbitals = carriers.shape[1] // 2
     parts = orbitals // LANE
 
     @pl.when(lax.axis_index("en") == stage)
@@ -537,7 +506,9 @@
                 wide[span(parts + r), span(c)] = -block
 
         unpack_blocks(arrived, put, parts)
-        half_way[...] = jnp.dot(carrier[...], wide[...], preferred_element_type=F32).astype(BF16)
+        half_way[...] = jnp.dot(
+            carriers[carriers.shape[0] - orbitals :, :], wide[...], preferred_element_type=F32
+        ).astype(BF16)
         out = jnp.dot(half_way[...], cross[...], preferred_element_type=F32)
         middles = []
         for k, (r, c) in enumerate(blocks_on_or_below(parts)):
@@ -549,7 +520,52 @@
         pack_middles(sent, middles, parts)
 
 
-def vmem_call(kernel, outs, operands, in_specs, scratch, name, flops, **more):
+def density_kernel(carriers, entry, local_densities, so_far, *refs):
+    arrived, (density, wide, total) = refs[:-3], refs[-3:]
+    slabs, orbitals = so_far.shape
+    parts = orbitals // LANE
+    position = lax.axis_index("en")
+    density[...] = so_far[...]
+
+    def put(half, r, c, block):
+        if half == 0:
+            wide[span(r), span(2 * c)] = block
+            wide[span(parts + r), span(2 * c + 1)] = block
+        else:
+            wide[span(r), span(2 * c + 1)] = block
+            wide[span(parts + r), span(2 * c)] = -block
+
+    for stage, block in enumerate(arrived, 1):
+
+        @pl.when(position == stage)
+        def _():
+            unpack_blocks(block, put, parts)
+
+    @pl.when(position > 0)
+    def _():
+        for c in range(parts):
+            product = jnp.dot(
+                carriers[...],
+                wide[:, 2 * c * LANE : 2 * (c + 1) * LANE],
+                preferred_element_type=F32,
+            )
+            term = product[:, :LANE] * carriers[:, span(parts + c)].astype(F32) + product[
+                :, LANE:
+            ] * carriers[:, span(c)].astype(F32)
+            if c == 0:
+                total[...] = term
+            else:
+                total[...] += term
+        weight = entry[2 * slabs, 0:1, :LANE]
+        for s in range(slabs):
+            for r in range(parts):
+                row = jnp.sum(total[span(s * parts + r), :].T, axis=0, keepdims=True)
+                density[s : s + 1, span(r)] += (
+                    local_densities[s : s + 1, span(r)] - weight * row
+                )
+
+
+def vmem_call(kernel, outs, operands, in_specs, scratch, name, flops, traffic=2**21, **more):
     vmem = pl.BlockSpec(memory_space=pltpu.VMEM)
     return pl.pallas_call(
         kernel,
@@ -558,7 +574,7 @@
         out_specs=(vmem,) * len(outs),
         scratch_shapes=scratch,
         compiler_params=pltpu.CompilerParams(vmem_limit_bytes=16 * 2**20),
-        cost_estimate=pl.CostEstimate(flops=flops, bytes_accessed=2**21, transcendentals=0),
+        cost_estimate=pl.CostEstimate(flops=flops, bytes_accessed=traffic, transcendentals=0),
         name=name,
         **more,
     )(*operands)
@@ -689,38 +705,52 @@
     small, _ = lax.optimization_barrier((small, block))
     made = vmem_call(
         functools.partial(prepare_kernel, impulse_count),
-        (couple_shape, couple_shape, scales_shape, entry_shape) * 2,
+        (couple_shape, scales_shape, entry_shape) * 2,
         (*small, *loaded),
         [anywhere] * 3 + [vmem] * 5,
         scalar_scratch,
         "prepare",
-        flops,
+        flops // 16,
+        2**16,
     )
-    made = [made[:4], made[4:]]
-
-    def operator_of(slot, made):
+    made = [made[:3], made[3:]]
+
+    carriers_shape = jax.ShapeDtypeStruct((slabs * orbitals, 2 * orbitals), BF16)
+    double_shape = jax.ShapeDtypeStruct((2 * orbitals, 2 * orbitals), BF16)
+
+    def carriers_of(slot):
+        couple, _, entry = made[slot]
         return vmem_call(
-            operator_kernel,
-            (
-                jax.ShapeDtypeStruct((scale_rows(parts), LANE), F32),
-                jax.ShapeDtypeStruct((orbitals, 2 * orbitals), BF16),
-                jax.ShapeDtypeStruct((2 * orbitals, 2 * orbitals), BF16),
-            ),
-            made,
-            [vmem] * 4,
+            carrier_kernel,
+            (carriers_shape, double_shape),
+            (couple, entry),
+            [vmem] * 2,
+            [],
+            f"carriers_{slot}",
+            flops // 16,
+            2**16,
+        )
+
+    def local_of(slot):
+        return vmem_call(
+            local_kernel,
+            (jax.ShapeDtypeStruct((scale_rows(parts), LANE), F32), density_shape),
+            made[slot],
+            [vmem] * 3,
             work,
-            f"operator_{slot}",
-            6 * flops,
-        )
-
-    def pass_on(stage, slot, operator, block):
+            f"local_{slot}",
+            flops // 16,
+            2**16,
+        )
+
+    def pass_on(stage, slot, block):
         return vmem_call(
             functools.partial(pass_kernel, stage),
             (block_shape,),
-            (*operator, block),
+            (local[slot][0], *carried[slot], block),
             [vmem] * 4,
             [
-                pltpu.VMEM((2 * orbitals, 2 * orbitals), BF16),
+                pltpu.VMEM(double_shape.shape, BF16),
                 pltpu.VMEM((orbitals, 2 * orbitals), BF16),
             ],
             f"pass_{stage}_{slot}",
@@ -731,23 +761,28 @@
         return vmem_call(
             density_kernel,
             (density_shape,),
-            (*made[slot], density, *came),
-            [vmem] * (5 + len(came)),
-            work + [pltpu.VMEM((slabs, 8, orbitals), F32)],
+            (carried[slot][0], made[slot][2], local[slot][1], density, *came),
+            [vmem] * (4 + len(came)),
+            [
+                pltpu.VMEM(double_shape.shape, BF16),
+                pltpu.VMEM((slabs * orbitals, LANE), F32),
+            ],
             f"density_{slot}",
             4 * flops,
-            input_output_aliases={4: 0},
+            input_output_aliases={3: 0},
         )[0]
 
-    operators = []
     came = [[arrived[0]], [arrived[1]]]
+    carried, local = [carriers_of(0)], [local_of(0)]
+    made[1], _ = lax.optimization_barrier((made[1], local[0][1]))
+    carried.append(carriers_of(1))
+    came[0][0], _ = lax.optimization_barrier((came[0][0], carried[1]))
     for stage in range(1, en_size - 1):
         for slot in range(2):
-            if stage == 1:
-                if slot == 1:
-                    made[1], _ = lax.optimization_barrier((made[1], block))
-                operators.append(operator_of(slot, made[slot]))
-            block = pass_on(stage, slot, operators[slot], came[slot][-1])
+            if stage == 1 and slot == 1:
+                made[1], _ = lax.optimization_barrier((made[1], block))
+                local.append(local_of(1))
+            block = pass_on(stage, slot, came[slot][-1])
             came[slot].append(forward(block, stage))
     for slot in range(2):
         density = densities(slot, density, came[slot])

time: 59.3 us -> 60.2 us (1.015)
  Pallas kernels: 14.8 us -> 20.4 us
  waiting for transfers between devices: 24.9 us -> 20.5 us
    pallas_call x14 -> x16, Pallas kernels: 14.8 us -> 20.4 us  [vmem_call(): pl.pallas_call(kernel, out_shape=tuple(outs), in_specs=in_specs, out_spec...]
    ppermute x6, waiting for transfers between devices: 22.1 us -> 17.7 us  [forward(): return lax.ppermute(block, 'en', [(stage, stage + 1)])]
  transfers between devices with their start and end apart: 7 -> 7, of which waited for: 3 -> 3; matrix products, arithmetic and copies ran while one was open for 0% -> 0% of each run, Pallas kernels for 17% -> 29%
where the time goes in v5:
time: 60.2 us; the launch traced here: 59.9 us
  waiting for transfers between devices  20.5 us (34%)
  Pallas kernels  20.4 us (34%)
  starting transfers between devices  9.16 us (15%)
  blocking collectives  7.31 us (12%)
  between operations  1.56 us (3%)
  local copies, waits for them, and re-layouts  0.69 us (1%)
    pallas_call x16, Pallas kernels, vmem_call(): pl.pallas_call(kernel, out_shape=tuple(outs), in_specs=in_specs, out_spec...  20.4 us
    ppermute x6, waiting for transfers between devices, forward(): return lax.ppermute(block, 'en', [(stage, stage + 1)])  17.7 us
    all_to_all x1, blocking collectives, gather_over(): return lax.all_to_all(copies, axis, 0, 0)  7.31 us
    ppermute x6, starting transfers between devices, forward(): return lax.ppermute(block, 'en', [(stage, stage + 1)])  5.44 us
    all_to_all x1, starting transfers between devices, body(): lax.all_to_all(jnp.tile(counts, kt_size), 'kt', 0, 0, tiled=True)  3.72 us
    all_to_all x1, waiting for transfers between devices, body(): lax.all_to_all(jnp.tile(counts, kt_size), 'kt', 0, 0, tiled=True)  2.8 us
  transfers between devices with their start and end apart: 7, of which 3 were waited for; matrix products, arithmetic and copies ran while one was open for 0% of the time, Pallas kernels for 29%

profile of v5, /device:TPU:24, one launch (start us, length us, event | category | flops | bytes accessed | tf_op | source)
XLA Modules:
  0.0 59.9 jit_solution(17960407612653882817)
XLA Ops:
  1.3 0.6 tile.10
  1.9 3.7 %all-to-all-start = ((s32[8,1,1]{2,1,0:T(1,128)}), s32[8,1,1]{2,1,0:T(1,128)S(1)}, u32[]{:S(2)}, u32[]{:S(2)}) async-start(s32[8,1,1]{2,1,0:T(1,128)} %tile.10), calls=%async_computation | async-start | bytes 8192 | tf_op jit(solution)/shard_map/all_to_all | solution.py:655
  5.6 0.0 copy-start.1
  5.6 0.0 copy-start.2
  5.6 0.0 copy-start.3
  5.6 0.0 copy-start.4
  5.6 0.0 copy-start.5
  5.6 1.7 %lead.1 = (bf16[1168,128]{1,0:T(8,128)(2,1)S(1)}, f32[4,384]{1,0:T(4,128)S(1)}, bf16[4,384,384]{2,1,0:T(8,128)(2,1)S(1)}, bf16[4,384,384]{2,1,0:T(8,128)(2,1)S(1)}) custom-call(f32[12]{0:T(128)} %constant.4.clone.constants_hbm.constants_ref, s32[2]{0:T(128)} %contact_ref.4, f32[4,384]{1,0:T(4,128)} %onsite.4, f32[4,384]{1,0:T(4,128)} %hopping.4, ...), custom_call_target="tpu_custom_call" | custom-call | flops 1358954496 | bytes 2097152 | tf_op jit(solution)/shard_map/lead/pallas_call | solution.py:570
  7.4 2.8 %all-to-all-done = s32[8,1,1]{2,1,0:T(1,128)S(1)} async-done(((s32[8,1,1]{2,1,0:T(1,128)}), s32[8,1,1]{2,1,0:T(1,128)S(1)}, u32[]{:S(2)}, u32[]{:S(2)}) %all-to-all-start) | async-done | bytes 64 | tf_op jit(solution)/shard_map/all_to_all | solution.py:655
  10.2 0.2 reduce.counts_ref
  10.4 0.0 copy-done.1
  10.4 0.0 copy-done.2
  10.4 0.0 copy-done.3
  10.4 0.0 copy-done.4
  10.4 0.0 copy-done.5
  10.5 0.7 %collective-permute-start = (bf16[1168,128]{1,0:T(8,128)(2,1)S(1)}, bf16[1168,128]{1,0:T(8,128)(2,1)S(1)}, u32[]{:S(2)}, u32[]{:S(2)}) collective-permute-start(bf16[1168,128]{1,0:T(8,128)(2,1)S(1)} %get-tuple-element.75), channel_id=1, source_target_pairs={{0,1},{4,5},{8,9},{12,13},{16,17},{20,21},{24,25},{28,29}} | collective-permute-start | bytes 897032 | tf_op jit(solution)/shard_map/ppermute | solution.py:642
  11.3 0.7 %collective-permute-start.3 = (bf16[1168,128]{1,0:T(8,128)(2,1)S(1)}, bf16[1168,128]{1,0:T(8,128)(2,1)S(1)}, u32[]{:S(2)}, u32[]{:S(2)}) collective-permute-start(bf16[1168,128]{1,0:T(8,128)(2,1)S(1)} %get-tuple-element.54), channel_id=1, source_target_pairs={{0,1},{4,5},{8,9},{12,13},{16,17},{20,21},{24,25},{28,29}} | collective-permute-start | bytes 897032 | tf_op jit(solution)/shard_map/ppermute | solution.py:642
  12.0 2.9 %prepare.1 = (bf16[4,384,384]{2,1,0:T(8,128)(2,1)S(1)}, f32[4,1536,128]{2,1,0:T(8,128)S(1)}, f32[9,8,384]{2,1,0:T(8,128)S(1)}, bf16[4,384,384]{2,1,0:T(8,128)(2,...) custom-call(f32[12]{0:T(128)S(1)} %copy-done.5, s32[2]{0:T(128)S(1)} %copy-done.4, s32[8]{0:T(128)S(1)} %reduce.counts_ref, ...), custom_call_target="tpu_custom_call" | custom-call | flops 28311552 | bytes 65536 | tf_op jit(solution)/shard_map/prepare/pallas_call | solution.py:570
  14.9 2.8 %local_0.1 = (f32[1536,128]{1,0:T(8,128)S(1)}, f32[4,384]{1,0:T(4,128)S(1)}) custom-call(bf16[4,384,384]{2,1,0:T(8,128)(2,1)S(1)} %get-tuple-element.64.couple, f32[4,1536,128]{2,1,0:T(8,128)S(1)} %get-tuple-element.65.scales, f32[9,8,384]{2,1,0:T(8,128)S(1)} %get-tuple-element.66.entry), custom_call_target="tpu_custom_call" | custom-call | flops 28311552 | bytes 65536 | tf_op jit(solution)/shard_map/local_0/pallas_call | solution.py:570
  17.7 2.1 %carriers_0.1 = (bf16[1536,768]{1,0:T(8,128)(2,1)S(1)}, bf16[768,768]{1,0:T(8,128)(2,1)S(1)}) custom-call(bf16[4,384,384]{2,1,0:T(8,128)(2,1)S(1)} %get-tuple-element.64.couple, f32[9,8,384]{2,1,0:T(8,128)S(1)} %get-tuple-element.66.entry), custom_call_target="tpu_custom_call" | custom-call | flops 28311552 | bytes 65536 | tf_op jit(solution)/shard_map/carriers_0/pallas_call | solution.py:570
  19.7 2.1 %carriers_1.1 = (bf16[1536,768]{1,0:T(8,128)(2,1)S(1)}, bf16[768,768]{1,0:T(8,128)(2,1)S(1)}) custom-call(bf16[4,384,384]{2,1,0:T(8,128)(2,1)S(1)} %get-tuple-element.79.couple, f32[9,8,384]{2,1,0:T(8,128)S(1)} %get-tuple-element.78.entry), custom_call_target="tpu_custom_call" | custom-call | flops 28311552 | bytes 65536 | tf_op jit(solution)/shard_map/carriers_1/pallas_call | solution.py:570
  21.8 0.0 collective-permute-done.arrived.refs_0_
  21.8 0.7 %collective-permute-start.1 = (bf16[1168,128]{1,0:T(8,128)(2,1)S(1)}, bf16[1168,128]{1,0:T(8,128)(2,1)S(1)}, u32[]{:S(2)}, u32[]{:S(2)}) collective-permute-start(bf16[1168,128]{1,0:T(8,128)(2,1)S(1)} %pass_1_0.1), channel_id=1, source_target_pairs={{1,2},{5,6},{9,10},{13,14},{17,18},{21,22},{25,26},{29,30}} | collective-permute-start | bytes 897032 | tf_op jit(solution)/shard_map/ppermute | solution.py:642
  22.5 2.6 %local_1.1 = (f32[1536,128]{1,0:T(8,128)S(1)}, f32[4,384]{1,0:T(4,128)S(1)}) custom-call(bf16[4,384,384]{2,1,0:T(8,128)(2,1)S(1)} %get-tuple-element.79.couple, f32[4,1536,128]{2,1,0:T(8,128)S(1)} %get-tuple-element.80.scales, f32[9,8,384]{2,1,0:T(8,128)S(1)} %get-tuple-element.78.entry), custom_call_target="tpu_custom_call" | custom-call | flops 28311552 | bytes 65536 | tf_op jit(solution)/shard_map/local_1/pallas_call | solution.py:570
  25.2 0.0 collective-permute-done.3.arrived.refs_0_
  25.2 0.7 %collective-permute-start.4 = (bf16[1168,128]{1,0:T(8,128)(2,1)S(1)}, bf16[1168,128]{1,0:T(8,128)(2,1)S(1)}, u32[]{:S(2)}, u32[]{:S(2)}) collective-permute-start(bf16[1168,128]{1,0:T(8,128)(2,1)S(1)} %pass_1_1.1), channel_id=1, source_target_pairs={{1,2},{5,6},{9,10},{13,14},{17,18},{21,22},{25,26},{29,30}} | collective-permute-start | bytes 897032 | tf_op jit(solution)/shard_map/ppermute | solution.py:642
  25.9 0.0 collective-permute-done.1.arrived.refs_1_
  25.9 0.0 copy-start.6
  25.9 1.4 %collective-permute-start.2 = (bf16[1168,128]{1,0:T(8,128)(2,1)S(1)}, bf16[1168,128]{1,0:T(8,128)(2,1)S(1)}, u32[]{:S(2)}, u32[]{:S(2)}) collective-permute-start(bf16[1168,128]{1,0:T(8,128)(2,1)S(1)} %pass_2_0.1), channel_id=1, source_target_pairs={{2,3},{6,7},{10,11},{14,15},{18,19},{22,23},{26,27},{30,31}} | collective-permute-start | bytes 897032 | tf_op jit(solution)/shard_map/ppermute | solution.py:642
  27.4 0.0 collective-permute-done.4.arrived.refs_1_
  27.4 0.2 pass_2_1.1
  27.6 1.3 %collective-permute-start.5 = (bf16[1168,128]{1,0:T(8,128)(2,1)S(1)}, bf16[1168,128]{1,0:T(8,128)(2,1)S(1)}, u32[]{:S(2)}, u32[]{:S(2)}) collective-permute-start(bf16[1168,128]{1,0:T(8,128)(2,1)S(1)} %pass_2_1.1), channel_id=1, source_target_pairs={{2,3},{6,7},{10,11},{14,15},{18,19},{22,23},{26,27},{30,31}} | collective-permute-start | bytes 897032 | tf_op jit(solution)/shard_map/ppermute | solution.py:642
  28.9 0.0 copy-done.6
  28.9 0.2 split_inverse.1
  29.2 13.8 %collective-permute-done.2.refs_2_ = bf16[1168,128]{1,0:T(8,128)(2,1)S(1)} collective-permute-done((bf16[1168,128]{1,0:T(8,128)(2,1)S(1)}, bf16[1168,128]{1,0:T(8,128)(2,1)S(1)}, u32[]{:S(2)}, u32[]{:S(2)}) %collective-permute-start.2) | collective-permute-done | bytes 299040 | tf_op jit(solution)/shard_map/ppermute | solution.py:642
  43.0 2.4 %density_0.1.so_far = f32[4,384]{1,0:T(4,128)S(1)} custom-call(bf16[1536,768]{1,0:T(8,128)(2,1)S(1)} %get-tuple-element.73.carriers, f32[9,8,384]{2,1,0:T(8,128)S(1)} %get-tuple-element.66.entry, f32[4,384]{1,0:T(4,128)S(1)} %get-tuple-element.67.local_densities, f32[4,384]{1,0:T(4,128)S(1)} %get-tuple-element.82.so_far, ...), custom_call_target="tpu_custom_call", output_to_operand_aliasing={{}: (3, {})} | custom-call | flops 1811939328 | bytes 2097152 | tf_op jit(solution)/shard_map/density_0/pallas_call | solution.py:570
  45.4 3.9 %collective-permute-done.5.refs_2_ = bf16[1168,128]{1,0:T(8,128)(2,1)S(1)} collective-permute-done((bf16[1168,128]{1,0:T(8,128)(2,1)S(1)}, bf16[1168,128]{1,0:T(8,128)(2,1)S(1)}, u32[]{:S(2)}, u32[]{:S(2)}) %collective-permute-start.5) | collective-permute-done | bytes 299040 | tf_op jit(solution)/shard_map/ppermute | solution.py:642
  49.3 0.0 copy-start
  49.3 2.4 %density_1.1 = f32[4,384]{1,0:T(4,128)S(1)} custom-call(bf16[1536,768]{1,0:T(8,128)(2,1)S(1)} %get-tuple-element.70.carriers, f32[9,8,384]{2,1,0:T(8,128)S(1)} %get-tuple-element.78.entry, f32[4,384]{1,0:T(4,128)S(1)} %get-tuple-element.81.local_densities, f32[4,384]{1,0:T(4,128)S(1)} %density_0.1.so_far, ...), custom_call_target="tpu_custom_call", output_to_operand_aliasing={{}: (3, {})} | custom-call | flops 1811939328 | bytes 2097152 | tf_op jit(solution)/shard_map/density_1/pallas_call | solution.py:570
  51.7 7.3 %all_to_all.14.gathered = f32[8,4,384]{2,1,0:T(4,128)S(1)} all-to-all(f32[8,4,384]{2,1,0:T(4,128)S(1)} %broadcast_in_dim.10), channel_id=1, replica_groups=mesh['kt'=8,'en'=4] {'kt'}, dimensions={0} | all-to-all | bytes 98304 | tf_op jit(solution)/shard_map/all_to_all | solution.py:616
  59.0 0.0 copy-done
  59.0 0.9 %last.1 = (f32[4,384]{1,0:T(4,128)}, f32[4,384]{1,0:T(4,128)}) custom-call(f32[8,4,384]{2,1,0:T(4,128)S(1)} %all_to_all.14.gathered, f32[4,384]{1,0:T(4,128)S(1)} %copy-done, bf16[384,384]{1,0:T(8,128)(2,1)S(1)} %get-tuple-element.89.high, bf16[384,384]{1,0:T(8,128)(2,1)S(1)} %get-tuple-element.90.middle, bf16[384,384]{1,0:T(8,128)(2,1)S(1)} %get-tuple-element.91.low), custom_call_target="tpu_custom_call" | custom-call | flops 113246208 | bytes 2097152 | tf_op jit(solution)/shard_map/last/pallas_call | solution.py:570
  (7 shorter events, 0.2 us)
Async XLA Ops:
  1.9 8.3 %all-to-all-start = ((s32[8,1,1]{2,1,0:T(1,128)}), s32[8,1,1]{2,1,0:T(1,128)S(1)}, u32[]{:S(2)}, u32[]{:S(2)}) async-start(s32[8,1,1]{2,1,0:T(1,128)} %tile.10), calls=%async_computation | async-start | bytes 8192 | tf_op jit(solution)/shard_map/all_to_all | solution.py:655
  5.6 4.8 %copy-start.1 = (f32[4,384]{1,0:T(4,128)S(1)}, f32[4,384]{1,0:T(4,128)}, u32[]{:S(2)}) copy-start(f32[4,384]{1,0:T(4,128)} %onsite.4) | copy-start | bytes 18436
  5.6 4.8 %copy-start.2 = (f32[4,384]{1,0:T(4,128)S(1)}, f32[4,384]{1,0:T(4,128)}, u32[]{:S(2)}) copy-start(f32[4,384]{1,0:T(4,128)} %hopping.4) | copy-start | bytes 18436
  5.6 4.8 %copy-start.3 = (f32[4,384]{1,0:T(4,128)S(1)}, f32[4,384]{1,0:T(4,128)}, u32[]{:S(2)}) copy-start(f32[4,384]{1,0:T(4,128)} %potential.4) | copy-start | bytes 18436
  5.6 4.8 %copy-start.4 = (s32[2]{0:T(128)S(1)}, s32[2]{0:T(128)}, u32[]{:S(2)}) copy-start(s32[2]{0:T(128)} %contact_ref.4) | copy-start | bytes 28
  5.6 4.8 %copy-start.5 = (f32[12]{0:T(128)S(1)}, f32[12]{0:T(128)}, u32[]{:S(2)}) copy-start(f32[12]{0:T(128)} %constant.4.clone.constants_hbm.constants_ref) | copy-start | bytes 148
  10.5 11.3 %collective-permute-start = (bf16[1168,128]{1,0:T(8,128)(2,1)S(1)}, bf16[1168,128]{1,0:T(8,128)(2,1)S(1)}, u32[]{:S(2)}, u32[]{:S(2)}) collective-permute-start(bf16[1168,128]{1,0:T(8,128)(2,1)S(1)} %get-tuple-element.75), channel_id=1, source_target_pairs={{0,1},{4,5},{8,9},{12,13},{16,17},{20,21},{24,25},{28,29}} | collective-permute-start | bytes 897032 | tf_op jit(solution)/shard_map/ppermute | solution.py:642
  11.3 13.9 %collective-permute-start.3 = (bf16[1168,128]{1,0:T(8,128)(2,1)S(1)}, bf16[1168,128]{1,0:T(8,128)(2,1)S(1)}, u32[]{:S(2)}, u32[]{:S(2)}) collective-permute-start(bf16[1168,128]{1,0:T(8,128)(2,1)S(1)} %get-tuple-element.54), channel_id=1, source_target_pairs={{0,1},{4,5},{8,9},{12,13},{16,17},{20,21},{24,25},{28,29}} | collective-permute-start | bytes 897032 | tf_op jit(solution)/shard_map/ppermute | solution.py:642
  21.8 4.1 %collective-permute-start.1 = (bf16[1168,128]{1,0:T(8,128)(2,1)S(1)}, bf16[1168,128]{1,0:T(8,128)(2,1)S(1)}, u32[]{:S(2)}, u32[]{:S(2)}) collective-permute-start(bf16[1168,128]{1,0:T(8,128)(2,1)S(1)} %pass_1_0.1), channel_id=1, source_target_pairs={{1,2},{5,6},{9,10},{13,14},{17,18},{21,22},{25,26},{29,30}} | collective-permute-start | bytes 897032 | tf_op jit(solution)/shard_map/ppermute | solution.py:642
  25.2 2.2 %collective-permute-start.4 = (bf16[1168,128]{1,0:T(8,128)(2,1)S(1)}, bf16[1168,128]{1,0:T(8,128)(2,1)S(1)}, u32[]{:S(2)}, u32[]{:S(2)}) collective-permute-start(bf16[1168,128]{1,0:T(8,128)(2,1)S(1)} %pass_1_1.1), channel_id=1, source_target_pairs={{1,2},{5,6},{9,10},{13,14},{17,18},{21,22},{25,26},{29,30}} | collective-permute-start | bytes 897032 | tf_op jit(solution)/shard_map/ppermute | solution.py:642
  25.9 3.0 %copy-start.6 = (f32[384,384]{1,0:T(8,128)S(1)}, f32[384,384]{1,0:T(8,128)}, u32[]{:S(2)}) copy-start(f32[384,384]{1,0:T(8,128)} %inverse) | copy-start | bytes 1769476
  25.9 17.0 %collective-permute-start.2 = (bf16[1168,128]{1,0:T(8,128)(2,1)S(1)}, bf16[1168,128]{1,0:T(8,128)(2,1)S(1)}, u32[]{:S(2)}, u32[]{:S(2)}) collective-permute-start(bf16[1168,128]{1,0:T(8,128)(2,1)S(1)} %pass_2_0.1), channel_id=1, source_target_pairs={{2,3},{6,7},{10,11},{14,15},{18,19},{22,23},{26,27},{30,31}} | collective-permute-start | bytes 897032 | tf_op jit(solution)/shard_map/ppermute | solution.py:642
  27.6 21.7 %collective-permute-start.5 = (bf16[1168,128]{1,0:T(8,128)(2,1)S(1)}, bf16[1168,128]{1,0:T(8,128)(2,1)S(1)}, u32[]{:S(2)}, u32[]{:S(2)}) collective-permute-start(bf16[1168,128]{1,0:T(8,128)(2,1)S(1)} %pass_2_1.1), channel_id=1, source_target_pairs={{2,3},{6,7},{10,11},{14,15},{18,19},{22,23},{26,27},{30,31}} | collective-permute-start | bytes 897032 | tf_op jit(solution)/shard_map/ppermute | solution.py:642
  49.3 9.7 %copy-start = (f32[4,384]{1,0:T(4,128)S(1)}, f32[4,384]{1,0:T(4,128)}, u32[]{:S(2)}) copy-start(f32[4,384]{1,0:T(4,128)} %doping.1) | copy-start | bytes 18436

commit v6 on v5

--- a/solution.py
+++ b/solution.py
@@ -366,17 +366,21 @@
 def begin_kernel(
     impulse_count, slot,
     constants_ref, contact_ref, counts_ref,
-    onsite, hopping, potential, base, wave, so_far, held,
-    density, sent,
-    constants, contact, counts, scalar_sem, scales, g, left,
+    onsite, hopping, potential, base, wave, so_far, *refs,
 ):
-    del held
+    held, refs = refs[:-9], refs[-9:]
+    density, sent, constants, contact, counts, scalar_sem, scales, g, left = refs
     slabs, orbitals = onsite.shape
     parts = orbitals // LANE
     position = lax.axis_index("en")
     density[...] = so_far[...]
     active = position == 0
     if slot == 0:
+
+        @pl.when(jnp.logical_and(active, takes_first_levels()))
+        def _():
+            sent[...] = held[0][...]
+
         active = jnp.logical_and(active, jnp.logical_not(takes_first_levels()))
 
     @pl.when(active)
@@ -686,21 +690,21 @@
         pltpu.SemaphoreType.DMA((3,)),
     ]
 
-    def begin(slot, density, held):
+    def begin(slot, density, *held):
         return vmem_call(
             functools.partial(begin_kernel, impulse_count, slot),
             (density_shape, block_shape),
-            (*small, *loaded, density, held),
-            [anywhere] * 3 + [vmem] * 7,
+            (*small, *loaded, density, *held),
+            [anywhere] * 3 + [vmem] * (6 + len(held)),
             scalar_scratch + [scales_scratch] + work,
             f"begin_{slot}",
             3 * flops,
-            input_output_aliases={8: 0, 9: 1},
+            input_output_aliases={8: 0, 9: 1} if held else {8: 0},
         )
 
     density, block = begin(0, density, block)
     arrived = [forward(block, 0)]
-    density, block = begin(1, density, jnp.zeros(block_shape.shape, BF16))
+    density, block = begin(1, density)
     arrived.append(forward(block, 0))
     small, _ = lax.optimization_barrier((small, block))
     made = vmem_call(
@@ -774,13 +778,11 @@
 
     came = [[arrived[0]], [arrived[1]]]
     carried, local = [carriers_of(0)], [local_of(0)]
-    made[1], _ = lax.optimization_barrier((made[1], local[0][1]))
-    carried.append(carriers_of(1))
-    came[0][0], _ = lax.optimization_barrier((came[0][0], carried[1]))
     for stage in range(1, en_size - 1):
         for slot in range(2):
             if stage == 1 and slot == 1:
                 made[1], _ = lax.optimization_barrier((made[1], block))
+                carried.append(carriers_of(1))
                 local.append(local_of(1))
             block = pass_on(stage, slot, came[slot][-1])
             came[slot].append(forward(block, stage))

time: 60.2 us -> 57.3 us (0.952)
  waiting for transfers between devices: 20.5 us -> 17.6 us
    ppermute x6, waiting for transfers between devices: 17.7 us -> 14.7 us  [forward(): return lax.ppermute(block, 'en', [(stage, stage + 1)])]
  transfers between devices with their start and end apart: 7 -> 7, of which waited for: 3 -> 3; matrix products, arithmetic and copies ran while one was open for 0% -> 0% of each run, Pallas kernels for 29% -> 30%
where the time goes in v6:
time: 57.3 us; the launch traced here: 56.9 us
  Pallas kernels  20.5 us (36%)
  waiting for transfers between devices  17.6 us (31%)
  starting transfers between devices  9.16 us (16%)
  blocking collectives  7.31 us (13%)
  between operations  1.55 us (3%)
  local copies, waits for them, and re-layouts  0.65 us (1%)
    pallas_call x16, Pallas kernels, vmem_call(): pl.pallas_call(kernel, out_shape=tuple(outs), in_specs=in_specs, out_spec...  20.5 us
    ppermute x6, waiting for transfers between devices, forward(): return lax.ppermute(block, 'en', [(stage, stage + 1)])  14.7 us
    all_to_all x1, blocking collectives, gather_over(): return lax.all_to_all(copies, axis, 0, 0)  7.31 us
    ppermute x6, starting transfers between devices, forward(): return lax.ppermute(block, 'en', [(stage, stage + 1)])  5.44 us
    all_to_all x1, starting transfers between devices, body(): lax.all_to_all(jnp.tile(counts, kt_size), 'kt', 0, 0, tiled=True)  3.72 us
    all_to_all x1, waiting for transfers between devices, body(): lax.all_to_all(jnp.tile(counts, kt_size), 'kt', 0, 0, tiled=True)  2.8 us
  transfers between devices with their start and end apart: 7, of which 3 were waited for; matrix products, arithmetic and copies ran while one was open for 0% of the time, Pallas kernels for 30%

profile of v6, /device:TPU:24, one launch (start us, length us, event | category | flops | bytes accessed | tf_op | source)
XLA Modules:
  0.0 56.9 jit_solution(127675880547021761)
XLA Ops:
  1.3 0.6 %tile.10 = s32[8,1,1]{2,1,0:T(1,128)} broadcast(s32[]{:T(128)} %bitcast.1), dimensions={} | broadcast | bytes 36 | tf_op jit(solution)/shard_map/tile | solution.py:659
  1.9 3.7 %all-to-all-start = ((s32[8,1,1]{2,1,0:T(1,128)}), s32[8,1,1]{2,1,0:T(1,128)S(1)}, u32[]{:S(2)}, u32[]{:S(2)}) async-start(s32[8,1,1]{2,1,0:T(1,128)} %tile.10), calls=%async_computation | async-start | bytes 8192 | tf_op jit(solution)/shard_map/all_to_all | solution.py:659
  5.6 0.0 copy-start.1
  5.6 0.0 copy-start.2
  5.6 0.0 copy-start.3
  5.6 0.0 copy-start.4
  5.6 0.0 copy-start.5
  5.6 1.7 %lead.1 = (bf16[1168,128]{1,0:T(8,128)(2,1)S(1)}, f32[4,384]{1,0:T(4,128)S(1)}, bf16[4,384,384]{2,1,0:T(8,128)(2,1)S(1)}, bf16[4,384,384]{2,1,0:T(8,128)(2,1)S(1)}) custom-call(f32[12]{0:T(128)} %constant.2.clone.constants_hbm.constants_ref, s32[2]{0:T(128)} %contact_ref.4, f32[4,384]{1,0:T(4,128)} %onsite.4, f32[4,384]{1,0:T(4,128)} %hopping.4, ...), custom_call_target="tpu_custom_call" | custom-call | flops 1358954496 | bytes 2097152 | tf_op jit(solution)/shard_map/lead/pallas_call | solution.py:574
  7.4 2.8 %all-to-all-done = s32[8,1,1]{2,1,0:T(1,128)S(1)} async-done(((s32[8,1,1]{2,1,0:T(1,128)}), s32[8,1,1]{2,1,0:T(1,128)S(1)}, u32[]{:S(2)}, u32[]{:S(2)}) %all-to-all-start) | async-done | bytes 64 | tf_op jit(solution)/shard_map/all_to_all | solution.py:659
  10.2 0.2 reduce.counts_ref
  10.4 0.0 copy-done.1
  10.4 0.0 copy-done.2
  10.4 0.0 copy-done.3
  10.4 0.0 copy-done.4
  10.4 0.0 copy-done.5
  10.5 0.1 begin_0.1
  10.5 0.7 %collective-permute-start = (bf16[1168,128]{1,0:T(8,128)(2,1)S(1)}, bf16[1168,128]{1,0:T(8,128)(2,1)S(1)}, u32[]{:S(2)}, u32[]{:S(2)}) collective-permute-start(bf16[1168,128]{1,0:T(8,128)(2,1)S(1)} %get-tuple-element.66), channel_id=1, source_target_pairs={{0,1},{4,5},{8,9},{12,13},{16,17},{20,21},{24,25},{28,29}} | collective-permute-start | bytes 897032 | tf_op jit(solution)/shard_map/ppermute | solution.py:646
  11.3 0.7 %collective-permute-start.3 = (bf16[1168,128]{1,0:T(8,128)(2,1)S(1)}, bf16[1168,128]{1,0:T(8,128)(2,1)S(1)}, u32[]{:S(2)}, u32[]{:S(2)}) collective-permute-start(bf16[1168,128]{1,0:T(8,128)(2,1)S(1)} %get-tuple-element.50), channel_id=1, source_target_pairs={{0,1},{4,5},{8,9},{12,13},{16,17},{20,21},{24,25},{28,29}} | collective-permute-start | bytes 897032 | tf_op jit(solution)/shard_map/ppermute | solution.py:646
  11.9 2.9 %prepare.1 = (bf16[4,384,384]{2,1,0:T(8,128)(2,1)S(1)}, f32[4,1536,128]{2,1,0:T(8,128)S(1)}, f32[9,8,384]{2,1,0:T(8,128)S(1)}, bf16[4,384,384]{2,1,0:T(8,128)(2,...) custom-call(f32[12]{0:T(128)S(1)} %copy-done.5, s32[2]{0:T(128)S(1)} %copy-done.4, s32[8]{0:T(128)S(1)} %reduce.counts_ref, ...), custom_call_target="tpu_custom_call" | custom-call | flops 28311552 | bytes 65536 | tf_op jit(solution)/shard_map/prepare/pallas_call | solution.py:574
  14.8 2.1 %carriers_0.1 = (bf16[1536,768]{1,0:T(8,128)(2,1)S(1)}, bf16[768,768]{1,0:T(8,128)(2,1)S(1)}) custom-call(bf16[4,384,384]{2,1,0:T(8,128)(2,1)S(1)} %get-tuple-element.60.couple, f32[9,8,384]{2,1,0:T(8,128)S(1)} %get-tuple-element.62.entry), custom_call_target="tpu_custom_call" | custom-call | flops 28311552 | bytes 65536 | tf_op jit(solution)/shard_map/carriers_0/pallas_call | solution.py:574
  16.9 2.8 %local_0.1 = (f32[1536,128]{1,0:T(8,128)S(1)}, f32[4,384]{1,0:T(4,128)S(1)}) custom-call(bf16[4,384,384]{2,1,0:T(8,128)(2,1)S(1)} %get-tuple-element.60.couple, f32[4,1536,128]{2,1,0:T(8,128)S(1)} %get-tuple-element.61.scales, f32[9,8,384]{2,1,0:T(8,128)S(1)} %get-tuple-element.62.entry), custom_call_target="tpu_custom_call" | custom-call | flops 28311552 | bytes 65536 | tf_op jit(solution)/shard_map/local_0/pallas_call | solution.py:574
  19.7 0.0 collective-permute-done.arrived.refs_0_
  19.8 0.7 %collective-permute-start.1 = (bf16[1168,128]{1,0:T(8,128)(2,1)S(1)}, bf16[1168,128]{1,0:T(8,128)(2,1)S(1)}, u32[]{:S(2)}, u32[]{:S(2)}) collective-permute-start(bf16[1168,128]{1,0:T(8,128)(2,1)S(1)} %pass_1_0.1), channel_id=1, source_target_pairs={{1,2},{5,6},{9,10},{13,14},{17,18},{21,22},{25,26},{29,30}} | collective-permute-start | bytes 897032 | tf_op jit(solution)/shard_map/ppermute | solution.py:646
  20.4 2.1 %carriers_1.1 = (bf16[1536,768]{1,0:T(8,128)(2,1)S(1)}, bf16[768,768]{1,0:T(8,128)(2,1)S(1)}) custom-call(bf16[4,384,384]{2,1,0:T(8,128)(2,1)S(1)} %get-tuple-element.67.couple, f32[9,8,384]{2,1,0:T(8,128)S(1)} %get-tuple-element.68.entry), custom_call_target="tpu_custom_call" | custom-call | flops 28311552 | bytes 65536 | tf_op jit(solution)/shard_map/carriers_1/pallas_call | solution.py:574
  22.5 2.6 %local_1.1 = (f32[1536,128]{1,0:T(8,128)S(1)}, f32[4,384]{1,0:T(4,128)S(1)}) custom-call(bf16[4,384,384]{2,1,0:T(8,128)(2,1)S(1)} %get-tuple-element.67.couple, f32[4,1536,128]{2,1,0:T(8,128)S(1)} %get-tuple-element.70.scales, f32[9,8,384]{2,1,0:T(8,128)S(1)} %get-tuple-element.68.entry), custom_call_target="tpu_custom_call" | custom-call | flops 28311552 | bytes 65536 | tf_op jit(solution)/shard_map/local_1/pallas_call | solution.py:574
  25.2 0.0 collective-permute-done.3.arrived.refs_0_
  25.2 0.7 %collective-permute-start.4 = (bf16[1168,128]{1,0:T(8,128)(2,1)S(1)}, bf16[1168,128]{1,0:T(8,128)(2,1)S(1)}, u32[]{:S(2)}, u32[]{:S(2)}) collective-permute-start(bf16[1168,128]{1,0:T(8,128)(2,1)S(1)} %pass_1_1.1), channel_id=1, source_target_pairs={{1,2},{5,6},{9,10},{13,14},{17,18},{21,22},{25,26},{29,30}} | collective-permute-start | bytes 897032 | tf_op jit(solution)/shard_map/ppermute | solution.py:646
  25.9 0.0 collective-permute-done.1.arrived.refs_1_
  25.9 0.0 copy-start.6
  25.9 1.4 %collective-permute-start.2 = (bf16[1168,128]{1,0:T(8,128)(2,1)S(1)}, bf16[1168,128]{1,0:T(8,128)(2,1)S(1)}, u32[]{:S(2)}, u32[]{:S(2)}) collective-permute-start(bf16[1168,128]{1,0:T(8,128)(2,1)S(1)} %pass_2_0.1), channel_id=1, source_target_pairs={{2,3},{6,7},{10,11},{14,15},{18,19},{22,23},{26,27},{30,31}} | collective-permute-start | bytes 897032 | tf_op jit(solution)/shard_map/ppermute | solution.py:646
  27.4 0.0 collective-permute-done.4.arrived.refs_1_
  27.4 1.3 %collective-permute-start.5 = (bf16[1168,128]{1,0:T(8,128)(2,1)S(1)}, bf16[1168,128]{1,0:T(8,128)(2,1)S(1)}, u32[]{:S(2)}, u32[]{:S(2)}) collective-permute-start(bf16[1168,128]{1,0:T(8,128)(2,1)S(1)} %pass_2_1.1), channel_id=1, source_target_pairs={{2,3},{6,7},{10,11},{14,15},{18,19},{22,23},{26,27},{30,31}} | collective-permute-start | bytes 897032 | tf_op jit(solution)/shard_map/ppermute | solution.py:646
  28.7 0.0 copy-done.6
  28.7 0.2 split_inverse.1
  28.9 10.1 %collective-permute-done.2.refs_2_ = bf16[1168,128]{1,0:T(8,128)(2,1)S(1)} collective-permute-done((bf16[1168,128]{1,0:T(8,128)(2,1)S(1)}, bf16[1168,128]{1,0:T(8,128)(2,1)S(1)}, u32[]{:S(2)}, u32[]{:S(2)}) %collective-permute-start.2) | collective-permute-done | bytes 299040 | tf_op jit(solution)/shard_map/ppermute | solution.py:646
  39.1 2.6 %density_0.1.so_far = f32[4,384]{1,0:T(4,128)S(1)} custom-call(bf16[1536,768]{1,0:T(8,128)(2,1)S(1)} %get-tuple-element.64.carriers, f32[9,8,384]{2,1,0:T(8,128)S(1)} %get-tuple-element.62.entry, f32[4,384]{1,0:T(4,128)S(1)} %get-tuple-element.72.local_densities, f32[4,384]{1,0:T(4,128)S(1)} %get-tuple-element.73.so_far, ...), custom_call_target="tpu_custom_call", output_to_operand_aliasing={{}: (3, {})} | custom-call | flops 1811939328 | bytes 2097152 | tf_op jit(solution)/shard_map/density_0/pallas_call | solution.py:574
  41.7 4.6 %collective-permute-done.5.refs_2_ = bf16[1168,128]{1,0:T(8,128)(2,1)S(1)} collective-permute-done((bf16[1168,128]{1,0:T(8,128)(2,1)S(1)}, bf16[1168,128]{1,0:T(8,128)(2,1)S(1)}, u32[]{:S(2)}, u32[]{:S(2)}) %collective-permute-start.5) | collective-permute-done | bytes 299040 | tf_op jit(solution)/shard_map/ppermute | solution.py:646
  46.3 0.0 copy-start
  46.3 2.4 %density_1.1 = f32[4,384]{1,0:T(4,128)S(1)} custom-call(bf16[1536,768]{1,0:T(8,128)(2,1)S(1)} %get-tuple-element.69.carriers, f32[9,8,384]{2,1,0:T(8,128)S(1)} %get-tuple-element.68.entry, f32[4,384]{1,0:T(4,128)S(1)} %get-tuple-element.71.local_densities, f32[4,384]{1,0:T(4,128)S(1)} %density_0.1.so_far, ...), custom_call_target="tpu_custom_call", output_to_operand_aliasing={{}: (3, {})} | custom-call | flops 1811939328 | bytes 2097152 | tf_op jit(solution)/shard_map/density_1/pallas_call | solution.py:574
  48.8 7.3 %all_to_all.14.gathered = f32[8,4,384]{2,1,0:T(4,128)S(1)} all-to-all(f32[8,4,384]{2,1,0:T(4,128)S(1)} %broadcast_in_dim.2), channel_id=1, replica_groups=mesh['kt'=8,'en'=4] {'kt'}, dimensions={0} | all-to-all | bytes 98304 | tf_op jit(solution)/shard_map/all_to_all | solution.py:620
  56.1 0.0 copy-done
  56.1 0.9 %last.1 = (f32[4,384]{1,0:T(4,128)}, f32[4,384]{1,0:T(4,128)}) custom-call(f32[8,4,384]{2,1,0:T(4,128)S(1)} %all_to_all.14.gathered, f32[4,384]{1,0:T(4,128)S(1)} %copy-done, bf16[384,384]{1,0:T(8,128)(2,1)S(1)} %get-tuple-element.81.high, bf16[384,384]{1,0:T(8,128)(2,1)S(1)} %get-tuple-element.82.middle, bf16[384,384]{1,0:T(8,128)(2,1)S(1)} %get-tuple-element.83.low), custom_call_target="tpu_custom_call" | custom-call | flops 113246208 | bytes 2097152 | tf_op jit(solution)/shard_map/last/pallas_call | solution.py:574
  (6 shorter events, 0.1 us)
Async XLA Ops:
  1.9 8.3 %all-to-all-start = ((s32[8,1,1]{2,1,0:T(1,128)}), s32[8,1,1]{2,1,0:T(1,128)S(1)}, u32[]{:S(2)}, u32[]{:S(2)}) async-start(s32[8,1,1]{2,1,0:T(1,128)} %tile.10), calls=%async_computation | async-start | bytes 8192 | tf_op jit(solution)/shard_map/all_to_all | solution.py:659
  5.6 4.8 %copy-start.1 = (f32[4,384]{1,0:T(4,128)S(1)}, f32[4,384]{1,0:T(4,128)}, u32[]{:S(2)}) copy-start(f32[4,384]{1,0:T(4,128)} %onsite.4) | copy-start | bytes 18436
  5.6 4.8 %copy-start.2 = (f32[4,384]{1,0:T(4,128)S(1)}, f32[4,384]{1,0:T(4,128)}, u32[]{:S(2)}) copy-start(f32[4,384]{1,0:T(4,128)} %hopping.4) | copy-start | bytes 18436
  5.6 4.8 %copy-start.3 = (f32[4,384]{1,0:T(4,128)S(1)}, f32[4,384]{1,0:T(4,128)}, u32[]{:S(2)}) copy-start(f32[4,384]{1,0:T(4,128)} %potential.4) | copy-start | bytes 18436
  5.6 4.8 %copy-start.4 = (s32[2]{0:T(128)S(1)}, s32[2]{0:T(128)}, u32[]{:S(2)}) copy-start(s32[2]{0:T(128)} %contact_ref.4) | copy-start | bytes 28
  5.6 4.8 %copy-start.5 = (f32[12]{0:T(128)S(1)}, f32[12]{0:T(128)}, u32[]{:S(2)}) copy-start(f32[12]{0:T(128)} %constant.2.clone.constants_hbm.constants_ref) | copy-start | bytes 148
  10.5 9.2 %collective-permute-start = (bf16[1168,128]{1,0:T(8,128)(2,1)S(1)}, bf16[1168,128]{1,0:T(8,128)(2,1)S(1)}, u32[]{:S(2)}, u32[]{:S(2)}) collective-permute-start(bf16[1168,128]{1,0:T(8,128)(2,1)S(1)} %get-tuple-element.66), channel_id=1, source_target_pairs={{0,1},{4,5},{8,9},{12,13},{16,17},{20,21},{24,25},{28,29}} | collective-permute-start | bytes 897032 | tf_op jit(solution)/shard_map/ppermute | solution.py:646
  11.3 13.9 %collective-permute-start.3 = (bf16[1168,128]{1,0:T(8,128)(2,1)S(1)}, bf16[1168,128]{1,0:T(8,128)(2,1)S(1)}, u32[]{:S(2)}, u32[]{:S(2)}) collective-permute-start(bf16[1168,128]{1,0:T(8,128)(2,1)S(1)} %get-tuple-element.50), channel_id=1, source_target_pairs={{0,1},{4,5},{8,9},{12,13},{16,17},{20,21},{24,25},{28,29}} | collective-permute-start | bytes 897032 | tf_op jit(solution)/shard_map/ppermute | solution.py:646
  19.8 6.1 %collective-permute-start.1 = (bf16[1168,128]{1,0:T(8,128)(2,1)S(1)}, bf16[1168,128]{1,0:T(8,128)(2,1)S(1)}, u32[]{:S(2)}, u32[]{:S(2)}) collective-permute-start(bf16[1168,128]{1,0:T(8,128)(2,1)S(1)} %pass_1_0.1), channel_id=1, source_target_pairs={{1,2},{5,6},{9,10},{13,14},{17,18},{21,22},{25,26},{29,30}} | collective-permute-start | bytes 897032 | tf_op jit(solution)/shard_map/ppermute | solution.py:646
  25.2 2.2 %collective-permute-start.4 = (bf16[1168,128]{1,0:T(8,128)(2,1)S(1)}, bf16[1168,128]{1,0:T(8,128)(2,1)S(1)}, u32[]{:S(2)}, u32[]{:S(2)}) collective-permute-start(bf16[1168,128]{1,0:T(8,128)(2,1)S(1)} %pass_1_1.1), channel_id=1, source_target_pairs={{1,2},{5,6},{9,10},{13,14},{17,18},{21,22},{25,26},{29,30}} | collective-permute-start | bytes 897032 | tf_op jit(solution)/shard_map/ppermute | solution.py:646
  25.9 2.8 %copy-start.6 = (f32[384,384]{1,0:T(8,128)S(1)}, f32[384,384]{1,0:T(8,128)}, u32[]{:S(2)}) copy-start(f32[384,384]{1,0:T(8,128)} %inverse) | copy-start | bytes 1769476
  25.9 13.1 %collective-permute-start.2 = (bf16[1168,128]{1,0:T(8,128)(2,1)S(1)}, bf16[1168,128]{1,0:T(8,128)(2,1)S(1)}, u32[]{:S(2)}, u32[]{:S(2)}) collective-permute-start(bf16[1168,128]{1,0:T(8,128)(2,1)S(1)} %pass_2_0.1), channel_id=1, source_target_pairs={{2,3},{6,7},{10,11},{14,15},{18,19},{22,23},{26,27},{30,31}} | collective-permute-start | bytes 897032 | tf_op jit(solution)/shard_map/ppermute | solution.py:646
  27.4 18.9 %collective-permute-start.5 = (bf16[1168,128]{1,0:T(8,128)(2,1)S(1)}, bf16[1168,128]{1,0:T(8,128)(2,1)S(1)}, u32[]{:S(2)}, u32[]{:S(2)}) collective-permute-start(bf16[1168,128]{1,0:T(8,128)(2,1)S(1)} %pass_2_1.1), channel_id=1, source_target_pairs={{2,3},{6,7},{10,11},{14,15},{18,19},{22,23},{26,27},{30,31}} | collective-permute-start | bytes 897032 | tf_op jit(solution)/shard_map/ppermute | solution.py:646
  46.3 9.7 %copy-start = (f32[4,384]{1,0:T(4,128)S(1)}, f32[4,384]{1,0:T(4,128)}, u32[]{:S(2)}) copy-start(f32[4,384]{1,0:T(4,128)} %doping.1) | copy-start | bytes 18436

commit v7 on v6

--- a/solution.py
+++ b/solution.py
@@ -108,6 +108,17 @@
     return lax.axis_index("kt") % 2 == 1
 
 
+class Either:
+    def __init__(self, refs):
+        self.refs = refs
+        self.shape = refs[0].shape
+
+    def __getitem__(self, index):
+        if len(self.refs) == 1:
+            return self.refs[0][index]
+        return jnp.where(takes_first_levels(), self.refs[1][index], self.refs[0][index])
+
+
 def first_level_item(slot):
     return lax.axis_index("kt") - 1 + slot, jnp.int32(0)
 
@@ -146,21 +157,12 @@
     return inv_real, inv_imag
 
 
-def scale_rows(parts):
+def local_rows(parts):
     return 2 * len(blocks_on_or_below(parts)) * LANE
 
 
-def form_scales(slabs_wanted, inv_real, inv_imag, scales, parts):
-    slabs = inv_real.shape[0]
-    down = jnp.concatenate([inv_real, inv_imag], axis=0).T
-    for s in slabs_wanted:
-        for k, (r, c) in enumerate(blocks_on_or_below(parts)):
-            real_col = down[span(r), s : s + 1]
-            imag_col = down[span(r), slabs + s : slabs + s + 1]
-            rr = inv_real[s : s + 1, span(c)]
-            ri = inv_imag[s : s + 1, span(c)]
-            scales[s, span(2 * k), :] = real_col * rr - imag_col * ri
-            scales[s, span(2 * k + 1), :] = real_col * ri + imag_col * rr
+def columns_of(inv_real, inv_imag):
+    return jnp.concatenate([inv_real, inv_imag], axis=0).T
 
 
 def store_left(left, piece, half, c, parts):
@@ -182,7 +184,7 @@
 
 
 def finish_slab(
-    s, times_turned, left, g, packed, real_row, imag_row, scales, note, parts, local=None
+    s, times_turned, left, g, packed, columns, real_row, imag_row, note, parts, local=None
 ):
     last = (parts - 1) * LANE
     rows, cols = tile_indices()
@@ -192,10 +194,12 @@
 
     def finish(r, c, sr, si):
         k = numbers[r, c]
-        scale_real = scales[s, span(2 * k), :]
-        scale_imag = scales[s, span(2 * k + 1), :]
-        green_real = scale_real * sr - scale_imag * si
-        green_imag = scale_real * si + scale_imag * sr
+        real_col, imag_col = columns[0][span(r)], columns[1][span(r)]
+        half_real = real_col * sr - imag_col * si
+        half_imag = real_col * si + imag_col * sr
+        rr, ri = real_row[:, span(c)], imag_row[:, span(c)]
+        green_real = half_real * rr - half_imag * ri
+        green_imag = half_real * ri + half_imag * rr
         if r == c:
             green_real = green_real + jnp.where(diagonal, real_row[:, span(c)], 0.0)
             green_imag = green_imag + jnp.where(diagonal, imag_row[:, span(c)], 0.0)
@@ -232,10 +236,11 @@
 
 
 def first_segment(
-    coupled_of, inv_real, inv_imag, scales, weight, g, left, sent, density, local=None
+    coupled_of, inv_real, inv_imag, weight, g, left, sent, density, local=None
 ):
     slabs, orbitals = inv_real.shape
     parts = orbitals // LANE
+    down = columns_of(inv_real, inv_imag)
     if density is not None:
         density[0:1, :] += -weight * inv_imag[0:1, :]
     for s in range(1, slabs):
@@ -260,8 +265,9 @@
         final = s == slabs - 1
         finish_slab(
             s, times_turned, left, None if final else g, sent if final else None,
-            inv_real[s : s + 1, :], inv_imag[s : s + 1, :], scales, None if density is None else note, parts,
-            local if final else None,
+            (down[:, s : s + 1], down[:, slabs + s : slabs + s + 1]),
+            inv_real[s : s + 1, :], inv_imag[s : s + 1, :],
+            None if density is None else note, parts, local if final else None,
         )
 
 
@@ -285,27 +291,35 @@
 def lead_kernel(
     impulse_count,
     constants_hbm, contact_hbm, onsite_hbm, hopping_hbm, potential_hbm, base_hbm, wave_hbm,
-    sent, density, base, wave,
-    constants, contact, tables, scales, g, left, small_sem, table_sem, couple_sem,
+    sent, density, base, wave, couple_0, entry_0,
+    constants, contact, tables, g, left, small_sem, table_sem, couple_sem,
 ):
     slabs, orbitals = onsite_hbm.shape
     parts = orbitals // LANE
     position = lax.axis_index("en")
     density[...] = jnp.zeros_like(density)
+    small_copies = copies_of_constants(
+        constants_hbm, contact_hbm, constants, contact, small_sem
+    ) + [
+        pltpu.make_async_copy(source, tables.at[k], table_sem.at[k])
+        for k, source in enumerate((onsite_hbm, hopping_hbm, potential_hbm))
+    ]
+    for copy in small_copies:
+        copy.start()
+
+    def first_level_amounts():
+        momentum, level = first_level_item(0)
+        cosine, energy, weight = entry_amounts(constants, impulse_count, momentum, level)
+        inv_real, inv_imag = inverse_diagonal(
+            position, cosine, energy, contact, tables.at[0], tables.at[1], tables.at[2]
+        )
+        return cosine, weight, inv_real, inv_imag
 
     @pl.when(position == 0)
     def _():
-        small_copies = copies_of_constants(
-            constants_hbm, contact_hbm, constants, contact, small_sem
-        ) + [
-            pltpu.make_async_copy(source, tables.at[k], table_sem.at[k])
-            for k, source in enumerate((onsite_hbm, hopping_hbm, potential_hbm))
-        ]
         couple_copies = copies_of_couplings(
             base_hbm, wave_hbm, base, wave, couple_sem, range(1, slabs)
         )
-        for copy in small_copies:
-            copy.start()
         for s in couple_copies:
             for copy in couple_copies[s]:
                 copy.start()
@@ -314,14 +328,7 @@
 
         @pl.when(takes_first_levels())
         def _():
-            momentum, level = first_level_item(0)
-            cosine, energy, weight = entry_amounts(
-                constants, impulse_count, momentum, level
-            )
-            inv_real, inv_imag = inverse_diagonal(
-                position, cosine, energy, contact, tables.at[0], tables.at[1], tables.at[2]
-            )
-            form_scales(range(1, slabs), inv_real, inv_imag, scales, parts)
+            cosine, weight, inv_real, inv_imag = first_level_amounts()
 
             def coupled_of(s):
                 for copy in couple_copies[s]:
@@ -329,7 +336,7 @@
                 return coupling_of(base[s], wave[s], cosine)
 
             first_segment(
-                coupled_of, inv_real, inv_imag, scales, weight, g, left, sent, density
+                coupled_of, inv_real, inv_imag, weight, g, left, sent, density
             )
 
         @pl.when(jnp.logical_not(takes_first_levels()))
@@ -347,9 +354,18 @@
         for s in couple_copies:
             for copy in couple_copies[s]:
                 copy.start()
+        for copy in small_copies:
+            copy.wait()
         for s in couple_copies:
             for copy in couple_copies[s]:
                 copy.wait()
+
+        @pl.when(takes_first_levels())
+        def _():
+            cosine, weight, inv_real, inv_imag = first_level_amounts()
+            prepare(
+                cosine, weight, inv_real, inv_imag, base, wave, couple_0, entry_0
+            )
 
 
 def with_scalars(refs, scratch, sem):
@@ -368,8 +384,8 @@
     constants_ref, contact_ref, counts_ref,
     onsite, hopping, potential, base, wave, so_far, *refs,
 ):
-    held, refs = refs[:-9], refs[-9:]
-    density, sent, constants, contact, counts, scalar_sem, scales, g, left = refs
+    held, refs = refs[:-8], refs[-8:]
+    density, sent, constants, contact, counts, scalar_sem, g, left = refs
     slabs, orbitals = onsite.shape
     parts = orbitals // LANE
     position = lax.axis_index("en")
@@ -393,18 +409,16 @@
         inv_real, inv_imag = inverse_diagonal(
             position, cosine, energy, contact, onsite, hopping, potential
         )
-        form_scales(range(1, slabs), inv_real, inv_imag, scales, parts)
 
         def coupled_of(s):
             return coupling_of(base[s], wave[s], cosine)
 
-        first_segment(coupled_of, inv_real, inv_imag, scales, weight, g, left, sent, density)
-
-
-def prepare(cosine, weight, inv_real, inv_imag, base, wave, couple, scales, entry):
+        first_segment(coupled_of, inv_real, inv_imag, weight, g, left, sent, density)
+
+
+def prepare(cosine, weight, inv_real, inv_imag, base, wave, couple, entry):
     slabs, orbitals = inv_real.shape
     parts = orbitals // LANE
-    form_scales(range(slabs), inv_real, inv_imag, scales, parts)
     for s in range(slabs):
         entry[s] = jnp.broadcast_to(inv_real[s : s + 1, :], entry.shape[1:])
         entry[slabs + s] = jnp.broadcast_to(inv_imag[s : s + 1, :], entry.shape[1:])
@@ -420,27 +434,31 @@
 def prepare_kernel(
     impulse_count,
     constants_ref, contact_ref, counts_ref, onsite, hopping, potential, base, wave,
-    couple_0, scales_0, entry_0,
-    couple_1, scales_1, entry_1,
+    couple_0, entry_0,
+    couple_1, entry_1,
     constants, contact, counts, scalar_sem,
 ):
     position = lax.axis_index("en")
+
+    def prepare_slot(slot, made):
+        momentum, level = item_of(counts, slot)
+        cosine, energy, weight = entry_amounts(constants, impulse_count, momentum, level)
+        inv_real, inv_imag = inverse_diagonal(
+            position, cosine, energy, contact, onsite, hopping, potential
+        )
+        prepare(cosine, weight, inv_real, inv_imag, base, wave, *made)
 
     @pl.when(position > 0)
     def _():
         with_scalars(
             (constants_ref, contact_ref, counts_ref), (constants, contact, counts), scalar_sem
         )
-        for slot, made in (
-            (0, (couple_0, scales_0, entry_0)),
-            (1, (couple_1, scales_1, entry_1)),
-        ):
-            momentum, level = item_of(counts, slot)
-            cosine, energy, weight = entry_amounts(constants, impulse_count, momentum, level)
-            inv_real, inv_imag = inverse_diagonal(
-                position, cosine, energy, contact, onsite, hopping, potential
-            )
-            prepare(cosine, weight, inv_real, inv_imag, base, wave, *made)
+
+        @pl.when(jnp.logical_not(takes_first_levels()))
+        def _():
+            prepare_slot(0, (couple_0, entry_0))
+
+        prepare_slot(1, (couple_1, entry_1))
 
 
 def rows_of_entry(entry, slabs):
@@ -449,7 +467,9 @@
     return inv_real, inv_imag, entry[2 * slabs, 0:1, 0:1]
 
 
-def carrier_kernel(couple, entry, carriers, cross):
+def carrier_kernel(calls, *refs):
+    couple, entry = Either(refs[:calls]), Either(refs[calls : 2 * calls])
+    carriers, cross = refs[2 * calls :]
     slabs, orbitals, _ = couple.shape
     parts = orbitals // LANE
 
@@ -483,19 +503,28 @@
                 cross[span(parts + c), span(r)] = -imag
 
 
-def local_kernel(couple, scales, entry, local, densities, g, left):
+def local_kernel(calls, odd_too, even_too, *refs):
+    couple, entry = Either(refs[:calls]), Either(refs[calls : 2 * calls])
+    local, densities, g, left = refs[2 * calls :]
     slabs = couple.shape[0]
-
-    @pl.when(lax.axis_index("en") > 0)
+    active = lax.axis_index("en") > 0
+    if not odd_too:
+        active = jnp.logical_and(active, jnp.logical_not(takes_first_levels()))
+    if not even_too:
+        active = jnp.logical_and(active, takes_first_levels())
+
+    @pl.when(active)
     def _():
         inv_real, inv_imag, weight = rows_of_entry(entry, slabs)
         densities[...] = jnp.zeros_like(densities)
         first_segment(
-            lambda s: couple[s], inv_real, inv_imag, scales, weight, g, left, None, densities, local
-        )
-
-
-def pass_kernel(stage, local, carriers, cross, arrived, sent, wide, half_way):
+            lambda s: couple[s], inv_real, inv_imag, weight, g, left, None, densities, local
+        )
+
+
+def pass_kernel(stage, calls, *refs):
+    local = Either(refs[:calls])
+    carriers, cross, arrived, sent, wide, half_way = refs[calls:]
     orbitals = carriers.shape[1] // 2
     parts = orbitals // LANE
 
@@ -524,8 +553,10 @@
         pack_middles(sent, middles, parts)
 
 
-def density_kernel(carriers, entry, local_densities, so_far, *refs):
-    arrived, (density, wide, total) = refs[:-3], refs[-3:]
+def density_kernel(calls, carriers, *refs):
+    entry, refs = Either(refs[: calls[0]]), refs[calls[0] :]
+    local_densities, refs = Either(refs[: calls[1]]), refs[calls[1] :]
+    so_far, arrived, (density, wide, total) = refs[0], refs[1:-3], refs[-3:]
     slabs, orbitals = so_far.shape
     parts = orbitals // LANE
     position = lax.axis_index("en")
@@ -648,9 +679,7 @@
     block_shape = jax.ShapeDtypeStruct((packed_rows(orbitals), LANE), BF16)
     density_shape = jax.ShapeDtypeStruct((slabs, orbitals), F32)
     couple_shape = jax.ShapeDtypeStruct((slabs, orbitals, orbitals), BF16)
-    scales_shape = jax.ShapeDtypeStruct((slabs, scale_rows(parts), LANE), F32)
     entry_shape = jax.ShapeDtypeStruct((2 * slabs + 1, 8, orbitals), F32)
-    scales_scratch = pltpu.VMEM(scales_shape.shape, F32)
     work = [
         pltpu.VMEM((orbitals, 2 * orbitals), BF16),
         pltpu.VMEM((2 * orbitals, orbitals), BF16),
@@ -659,16 +688,15 @@
     counts_all = lax.all_to_all(jnp.tile(counts, kt_size), "kt", 0, 0, tiled=True)
     given = (constants, contact_slabs, onsite, hopping, potential_in, couple_base, couple_wave)
     pinned = [pltpu.with_memory_space_constraint(t, pltpu.HBM) for t in given]
-    block, density, *loaded = vmem_call(
+    block, density, *rest = vmem_call(
         functools.partial(lead_kernel, impulse_count),
-        (block_shape, density_shape, couple_shape, couple_shape),
+        (block_shape, density_shape) + (couple_shape,) * 3 + (entry_shape,),
         pinned,
         [hbm] * len(pinned),
         [
             pltpu.SMEM(constants.shape, F32),
             pltpu.SMEM(contact_slabs.shape, jnp.int32),
             pltpu.VMEM((3, slabs, orbitals), F32),
-            scales_scratch,
         ]
         + work
         + [
@@ -679,6 +707,7 @@
         "lead",
         3 * flops,
     )
+    loaded, made_first = rest[:2], rest[2:]
     block, counts_all = lax.optimization_barrier((block, counts_all))
     small = (constants, contact_slabs, counts_all, onsite, hopping, potential_in)
 
@@ -696,7 +725,7 @@
             (density_shape, block_shape),
             (*small, *loaded, density, *held),
             [anywhere] * 3 + [vmem] * (6 + len(held)),
-            scalar_scratch + [scales_scratch] + work,
+            scalar_scratch + work,
             f"begin_{slot}",
             3 * flops,
             input_output_aliases={8: 0, 9: 1} if held else {8: 0},
@@ -709,7 +738,7 @@
     small, _ = lax.optimization_barrier((small, block))
     made = vmem_call(
         functools.partial(prepare_kernel, impulse_count),
-        (couple_shape, scales_shape, entry_shape) * 2,
+        (couple_shape, entry_shape) * 2,
         (*small, *loaded),
         [anywhere] * 3 + [vmem] * 5,
         scalar_scratch,
@@ -717,42 +746,44 @@
         flops // 16,
         2**16,
     )
-    made = [made[:3], made[3:]]
+    made = [list(zip(made[:2], made_first)), [(one,) for one in made[2:]]]
 
     carriers_shape = jax.ShapeDtypeStruct((slabs * orbitals, 2 * orbitals), BF16)
     double_shape = jax.ShapeDtypeStruct((2 * orbitals, 2 * orbitals), BF16)
 
     def carriers_of(slot):
-        couple, _, entry = made[slot]
+        couple, entry = made[slot]
         return vmem_call(
-            carrier_kernel,
+            functools.partial(carrier_kernel, len(couple)),
             (carriers_shape, double_shape),
-            (couple, entry),
-            [vmem] * 2,
+            (*couple, *entry),
+            [vmem] * (2 * len(couple)),
             [],
             f"carriers_{slot}",
             flops // 16,
             2**16,
         )
 
-    def local_of(slot):
+    def local_of(slot, odd_too=True, even_too=True):
+        couple, entry = made[slot]
         return vmem_call(
-            local_kernel,
-            (jax.ShapeDtypeStruct((scale_rows(parts), LANE), F32), density_shape),
-            made[slot],
-            [vmem] * 3,
+            functools.partial(local_kernel, len(couple), odd_too, even_too),
+            (jax.ShapeDtypeStruct((local_rows(parts), LANE), F32), density_shape),
+            (*couple, *entry),
+            [vmem] * (2 * len(couple)),
             work,
-            f"local_{slot}",
+            f"local_{slot}{int(even_too)}{int(odd_too)}",
             flops // 16,
             2**16,
         )
 
     def pass_on(stage, slot, block):
+        calls = [one[0] for one in local[slot]]
         return vmem_call(
-            functools.partial(pass_kernel, stage),
+            functools.partial(pass_kernel, stage, len(calls)),
             (block_shape,),
-            (local[slot][0], *carried[slot], block),
-            [vmem] * 4,
+            (*calls, *carried[slot], block),
+            [vmem] * (3 + len(calls)),
             [
                 pltpu.VMEM(double_shape.shape, BF16),
                 pltpu.VMEM((orbitals, 2 * orbitals), BF16),
@@ -762,28 +793,35 @@
         )[0]
 
     def densities(slot, density, came):
+        entry = made[slot][1]
+        calls = [one[1] for one in local[slot]]
+        before = 1 + len(entry) + len(calls)
         return vmem_call(
-            density_kernel,
+            functools.partial(density_kernel, (len(entry), len(calls))),
             (density_shape,),
-            (carried[slot][0], made[slot][2], local[slot][1], density, *came),
-            [vmem] * (4 + len(came)),
+            (carried[slot][0], *entry, *calls, density, *came),
+            [vmem] * (before + 1 + len(came)),
             [
                 pltpu.VMEM(double_shape.shape, BF16),
                 pltpu.VMEM((slabs * orbitals, LANE), F32),
             ],
             f"density_{slot}",
             4 * flops,
-            input_output_aliases={3: 0},
+            input_output_aliases={before: 0},
         )[0]
 
     came = [[arrived[0]], [arrived[1]]]
-    carried, local = [carriers_of(0)], [local_of(0)]
+    carried, local = [carriers_of(0)], [[local_of(0)]]
+    made[1], _ = lax.optimization_barrier((made[1], local[0][0][1]))
+    local.append([local_of(1, odd_too=False)])
+    came[0][0], local[1][0] = lax.optimization_barrier((came[0][0], local[1][0]))
     for stage in range(1, en_size - 1):
         for slot in range(2):
             if stage == 1 and slot == 1:
                 made[1], _ = lax.optimization_barrier((made[1], block))
                 carried.append(carriers_of(1))
-                local.append(local_of(1))
+                made[1], _ = lax.optimization_barrier((made[1], carried[1][1]))
+                local[1].append(local_of(1, even_too=False))
             block = pass_on(stage, slot, came[slot][-1])
             came[slot].append(forward(block, stage))
     for slot in range(2):

time: 57.3 us -> 66.2 us (1.16)
  local copies, waits for them, and re-layouts: 0.65 us -> 4.61 us
  blocking collectives: 7.31 us -> 9.95 us
  Pallas kernels: 20.5 us -> 22.1 us
  other arithmetic: 0.23 us -> 1.43 us
  waiting for transfers between devices: 17.6 us -> 16.7 us
    unnamed x14 -> x20, local copies, waits for them, and re-layouts: 0.04 us -> 4 us
    all_to_all x1, blocking collectives: 7.31 us -> 9.95 us  [gather_over(): return lax.all_to_all(copies, axis, 0, 0)]
    pallas_call x16 -> x17, Pallas kernels: 20.5 us -> 22.1 us  [vmem_call(): pl.pallas_call(kernel, out_shape=tuple(outs), in_specs=in_specs, out_spec...]
    all_to_all x1, waiting for transfers between devices: 2.8 us -> 1.47 us  [body(): lax.all_to_all(jnp.tile(counts, kt_size), 'kt', 0, 0, tiled=True)]
    all_to_all x1, other arithmetic: 0.23 us -> 1.43 us  [body(): lax.all_to_all(jnp.tile(counts, kt_size), 'kt', 0, 0, tiled=True)]
  transfers between devices with their start and end apart: 7 -> 7, of which waited for: 3 -> 3; matrix products, arithmetic and copies ran while one was open for 0% -> 0% of each run, Pallas kernels for 30% -> 26%
where the time goes in v7:
time: 66.2 us; the launch traced here: 65.7 us
  Pallas kernels  22.1 us (33%)
  waiting for transfers between devices  16.7 us (25%)
  blocking collectives  9.95 us (15%)
  starting transfers between devices  9.44 us (14%)
  local copies, waits for them, and re-layouts  4.61 us (7%)
  between operations  1.53 us (2%)
  other arithmetic  1.43 us (2%)
    pallas_call x17, Pallas kernels, vmem_call(): pl.pallas_call(kernel, out_shape=tuple(outs), in_specs=in_specs, out_spec...  22.1 us
    ppermute x6, waiting for transfers between devices, forward(): return lax.ppermute(block, 'en', [(stage, stage + 1)])  15.2 us
    all_to_all x1, blocking collectives, gather_over(): return lax.all_to_all(copies, axis, 0, 0)  9.95 us
    ppermute x6, starting transfers between devices, forward(): return lax.ppermute(block, 'en', [(stage, stage + 1)])  5.57 us
    unnamed x20, local copies, waits for them, and re-layouts  4 us
    all_to_all x1, starting transfers between devices, body(): lax.all_to_all(jnp.tile(counts, kt_size), 'kt', 0, 0, tiled=True)  3.87 us
    all_to_all x1, waiting for transfers between devices, body(): lax.all_to_all(jnp.tile(counts, kt_size), 'kt', 0, 0, tiled=True)  1.47 us
    all_to_all x1, other arithmetic, body(): lax.all_to_all(jnp.tile(counts, kt_size), 'kt', 0, 0, tiled=True)  1.43 us
  transfers between devices with their start and end apart: 7, of which 3 were waited for; matrix products, arithmetic and copies ran while one was open for 0% of the time, Pallas kernels for 26%

profile of v7, /device:TPU:24, one launch (start us, length us, event | category | flops | bytes accessed | tf_op | source)
XLA Modules:
  0.0 65.7 jit_solution(11152445772063737939)
XLA Ops:
  1.3 0.6 tile.10
  1.9 3.9 %all-to-all-start = ((s32[8,1,1]{2,1,0:T(1,128)}), s32[8,1,1]{2,1,0:T(1,128)}, u32[]{:S(2)}, u32[]{:S(2)}) async-start(s32[8,1,1]{2,1,0:T(1,128)} %tile.10), calls=%async_computation | async-start | bytes 8192 | tf_op jit(solution)/shard_map/all_to_all | solution.py:688
  5.7 0.0 copy-start.3
  5.8 2.5 %lead.1 = (bf16[1168,128]{1,0:T(8,128)(2,1)}, f32[4,384]{1,0:T(4,128)S(1)}, bf16[4,384,384]{2,1,0:T(8,128)(2,1)S(1)}, bf16[4,384,384]{2,1,0:T(8,128)(2,1)S(1)}, ...) custom-call(f32[12]{0:T(128)} %constant.2.clone.constants_hbm.constants_ref, s32[2]{0:T(128)} %contact_ref.4, ...), custom_call_target="tpu_custom_call" | custom-call | flops 1358954496 | bytes 2097152 | tf_op jit(solution)/shard_map/lead/pallas_call | solution.py:605
  8.2 0.0 copy-start
  8.2 0.6 copy-done
  8.9 1.5 %all-to-all-done = s32[8,1,1]{2,1,0:T(1,128)} async-done(((s32[8,1,1]{2,1,0:T(1,128)}), s32[8,1,1]{2,1,0:T(1,128)}, u32[]{:S(2)}, u32[]{:S(2)}) %all-to-all-start) | async-done | bytes 64 | tf_op jit(solution)/shard_map/all_to_all | solution.py:688
  10.3 1.4 %reduce.counts_ref = s32[8]{0:T(128)} reduce(s32[8,1,1]{2,1,0:T(1,128)} %all-to-all-done, s32[]{:T(128)} %constant.4), dimensions={1,2}, to_apply=%all_to_all.9.reduce_sub_computation | reduce | bytes 68 | tf_op jit(solution)/shard_map/all_to_all | solution.py:688
  11.8 0.0 copy-done.3
  11.8 0.0 copy-start.4
  11.8 0.7 %copy-done.4 = f32[4,384]{1,0:T(4,128)S(1)} copy-done((f32[4,384]{1,0:T(4,128)S(1)}, f32[4,384]{1,0:T(4,128)}, u32[]{:S(2)}) %copy-start.4) | copy-done | bytes 6168
  12.5 0.0 copy-start.5
  12.5 0.7 %copy-done.5 = f32[4,384]{1,0:T(4,128)S(1)} copy-done((f32[4,384]{1,0:T(4,128)S(1)}, f32[4,384]{1,0:T(4,128)}, u32[]{:S(2)}) %copy-start.5) | copy-done | bytes 6168
  13.2 0.0 copy-start.6
  13.2 0.7 copy-done.6
  13.8 0.0 copy-start.7
  13.8 0.7 copy-done.7
  14.5 0.0 copy-start.8
  14.5 0.7 copy-done.8
  15.1 1.7 %begin_0.1 = (f32[4,384]{1,0:T(4,128)S(1)}, bf16[1168,128]{1,0:T(8,128)(2,1)}) custom-call(f32[12]{0:T(128)S(1)} %copy-done.8, s32[2]{0:T(128)S(1)} %copy-done.7, s32[8]{0:T(128)S(1)} %copy-done.6, f32[4,384]{1,0:T(4,128)S(1)} %copy-done.3, f32[4,384]{1,0:T(4,128)S(1)} %copy-done.4, ...), custom_call_target="tpu_custom_call", output_to_operand_aliasing={{0}: (8, {}), {1}: (9, {})} | custom-call | flops 1358954496 | bytes 2097152 | tf_op jit(solution)/shard_map/begin_0/pallas_call | solution.py:605
  16.8 0.7 %collective-permute-start = (bf16[1168,128]{1,0:T(8,128)(2,1)}, bf16[1168,128]{1,0:T(8,128)(2,1)S(1)}, u32[]{:S(2)}, u32[]{:S(2)}) collective-permute-start(bf16[1168,128]{1,0:T(8,128)(2,1)} %get-tuple-element.77), channel_id=1, source_target_pairs={{0,1},{4,5},{8,9},{12,13},{16,17},{20,21},{24,25},{28,29}} | collective-permute-start | bytes 897032 | tf_op jit(solution)/shard_map/ppermute | solution.py:677
  17.6 0.0 copy-start.1
  17.6 0.8 %collective-permute-start.3 = (bf16[1168,128]{1,0:T(8,128)(2,1)S(1)}, bf16[1168,128]{1,0:T(8,128)(2,1)S(1)}, u32[]{:S(2)}, u32[]{:S(2)}) collective-permute-start(bf16[1168,128]{1,0:T(8,128)(2,1)S(1)} %get-tuple-element.58), channel_id=1, source_target_pairs={{0,1},{4,5},{8,9},{12,13},{16,17},{20,21},{24,25},{28,29}} | collective-permute-start | bytes 897032 | tf_op jit(solution)/shard_map/ppermute | solution.py:677
  18.4 1.5 %prepare.1 = (bf16[4,384,384]{2,1,0:T(8,128)(2,1)S(1)}, f32[9,8,384]{2,1,0:T(8,128)S(1)}, bf16[4,384,384]{2,1,0:T(8,128)(2,1)S(1)}, f32[9,8,384]{2,1,0:T(8,128)S(1)}) custom-call(f32[12]{0:T(128)S(1)} %copy-done.8, s32[2]{0:T(128)S(1)} %copy-done.7, s32[8]{0:T(128)S(1)} %copy-done.6, f32[4,384]{1,0:T(4,128)S(1)} %copy-done.3, f32[4,384]{1,0:T(4,128)S(1)} %copy-done.4, ...), custom_call_target="tpu_custom_call" | custom-call | flops 28311552 | bytes 65536 | tf_op jit(solution)/shard_map/prepare/pallas_call | solution.py:605
  19.9 0.0 copy-done.1
  20.0 2.9 %local_011.1 = (f32[1536,128]{1,0:T(8,128)S(1)}, f32[4,384]{1,0:T(4,128)S(1)}) custom-call(bf16[4,384,384]{2,1,0:T(8,128)(2,1)S(1)} %get-tuple-element.67.refs_0_, bf16[4,384,384]{2,1,0:T(8,128)(2,1)S(1)} %get-tuple-element.68.refs_1_, f32[9,8,384]{2,1,0:T(8,128)S(1)} %get-tuple-element.69.refs_2_.refs_0_, f32[9,8,384]{2,1,0:T(8,128)S(1)} %copy-done.1), custom_call_target="tpu_custom_call" | custom-call | flops 28311552 | bytes 65536 | tf_op jit(solution)/shard_map/local_011/pallas_call | solution.py:605
  22.8 2.3 %carriers_0.1 = (bf16[1536,768]{1,0:T(8,128)(2,1)S(1)}, bf16[768,768]{1,0:T(8,128)(2,1)S(1)}) custom-call(bf16[4,384,384]{2,1,0:T(8,128)(2,1)S(1)} %get-tuple-element.67.refs_0_, bf16[4,384,384]{2,1,0:T(8,128)(2,1)S(1)} %get-tuple-element.68.refs_1_, f32[9,8,384]{2,1,0:T(8,128)S(1)} %get-tuple-element.69.refs_2_.refs_0_, f32[9,8,384]{2,1,0:T(8,128)S(1)} %copy-done.1), custom_call_target="tpu_custom_call" | custom-call | flops 28311552 | bytes 65536 | tf_op jit(solution)/shard_map/carriers_0/pallas_call | solution.py:605
  25.2 2.8 %local_110.1 = (f32[1536,128]{1,0:T(8,128)S(1)}, f32[4,384]{1,0:T(4,128)S(1)}) custom-call(bf16[4,384,384]{2,1,0:T(8,128)(2,1)S(1)} %get-tuple-element.87.refs_0_, f32[9,8,384]{2,1,0:T(8,128)S(1)} %get-tuple-element.85.refs_1_.refs_0_), custom_call_target="tpu_custom_call" | custom-call | flops 28311552 | bytes 65536 | tf_op jit(solution)/shard_map/local_110/pallas_call | solution.py:605
  28.0 0.0 collective-permute-done.refs_3_.refs_4_
  28.0 0.7 %collective-permute-start.1 = (bf16[1168,128]{1,0:T(8,128)(2,1)S(1)}, bf16[1168,128]{1,0:T(8,128)(2,1)S(1)}, u32[]{:S(2)}, u32[]{:S(2)}) collective-permute-start(bf16[1168,128]{1,0:T(8,128)(2,1)S(1)} %pass_1_0.1), channel_id=1, source_target_pairs={{1,2},{5,6},{9,10},{13,14},{17,18},{21,22},{25,26},{29,30}} | collective-permute-start | bytes 897032 | tf_op jit(solution)/shard_map/ppermute | solution.py:677
  28.7 2.1 %carriers_1.1 = (bf16[1536,768]{1,0:T(8,128)(2,1)S(1)}, bf16[768,768]{1,0:T(8,128)(2,1)S(1)}) custom-call(bf16[4,384,384]{2,1,0:T(8,128)(2,1)S(1)} %get-tuple-element.87.refs_0_, f32[9,8,384]{2,1,0:T(8,128)S(1)} %get-tuple-element.85.refs_1_.refs_0_), custom_call_target="tpu_custom_call" | custom-call | flops 28311552 | bytes 65536 | tf_op jit(solution)/shard_map/carriers_1/pallas_call | solution.py:605
  30.8 0.0 collective-permute-done.3.refs_4_
  30.8 0.7 %collective-permute-start.4 = (bf16[1168,128]{1,0:T(8,128)(2,1)S(1)}, bf16[1168,128]{1,0:T(8,128)(2,1)S(1)}, u32[]{:S(2)}, u32[]{:S(2)}) collective-permute-start(bf16[1168,128]{1,0:T(8,128)(2,1)S(1)} %pass_1_1.1), channel_id=1, source_target_pairs={{1,2},{5,6},{9,10},{13,14},{17,18},{21,22},{25,26},{29,30}} | collective-permute-start | bytes 897032 | tf_op jit(solution)/shard_map/ppermute | solution.py:677
  31.5 0.0 collective-permute-done.1.refs_3_.refs_5_
  31.5 0.0 copy-start.9
  31.6 1.4 %collective-permute-start.2 = (bf16[1168,128]{1,0:T(8,128)(2,1)S(1)}, bf16[1168,128]{1,0:T(8,128)(2,1)S(1)}, u32[]{:S(2)}, u32[]{:S(2)}) collective-permute-start(bf16[1168,128]{1,0:T(8,128)(2,1)S(1)} %pass_2_0.1), channel_id=1, source_target_pairs={{2,3},{6,7},{10,11},{14,15},{18,19},{22,23},{26,27},{30,31}} | collective-permute-start | bytes 897032 | tf_op jit(solution)/shard_map/ppermute | solution.py:677
  33.0 0.0 collective-permute-done.4.refs_4_.refs_5_
  33.0 0.2 pass_2_1.1
  33.2 1.3 %collective-permute-start.5 = (bf16[1168,128]{1,0:T(8,128)(2,1)S(1)}, bf16[1168,128]{1,0:T(8,128)(2,1)S(1)}, u32[]{:S(2)}, u32[]{:S(2)}) collective-permute-start(bf16[1168,128]{1,0:T(8,128)(2,1)S(1)} %pass_2_1.1), channel_id=1, source_target_pairs={{2,3},{6,7},{10,11},{14,15},{18,19},{22,23},{26,27},{30,31}} | collective-permute-start | bytes 897032 | tf_op jit(solution)/shard_map/ppermute | solution.py:677
  34.5 0.0 copy-done.9
  34.6 0.2 split_inverse.1
  34.8 10.2 %collective-permute-done.2.refs_6_ = bf16[1168,128]{1,0:T(8,128)(2,1)S(1)} collective-permute-done((bf16[1168,128]{1,0:T(8,128)(2,1)S(1)}, bf16[1168,128]{1,0:T(8,128)(2,1)S(1)}, u32[]{:S(2)}, u32[]{:S(2)}) %collective-permute-start.2) | collective-permute-done | bytes 299040 | tf_op jit(solution)/shard_map/ppermute | solution.py:677
  45.0 2.5 %density_0.1.refs_3_ = f32[4,384]{1,0:T(4,128)S(1)} custom-call(bf16[1536,768]{1,0:T(8,128)(2,1)S(1)} %get-tuple-element.75.refs_1_.carriers, f32[9,8,384]{2,1,0:T(8,128)S(1)} %get-tuple-element.69.refs_2_.refs_0_, f32[9,8,384]{2,1,0:T(8,128)S(1)} %copy-done.1, f32[4,384]{1,0:T(4,128)S(1)} %get-tuple-element.71.refs_2_, ...), custom_call_target="tpu_custom_call", output_to_operand_aliasing={{}: (4, {})} | custom-call | flops 1811939328 | bytes 2097152 | tf_op jit(solution)/shard_map/density_0/pallas_call | solution.py:605
  47.4 5.0 %collective-permute-done.5.refs_6_ = bf16[1168,128]{1,0:T(8,128)(2,1)S(1)} collective-permute-done((bf16[1168,128]{1,0:T(8,128)(2,1)S(1)}, bf16[1168,128]{1,0:T(8,128)(2,1)S(1)}, u32[]{:S(2)}, u32[]{:S(2)}) %collective-permute-start.5) | collective-permute-done | bytes 299040 | tf_op jit(solution)/shard_map/ppermute | solution.py:677
  52.4 2.5 %density_1.1 = f32[4,384]{1,0:T(4,128)S(1)} custom-call(bf16[1536,768]{1,0:T(8,128)(2,1)S(1)} %get-tuple-element.83.refs_2_.carriers, f32[9,8,384]{2,1,0:T(8,128)S(1)} %get-tuple-element.85.refs_1_.refs_0_, f32[4,384]{1,0:T(4,128)S(1)} %get-tuple-element.86.refs_1_, f32[4,384]{1,0:T(4,128)S(1)} %get-tuple-element.88.refs_2_, ...), custom_call_target="tpu_custom_call", output_to_operand_aliasing={{}: (4, {})} | custom-call | flops 1811939328 | bytes 2097152 | tf_op jit(solution)/shard_map/density_1/pallas_call | solution.py:605
  54.9 9.9 %all_to_all.14.gathered = f32[8,4,384]{2,1,0:T(4,128)S(1)} all-to-all(f32[8,4,384]{2,1,0:T(4,128)S(1)} %broadcast_in_dim.2), channel_id=1, replica_groups=mesh['kt'=8,'en'=4] {'kt'}, dimensions={0} | all-to-all | bytes 98304 | tf_op jit(solution)/shard_map/all_to_all | solution.py:651
  64.9 0.0 copy-done.2
  64.9 0.9 %last.1 = (f32[4,384]{1,0:T(4,128)}, f32[4,384]{1,0:T(4,128)}) custom-call(f32[8,4,384]{2,1,0:T(4,128)S(1)} %all_to_all.14.gathered, f32[4,384]{1,0:T(4,128)S(1)} %copy-done.2, bf16[384,384]{1,0:T(8,128)(2,1)S(1)} %get-tuple-element.97.high, bf16[384,384]{1,0:T(8,128)(2,1)S(1)} %get-tuple-element.98.middle, bf16[384,384]{1,0:T(8,128)(2,1)S(1)} %get-tuple-element.99.low), custom_call_target="tpu_custom_call" | custom-call | flops 113246208 | bytes 2097152 | tf_op jit(solution)/shard_map/last/pallas_call | solution.py:605
  (7 shorter events, 0.1 us)
Async XLA Ops:
  1.9 8.5 %all-to-all-start = ((s32[8,1,1]{2,1,0:T(1,128)}), s32[8,1,1]{2,1,0:T(1,128)}, u32[]{:S(2)}, u32[]{:S(2)}) async-start(s32[8,1,1]{2,1,0:T(1,128)} %tile.10), calls=%async_computation | async-start | bytes 8192 | tf_op jit(solution)/shard_map/all_to_all | solution.py:688
  5.7 6.0 %copy-start.3 = (f32[4,384]{1,0:T(4,128)S(1)}, f32[4,384]{1,0:T(4,128)}, u32[]{:S(2)}) copy-start(f32[4,384]{1,0:T(4,128)} %onsite.4) | copy-start | bytes 18436
  8.2 0.6 copy-start
  11.8 0.7 %copy-start.4 = (f32[4,384]{1,0:T(4,128)S(1)}, f32[4,384]{1,0:T(4,128)}, u32[]{:S(2)}) copy-start(f32[4,384]{1,0:T(4,128)} %hopping.4) | copy-start | bytes 18436
  12.5 0.7 %copy-start.5 = (f32[4,384]{1,0:T(4,128)S(1)}, f32[4,384]{1,0:T(4,128)}, u32[]{:S(2)}) copy-start(f32[4,384]{1,0:T(4,128)} %potential.4) | copy-start | bytes 18436
  13.2 0.7 copy-start.6
  13.8 0.7 copy-start.7
  14.5 0.7 copy-start.8
  16.8 11.1 %collective-permute-start = (bf16[1168,128]{1,0:T(8,128)(2,1)}, bf16[1168,128]{1,0:T(8,128)(2,1)S(1)}, u32[]{:S(2)}, u32[]{:S(2)}) collective-permute-start(bf16[1168,128]{1,0:T(8,128)(2,1)} %get-tuple-element.77), channel_id=1, source_target_pairs={{0,1},{4,5},{8,9},{12,13},{16,17},{20,21},{24,25},{28,29}} | collective-permute-start | bytes 897032 | tf_op jit(solution)/shard_map/ppermute | solution.py:677
  17.6 2.4 %copy-start.1 = (f32[9,8,384]{2,1,0:T(8,128)S(1)}, f32[9,8,384]{2,1,0:T(8,128)}, u32[]{:S(2)}) copy-start(f32[9,8,384]{2,1,0:T(8,128)} %copy-done) | copy-start | bytes 331780
  17.6 13.2 %collective-permute-start.3 = (bf16[1168,128]{1,0:T(8,128)(2,1)S(1)}, bf16[1168,128]{1,0:T(8,128)(2,1)S(1)}, u32[]{:S(2)}, u32[]{:S(2)}) collective-permute-start(bf16[1168,128]{1,0:T(8,128)(2,1)S(1)} %get-tuple-element.58), channel_id=1, source_target_pairs={{0,1},{4,5},{8,9},{12,13},{16,17},{20,21},{24,25},{28,29}} | collective-permute-start | bytes 897032 | tf_op jit(solution)/shard_map/ppermute | solution.py:677
  28.0 3.5 %collective-permute-start.1 = (bf16[1168,128]{1,0:T(8,128)(2,1)S(1)}, bf16[1168,128]{1,0:T(8,128)(2,1)S(1)}, u32[]{:S(2)}, u32[]{:S(2)}) collective-permute-start(bf16[1168,128]{1,0:T(8,128)(2,1)S(1)} %pass_1_0.1), channel_id=1, source_target_pairs={{1,2},{5,6},{9,10},{13,14},{17,18},{21,22},{25,26},{29,30}} | collective-permute-start | bytes 897032 | tf_op jit(solution)/shard_map/ppermute | solution.py:677
  30.8 2.2 %collective-permute-start.4 = (bf16[1168,128]{1,0:T(8,128)(2,1)S(1)}, bf16[1168,128]{1,0:T(8,128)(2,1)S(1)}, u32[]{:S(2)}, u32[]{:S(2)}) collective-permute-start(bf16[1168,128]{1,0:T(8,128)(2,1)S(1)} %pass_1_1.1), channel_id=1, source_target_pairs={{1,2},{5,6},{9,10},{13,14},{17,18},{21,22},{25,26},{29,30}} | collective-permute-start | bytes 897032 | tf_op jit(solution)/shard_map/ppermute | solution.py:677
  31.5 3.0 %copy-start.9 = (f32[384,384]{1,0:T(8,128)S(1)}, f32[384,384]{1,0:T(8,128)}, u32[]{:S(2)}) copy-start(f32[384,384]{1,0:T(8,128)} %inverse) | copy-start | bytes 1769476
  31.6 13.4 %collective-permute-start.2 = (bf16[1168,128]{1,0:T(8,128)(2,1)S(1)}, bf16[1168,128]{1,0:T(8,128)(2,1)S(1)}, u32[]{:S(2)}, u32[]{:S(2)}) collective-permute-start(bf16[1168,128]{1,0:T(8,128)(2,1)S(1)} %pass_2_0.1), channel_id=1, source_target_pairs={{2,3},{6,7},{10,11},{14,15},{18,19},{22,23},{26,27},{30,31}} | collective-permute-start | bytes 897032 | tf_op jit(solution)/shard_map/ppermute | solution.py:677
  33.2 19.2 %collective-permute-start.5 = (bf16[1168,128]{1,0:T(8,128)(2,1)S(1)}, bf16[1168,128]{1,0:T(8,128)(2,1)S(1)}, u32[]{:S(2)}, u32[]{:S(2)}) collective-permute-start(bf16[1168,128]{1,0:T(8,128)(2,1)S(1)} %pass_2_1.1), channel_id=1, source_target_pairs={{2,3},{6,7},{10,11},{14,15},{18,19},{22,23},{26,27},{30,31}} | collective-permute-start | bytes 897032 | tf_op jit(solution)/shard_map/ppermute | solution.py:677
  52.4 12.4 %copy-start.2 = (f32[4,384]{1,0:T(4,128)S(1)}, f32[4,384]{1,0:T(4,128)}, u32[]{:S(2)}) copy-start(f32[4,384]{1,0:T(4,128)} %doping.1) | copy-start | bytes 18436

commit v8 on v7

--- a/solution.py
+++ b/solution.py
@@ -291,7 +291,7 @@
 def lead_kernel(
     impulse_count,
     constants_hbm, contact_hbm, onsite_hbm, hopping_hbm, potential_hbm, base_hbm, wave_hbm,
-    sent, density, base, wave, couple_0, entry_0,
+    sent, density, base, wave,
     constants, contact, tables, g, left, small_sem, table_sem, couple_sem,
 ):
     slabs, orbitals = onsite_hbm.shape
@@ -360,13 +360,6 @@
             for copy in couple_copies[s]:
                 copy.wait()
 
-        @pl.when(takes_first_levels())
-        def _():
-            cosine, weight, inv_real, inv_imag = first_level_amounts()
-            prepare(
-                cosine, weight, inv_real, inv_imag, base, wave, couple_0, entry_0
-            )
-
 
 def with_scalars(refs, scratch, sem):
     copies = [
@@ -453,11 +446,7 @@
         with_scalars(
             (constants_ref, contact_ref, counts_ref), (constants, contact, counts), scalar_sem
         )
-
-        @pl.when(jnp.logical_not(takes_first_levels()))
-        def _():
-            prepare_slot(0, (couple_0, entry_0))
-
+        prepare_slot(0, (couple_0, entry_0))
         prepare_slot(1, (couple_1, entry_1))
 
 
@@ -688,9 +677,9 @@
     counts_all = lax.all_to_all(jnp.tile(counts, kt_size), "kt", 0, 0, tiled=True)
     given = (constants, contact_slabs, onsite, hopping, potential_in, couple_base, couple_wave)
     pinned = [pltpu.with_memory_space_constraint(t, pltpu.HBM) for t in given]
-    block, density, *rest = vmem_call(
+    block, density, *loaded = vmem_call(
         functools.partial(lead_kernel, impulse_count),
-        (block_shape, density_shape) + (couple_shape,) * 3 + (entry_shape,),
+        (block_shape, density_shape, couple_shape, couple_shape),
         pinned,
         [hbm] * len(pinned),
         [
@@ -707,7 +696,6 @@
         "lead",
         3 * flops,
     )
-    loaded, made_first = rest[:2], rest[2:]
     block, counts_all = lax.optimization_barrier((block, counts_all))
     small = (constants, contact_slabs, counts_all, onsite, hopping, potential_in)
 
@@ -746,7 +734,7 @@
         flops // 16,
         2**16,
     )
-    made = [list(zip(made[:2], made_first)), [(one,) for one in made[2:]]]
+    made = [[(one,) for one in made[:2]], [(one,) for one in made[2:]]]
 
     carriers_shape = jax.ShapeDtypeStruct((slabs * orbitals, 2 * orbitals), BF16)
     double_shape = jax.ShapeDtypeStruct((2 * orbitals, 2 * orbitals), BF16)

time: 66.2 us -> 57.8 us (0.87)
  local copies, waits for them, and re-layouts: 4.61 us -> 0.65 us
  blocking collectives: 9.95 us -> 7.31 us
  Pallas kernels: 22.1 us -> 19.5 us
  waiting for transfers between devices: 16.7 us -> 19 us
  other arithmetic: 1.43 us -> 0.23 us
    unnamed x20 -> x14, local copies, waits for them, and re-layouts: 4 us -> 0.04 us
    all_to_all x1, blocking collectives: 9.95 us -> 7.31 us  [gather_over(): return lax.all_to_all(copies, axis, 0, 0)]
    pallas_call x17, Pallas kernels: 22.1 us -> 19.5 us  [vmem_call(): pl.pallas_call(kernel, out_shape=tuple(outs), in_specs=in_specs, out_spec...]
    all_to_all x1, waiting for transfers between devices: 1.47 us -> 2.75 us  [body(): lax.all_to_all(jnp.tile(counts, kt_size), 'kt', 0, 0, tiled=True)]
    all_to_all x1, other arithmetic: 1.43 us -> 0.23 us  [body(): lax.all_to_all(jnp.tile(counts, kt_size), 'kt', 0, 0, tiled=True)]
    ppermute x6, waiting for transfers between devices: 15.2 us -> 16.3 us  [forward(): return lax.ppermute(block, 'en', [(stage, stage + 1)])]
  transfers between devices with their start and end apart: 7 -> 7, of which waited for: 3 -> 3; matrix products, arithmetic and copies ran while one was open for 0% -> 0% of each run, Pallas kernels for 26% -> 28%
where the time goes in v8:
time: 57.8 us; the launch traced here: 57.5 us
  Pallas kernels  19.5 us (34%)
  waiting for transfers between devices  19 us (33%)
  starting transfers between devices  9.16 us (16%)
  blocking collectives  7.31 us (13%)
  between operations  1.56 us (3%)
  local copies, waits for them, and re-layouts  0.65 us (1%)
    pallas_call x17, Pallas kernels, vmem_call(): pl.pallas_call(kernel, out_shape=tuple(outs), in_specs=in_specs, out_spec...  19.5 us
    ppermute x6, waiting for transfers between devices, forward(): return lax.ppermute(block, 'en', [(stage, stage + 1)])  16.3 us
    all_to_all x1, blocking collectives, gather_over(): return lax.all_to_all(copies, axis, 0, 0)  7.31 us
    ppermute x6, starting transfers between devices, forward(): return lax.ppermute(block, 'en', [(stage, stage + 1)])  5.44 us
    all_to_all x1, starting transfers between devices, body(): lax.all_to_all(jnp.tile(counts, kt_size), 'kt', 0, 0, tiled=True)  3.72 us
    all_to_all x1, waiting for transfers between devices, body(): lax.all_to_all(jnp.tile(counts, kt_size), 'kt', 0, 0, tiled=True)  2.75 us
  transfers between devices with their start and end apart: 7, of which 3 were waited for; matrix products, arithmetic and copies ran while one was open for 0% of the time, Pallas kernels for 28%

profile of v8, /device:TPU:24, one launch (start us, length us, event | category | flops | bytes accessed | tf_op | source)
XLA Modules:
  0.0 57.5 jit_solution(17990098534193894829)
XLA Ops:
  1.3 0.6 %tile.10 = s32[8,1,1]{2,1,0:T(1,128)} broadcast(s32[]{:T(128)} %bitcast.1), dimensions={} | broadcast | bytes 36 | tf_op jit(solution)/shard_map/tile | solution.py:677
  1.9 3.7 %all-to-all-start = ((s32[8,1,1]{2,1,0:T(1,128)}), s32[8,1,1]{2,1,0:T(1,128)S(1)}, u32[]{:S(2)}, u32[]{:S(2)}) async-start(s32[8,1,1]{2,1,0:T(1,128)} %tile.10), calls=%async_computation | async-start | bytes 8192 | tf_op jit(solution)/shard_map/all_to_all | solution.py:677
  5.6 0.0 copy-start.1
  5.6 0.0 copy-start.2
  5.6 0.0 copy-start.3
  5.6 0.0 copy-start.4
  5.6 0.0 copy-start.5
  5.6 1.8 %lead.1 = (bf16[1168,128]{1,0:T(8,128)(2,1)S(1)}, f32[4,384]{1,0:T(4,128)S(1)}, bf16[4,384,384]{2,1,0:T(8,128)(2,1)S(1)}, bf16[4,384,384]{2,1,0:T(8,128)(2,1)S(1)}) custom-call(f32[12]{0:T(128)} %constant.2.clone.constants_hbm.constants_ref, s32[2]{0:T(128)} %contact_ref.4, f32[4,384]{1,0:T(4,128)} %onsite.4, f32[4,384]{1,0:T(4,128)} %hopping.4, ...), custom_call_target="tpu_custom_call" | custom-call | flops 1358954496 | bytes 2097152 | tf_op jit(solution)/shard_map/lead/pallas_call | solution.py:594
  7.4 2.8 %all-to-all-done = s32[8,1,1]{2,1,0:T(1,128)S(1)} async-done(((s32[8,1,1]{2,1,0:T(1,128)}), s32[8,1,1]{2,1,0:T(1,128)S(1)}, u32[]{:S(2)}, u32[]{:S(2)}) %all-to-all-start) | async-done | bytes 64 | tf_op jit(solution)/shard_map/all_to_all | solution.py:677
  10.2 0.2 reduce.counts_ref
  10.4 0.0 copy-done.1
  10.4 0.0 copy-done.2
  10.4 0.0 copy-done.3
  10.4 0.0 copy-done.4
  10.4 0.0 copy-done.5
  10.5 0.1 begin_0.1
  10.5 0.7 %collective-permute-start = (bf16[1168,128]{1,0:T(8,128)(2,1)S(1)}, bf16[1168,128]{1,0:T(8,128)(2,1)S(1)}, u32[]{:S(2)}, u32[]{:S(2)}) collective-permute-start(bf16[1168,128]{1,0:T(8,128)(2,1)S(1)} %get-tuple-element.73), channel_id=1, source_target_pairs={{0,1},{4,5},{8,9},{12,13},{16,17},{20,21},{24,25},{28,29}} | collective-permute-start | bytes 897032 | tf_op jit(solution)/shard_map/ppermute | solution.py:666
  11.3 0.7 %collective-permute-start.3 = (bf16[1168,128]{1,0:T(8,128)(2,1)S(1)}, bf16[1168,128]{1,0:T(8,128)(2,1)S(1)}, u32[]{:S(2)}, u32[]{:S(2)}) collective-permute-start(bf16[1168,128]{1,0:T(8,128)(2,1)S(1)} %get-tuple-element.56), channel_id=1, source_target_pairs={{0,1},{4,5},{8,9},{12,13},{16,17},{20,21},{24,25},{28,29}} | collective-permute-start | bytes 897032 | tf_op jit(solution)/shard_map/ppermute | solution.py:666
  11.9 1.5 %prepare.1 = (bf16[4,384,384]{2,1,0:T(8,128)(2,1)S(1)}, f32[9,8,384]{2,1,0:T(8,128)S(1)}, bf16[4,384,384]{2,1,0:T(8,128)(2,1)S(1)}, f32[9,8,384]{2,1,0:T(8,128)S(1)}) custom-call(f32[12]{0:T(128)S(1)} %copy-done.5, s32[2]{0:T(128)S(1)} %copy-done.4, s32[8]{0:T(128)S(1)} %reduce.counts_ref, f32[4,384]{1,0:T(4,128)S(1)} %copy-done.1, f32[4,384]{1,0:T(4,128)S(1)} %copy-done.2, ...), custom_call_target="tpu_custom_call" | custom-call | flops 28311552 | bytes 65536 | tf_op jit(solution)/shard_map/prepare/pallas_call | solution.py:594
  13.5 2.8 %local_011.1 = (f32[1536,128]{1,0:T(8,128)S(1)}, f32[4,384]{1,0:T(4,128)S(1)}) custom-call(bf16[4,384,384]{2,1,0:T(8,128)(2,1)S(1)} %get-tuple-element.65.refs_0_, f32[9,8,384]{2,1,0:T(8,128)S(1)} %get-tuple-element.66.refs_1_.refs_0_), custom_call_target="tpu_custom_call" | custom-call | flops 28311552 | bytes 65536 | tf_op jit(solution)/shard_map/local_011/pallas_call | solution.py:594
  16.3 2.2 %carriers_0.1 = (bf16[1536,768]{1,0:T(8,128)(2,1)S(1)}, bf16[768,768]{1,0:T(8,128)(2,1)S(1)}) custom-call(bf16[4,384,384]{2,1,0:T(8,128)(2,1)S(1)} %get-tuple-element.65.refs_0_, f32[9,8,384]{2,1,0:T(8,128)S(1)} %get-tuple-element.66.refs_1_.refs_0_), custom_call_target="tpu_custom_call" | custom-call | flops 28311552 | bytes 65536 | tf_op jit(solution)/shard_map/carriers_0/pallas_call | solution.py:594
  18.6 2.8 %local_110.1 = (f32[1536,128]{1,0:T(8,128)S(1)}, f32[4,384]{1,0:T(4,128)S(1)}) custom-call(bf16[4,384,384]{2,1,0:T(8,128)(2,1)S(1)} %get-tuple-element.83.refs_0_, f32[9,8,384]{2,1,0:T(8,128)S(1)} %get-tuple-element.81.refs_1_.refs_0_), custom_call_target="tpu_custom_call" | custom-call | flops 28311552 | bytes 65536 | tf_op jit(solution)/shard_map/local_110/pallas_call | solution.py:594
  21.4 0.0 collective-permute-done.refs_3_
  21.4 0.7 %collective-permute-start.1 = (bf16[1168,128]{1,0:T(8,128)(2,1)S(1)}, bf16[1168,128]{1,0:T(8,128)(2,1)S(1)}, u32[]{:S(2)}, u32[]{:S(2)}) collective-permute-start(bf16[1168,128]{1,0:T(8,128)(2,1)S(1)} %pass_1_0.1), channel_id=1, source_target_pairs={{1,2},{5,6},{9,10},{13,14},{17,18},{21,22},{25,26},{29,30}} | collective-permute-start | bytes 897032 | tf_op jit(solution)/shard_map/ppermute | solution.py:666
  22.1 2.1 %carriers_1.1 = (bf16[1536,768]{1,0:T(8,128)(2,1)S(1)}, bf16[768,768]{1,0:T(8,128)(2,1)S(1)}) custom-call(bf16[4,384,384]{2,1,0:T(8,128)(2,1)S(1)} %get-tuple-element.83.refs_0_, f32[9,8,384]{2,1,0:T(8,128)S(1)} %get-tuple-element.81.refs_1_.refs_0_), custom_call_target="tpu_custom_call" | custom-call | flops 28311552 | bytes 65536 | tf_op jit(solution)/shard_map/carriers_1/pallas_call | solution.py:594
  24.2 0.0 collective-permute-done.3.refs_4_
  24.2 0.7 %collective-permute-start.4 = (bf16[1168,128]{1,0:T(8,128)(2,1)S(1)}, bf16[1168,128]{1,0:T(8,128)(2,1)S(1)}, u32[]{:S(2)}, u32[]{:S(2)}) collective-permute-start(bf16[1168,128]{1,0:T(8,128)(2,1)S(1)} %pass_1_1.1), channel_id=1, source_target_pairs={{1,2},{5,6},{9,10},{13,14},{17,18},{21,22},{25,26},{29,30}} | collective-permute-start | bytes 897032 | tf_op jit(solution)/shard_map/ppermute | solution.py:666
  24.9 0.0 collective-permute-done.1.refs_3_.refs_4_
  24.9 0.0 copy-start.6
  24.9 1.4 %collective-permute-start.2 = (bf16[1168,128]{1,0:T(8,128)(2,1)S(1)}, bf16[1168,128]{1,0:T(8,128)(2,1)S(1)}, u32[]{:S(2)}, u32[]{:S(2)}) collective-permute-start(bf16[1168,128]{1,0:T(8,128)(2,1)S(1)} %pass_2_0.1), channel_id=1, source_target_pairs={{2,3},{6,7},{10,11},{14,15},{18,19},{22,23},{26,27},{30,31}} | collective-permute-start | bytes 897032 | tf_op jit(solution)/shard_map/ppermute | solution.py:666
  26.4 0.0 collective-permute-done.4.refs_4_.refs_5_
  26.4 0.2 pass_2_1.1
  26.6 1.3 %collective-permute-start.5 = (bf16[1168,128]{1,0:T(8,128)(2,1)S(1)}, bf16[1168,128]{1,0:T(8,128)(2,1)S(1)}, u32[]{:S(2)}, u32[]{:S(2)}) collective-permute-start(bf16[1168,128]{1,0:T(8,128)(2,1)S(1)} %pass_2_1.1), channel_id=1, source_target_pairs={{2,3},{6,7},{10,11},{14,15},{18,19},{22,23},{26,27},{30,31}} | collective-permute-start | bytes 897032 | tf_op jit(solution)/shard_map/ppermute | solution.py:666
  27.9 0.0 copy-done.6
  27.9 0.2 split_inverse.1
  28.2 10.2 %collective-permute-done.2.refs_5_ = bf16[1168,128]{1,0:T(8,128)(2,1)S(1)} collective-permute-done((bf16[1168,128]{1,0:T(8,128)(2,1)S(1)}, bf16[1168,128]{1,0:T(8,128)(2,1)S(1)}, u32[]{:S(2)}, u32[]{:S(2)}) %collective-permute-start.2) | collective-permute-done | bytes 299040 | tf_op jit(solution)/shard_map/ppermute | solution.py:666
  38.4 2.4 %density_0.1.refs_3_ = f32[4,384]{1,0:T(4,128)S(1)} custom-call(bf16[1536,768]{1,0:T(8,128)(2,1)S(1)} %get-tuple-element.71.refs_1_.carriers, f32[9,8,384]{2,1,0:T(8,128)S(1)} %get-tuple-element.66.refs_1_.refs_0_, f32[4,384]{1,0:T(4,128)S(1)} %get-tuple-element.67.refs_1_, f32[4,384]{1,0:T(4,128)S(1)} %get-tuple-element.85.refs_2_, ...), custom_call_target="tpu_custom_call", output_to_operand_aliasing={{}: (3, {})} | custom-call | flops 1811939328 | bytes 2097152 | tf_op jit(solution)/shard_map/density_0/pallas_call | solution.py:594
  40.8 6.0 %collective-permute-done.5.refs_6_ = bf16[1168,128]{1,0:T(8,128)(2,1)S(1)} collective-permute-done((bf16[1168,128]{1,0:T(8,128)(2,1)S(1)}, bf16[1168,128]{1,0:T(8,128)(2,1)S(1)}, u32[]{:S(2)}, u32[]{:S(2)}) %collective-permute-start.5) | collective-permute-done | bytes 299040 | tf_op jit(solution)/shard_map/ppermute | solution.py:666
  46.9 0.0 copy-start
  46.9 2.4 %density_1.1 = f32[4,384]{1,0:T(4,128)S(1)} custom-call(bf16[1536,768]{1,0:T(8,128)(2,1)S(1)} %get-tuple-element.79.refs_2_.carriers, f32[9,8,384]{2,1,0:T(8,128)S(1)} %get-tuple-element.81.refs_1_.refs_0_, f32[4,384]{1,0:T(4,128)S(1)} %get-tuple-element.82.refs_1_, f32[4,384]{1,0:T(4,128)S(1)} %get-tuple-element.84.refs_2_, ...), custom_call_target="tpu_custom_call", output_to_operand_aliasing={{}: (4, {})} | custom-call | flops 1811939328 | bytes 2097152 | tf_op jit(solution)/shard_map/density_1/pallas_call | solution.py:594
  49.3 7.3 %all_to_all.14.gathered = f32[8,4,384]{2,1,0:T(4,128)S(1)} all-to-all(f32[8,4,384]{2,1,0:T(4,128)S(1)} %broadcast_in_dim.2), channel_id=1, replica_groups=mesh['kt'=8,'en'=4] {'kt'}, dimensions={0} | all-to-all | bytes 98304 | tf_op jit(solution)/shard_map/all_to_all | solution.py:640
  56.6 0.0 copy-done
  56.6 0.9 %last.1 = (f32[4,384]{1,0:T(4,128)}, f32[4,384]{1,0:T(4,128)}) custom-call(f32[8,4,384]{2,1,0:T(4,128)S(1)} %all_to_all.14.gathered, f32[4,384]{1,0:T(4,128)S(1)} %copy-done, bf16[384,384]{1,0:T(8,128)(2,1)S(1)} %get-tuple-element.93.high, bf16[384,384]{1,0:T(8,128)(2,1)S(1)} %get-tuple-element.94.middle, bf16[384,384]{1,0:T(8,128)(2,1)S(1)} %get-tuple-element.95.low), custom_call_target="tpu_custom_call" | custom-call | flops 113246208 | bytes 2097152 | tf_op jit(solution)/shard_map/last/pallas_call | solution.py:594
  (6 shorter events, 0.1 us)
Async XLA Ops:
  1.9 8.3 %all-to-all-start = ((s32[8,1,1]{2,1,0:T(1,128)}), s32[8,1,1]{2,1,0:T(1,128)S(1)}, u32[]{:S(2)}, u32[]{:S(2)}) async-start(s32[8,1,1]{2,1,0:T(1,128)} %tile.10), calls=%async_computation | async-start | bytes 8192 | tf_op jit(solution)/shard_map/all_to_all | solution.py:677
  5.6 4.8 %copy-start.1 = (f32[4,384]{1,0:T(4,128)S(1)}, f32[4,384]{1,0:T(4,128)}, u32[]{:S(2)}) copy-start(f32[4,384]{1,0:T(4,128)} %onsite.4) | copy-start | bytes 18436
  5.6 4.8 %copy-start.2 = (f32[4,384]{1,0:T(4,128)S(1)}, f32[4,384]{1,0:T(4,128)}, u32[]{:S(2)}) copy-start(f32[4,384]{1,0:T(4,128)} %hopping.4) | copy-start | bytes 18436
  5.6 4.8 %copy-start.3 = (f32[4,384]{1,0:T(4,128)S(1)}, f32[4,384]{1,0:T(4,128)}, u32[]{:S(2)}) copy-start(f32[4,384]{1,0:T(4,128)} %potential.4) | copy-start | bytes 18436
  5.6 4.8 %copy-start.4 = (s32[2]{0:T(128)S(1)}, s32[2]{0:T(128)}, u32[]{:S(2)}) copy-start(s32[2]{0:T(128)} %contact_ref.4) | copy-start | bytes 28
  5.6 4.8 %copy-start.5 = (f32[12]{0:T(128)S(1)}, f32[12]{0:T(128)}, u32[]{:S(2)}) copy-start(f32[12]{0:T(128)} %constant.2.clone.constants_hbm.constants_ref) | copy-start | bytes 148
  10.5 10.8 %collective-permute-start = (bf16[1168,128]{1,0:T(8,128)(2,1)S(1)}, bf16[1168,128]{1,0:T(8,128)(2,1)S(1)}, u32[]{:S(2)}, u32[]{:S(2)}) collective-permute-start(bf16[1168,128]{1,0:T(8,128)(2,1)S(1)} %get-tuple-element.73), channel_id=1, source_target_pairs={{0,1},{4,5},{8,9},{12,13},{16,17},{20,21},{24,25},{28,29}} | collective-permute-start | bytes 897032 | tf_op jit(solution)/shard_map/ppermute | solution.py:666
  11.3 12.9 %collective-permute-start.3 = (bf16[1168,128]{1,0:T(8,128)(2,1)S(1)}, bf16[1168,128]{1,0:T(8,128)(2,1)S(1)}, u32[]{:S(2)}, u32[]{:S(2)}) collective-permute-start(bf16[1168,128]{1,0:T(8,128)(2,1)S(1)} %get-tuple-element.56), channel_id=1, source_target_pairs={{0,1},{4,5},{8,9},{12,13},{16,17},{20,21},{24,25},{28,29}} | collective-permute-start | bytes 897032 | tf_op jit(solution)/shard_map/ppermute | solution.py:666
  21.4 3.5 %collective-permute-start.1 = (bf16[1168,128]{1,0:T(8,128)(2,1)S(1)}, bf16[1168,128]{1,0:T(8,128)(2,1)S(1)}, u32[]{:S(2)}, u32[]{:S(2)}) collective-permute-start(bf16[1168,128]{1,0:T(8,128)(2,1)S(1)} %pass_1_0.1), channel_id=1, source_target_pairs={{1,2},{5,6},{9,10},{13,14},{17,18},{21,22},{25,26},{29,30}} | collective-permute-start | bytes 897032 | tf_op jit(solution)/shard_map/ppermute | solution.py:666
  24.2 2.2 %collective-permute-start.4 = (bf16[1168,128]{1,0:T(8,128)(2,1)S(1)}, bf16[1168,128]{1,0:T(8,128)(2,1)S(1)}, u32[]{:S(2)}, u32[]{:S(2)}) collective-permute-start(bf16[1168,128]{1,0:T(8,128)(2,1)S(1)} %pass_1_1.1), channel_id=1, source_target_pairs={{1,2},{5,6},{9,10},{13,14},{17,18},{21,22},{25,26},{29,30}} | collective-permute-start | bytes 897032 | tf_op jit(solution)/shard_map/ppermute | solution.py:666
  24.9 3.0 %copy-start.6 = (f32[384,384]{1,0:T(8,128)S(1)}, f32[384,384]{1,0:T(8,128)}, u32[]{:S(2)}) copy-start(f32[384,384]{1,0:T(8,128)} %inverse) | copy-start | bytes 1769476
  24.9 13.5 %collective-permute-start.2 = (bf16[1168,128]{1,0:T(8,128)(2,1)S(1)}, bf16[1168,128]{1,0:T(8,128)(2,1)S(1)}, u32[]{:S(2)}, u32[]{:S(2)}) collective-permute-start(bf16[1168,128]{1,0:T(8,128)(2,1)S(1)} %pass_2_0.1), channel_id=1, source_target_pairs={{2,3},{6,7},{10,11},{14,15},{18,19},{22,23},{26,27},{30,31}} | collective-permute-start | bytes 897032 | tf_op jit(solution)/shard_map/ppermute | solution.py:666
  26.6 20.2 %collective-permute-start.5 = (bf16[1168,128]{1,0:T(8,128)(2,1)S(1)}, bf16[1168,128]{1,0:T(8,128)(2,1)S(1)}, u32[]{:S(2)}, u32[]{:S(2)}) collective-permute-start(bf16[1168,128]{1,0:T(8,128)(2,1)S(1)} %pass_2_1.1), channel_id=1, source_target_pairs={{2,3},{6,7},{10,11},{14,15},{18,19},{22,23},{26,27},{30,31}} | collective-permute-start | bytes 897032 | tf_op jit(solution)/shard_map/ppermute | solution.py:666
  46.9 9.7 %copy-start = (f32[4,384]{1,0:T(4,128)S(1)}, f32[4,384]{1,0:T(4,128)}, u32[]{:S(2)}) copy-start(f32[4,384]{1,0:T(4,128)} %doping.1) | copy-start | bytes 18436

commit v9 on v8

--- a/solution.py
+++ b/solution.py
@@ -492,17 +492,12 @@
                 cross[span(parts + c), span(r)] = -imag
 
 
-def local_kernel(calls, odd_too, even_too, *refs):
+def local_kernel(calls, *refs):
     couple, entry = Either(refs[:calls]), Either(refs[calls : 2 * calls])
     local, densities, g, left = refs[2 * calls :]
     slabs = couple.shape[0]
-    active = lax.axis_index("en") > 0
-    if not odd_too:
-        active = jnp.logical_and(active, jnp.logical_not(takes_first_levels()))
-    if not even_too:
-        active = jnp.logical_and(active, takes_first_levels())
-
-    @pl.when(active)
+
+    @pl.when(lax.axis_index("en") > 0)
     def _():
         inv_real, inv_imag, weight = rows_of_entry(entry, slabs)
         densities[...] = jnp.zeros_like(densities)
@@ -752,15 +747,15 @@
             2**16,
         )
 
-    def local_of(slot, odd_too=True, even_too=True):
+    def local_of(slot):
         couple, entry = made[slot]
         return vmem_call(
-            functools.partial(local_kernel, len(couple), odd_too, even_too),
+            functools.partial(local_kernel, len(couple)),
             (jax.ShapeDtypeStruct((local_rows(parts), LANE), F32), density_shape),
             (*couple, *entry),
             [vmem] * (2 * len(couple)),
             work,
-            f"local_{slot}{int(even_too)}{int(odd_too)}",
+            f"local_{slot}",
             flops // 16,
             2**16,
         )
@@ -800,16 +795,12 @@
 
     came = [[arrived[0]], [arrived[1]]]
     carried, local = [carriers_of(0)], [[local_of(0)]]
-    made[1], _ = lax.optimization_barrier((made[1], local[0][0][1]))
-    local.append([local_of(1, odd_too=False)])
-    came[0][0], local[1][0] = lax.optimization_barrier((came[0][0], local[1][0]))
     for stage in range(1, en_size - 1):
         for slot in range(2):
             if stage == 1 and slot == 1:
                 made[1], _ = lax.optimization_barrier((made[1], block))
                 carried.append(carriers_of(1))
-                made[1], _ = lax.optimization_barrier((made[1], carried[1][1]))
-                local[1].append(local_of(1, even_too=False))
+                local.append([local_of(1)])
             block = pass_on(stage, slot, came[slot][-1])
             came[slot].append(forward(block, stage))
     for slot in range(2):

time: 57.8 us -> 56.8 us (0.983)
  waiting for transfers between devices: 19 us -> 18 us
    ppermute x6, waiting for transfers between devices: 16.3 us -> 15.2 us  [forward(): return lax.ppermute(block, 'en', [(stage, stage + 1)])]
    pallas_call x17 -> x16, Pallas kernels: 19.5 us -> 19.6 us  [vmem_call(): pl.pallas_call(kernel, out_shape=tuple(outs), in_specs=in_specs, out_spec...]
  transfers between devices with their start and end apart: 7 -> 7, of which waited for: 3 -> 3; matrix products, arithmetic and copies ran while one was open for 0% -> 0% of each run, Pallas kernels for 28% -> 29%
where the time goes in v9:
time: 56.8 us; the launch traced here: 56.5 us
  Pallas kernels  19.6 us (35%)
  waiting for transfers between devices  18 us (32%)
  starting transfers between devices  9.16 us (16%)
  blocking collectives  7.31 us (13%)
  between operations  1.55 us (3%)
  local copies, waits for them, and re-layouts  0.65 us (1%)
    pallas_call x16, Pallas kernels, vmem_call(): pl.pallas_call(kernel, out_shape=tuple(outs), in_specs=in_specs, out_spec...  19.6 us
    ppermute x6, waiting for transfers between devices, forward(): return lax.ppermute(block, 'en', [(stage, stage + 1)])  15.2 us
    all_to_all x1, blocking collectives, gather_over(): return lax.all_to_all(copies, axis, 0, 0)  7.31 us
    ppermute x6, starting transfers between devices, forward(): return lax.ppermute(block, 'en', [(stage, stage + 1)])  5.44 us
    all_to_all x1, starting transfers between devices, body(): lax.all_to_all(jnp.tile(counts, kt_size), 'kt', 0, 0, tiled=True)  3.72 us
    all_to_all x1, waiting for transfers between devices, body(): lax.all_to_all(jnp.tile(counts, kt_size), 'kt', 0, 0, tiled=True)  2.75 us
  transfers between devices with their start and end apart: 7, of which 3 were waited for; matrix products, arithmetic and copies ran while one was open for 0% of the time, Pallas kernels for 29%

profile of v9, /device:TPU:24, one launch (start us, length us, event | category | flops | bytes accessed | tf_op | source)
XLA Modules:
  0.0 56.5 jit_solution(17512643007903187405)
XLA Ops:
  1.3 0.6 %tile.10 = s32[8,1,1]{2,1,0:T(1,128)} broadcast(s32[]{:T(128)} %bitcast.1), dimensions={} | broadcast | bytes 36 | tf_op jit(solution)/shard_map/tile | solution.py:672
  1.9 3.7 %all-to-all-start = ((s32[8,1,1]{2,1,0:T(1,128)}), s32[8,1,1]{2,1,0:T(1,128)S(1)}, u32[]{:S(2)}, u32[]{:S(2)}) async-start(s32[8,1,1]{2,1,0:T(1,128)} %tile.10), calls=%async_computation | async-start | bytes 8192 | tf_op jit(solution)/shard_map/all_to_all | solution.py:672
  5.6 0.0 copy-start.1
  5.6 0.0 copy-start.2
  5.6 0.0 copy-start.3
  5.6 0.0 copy-start.4
  5.6 0.0 copy-start.5
  5.6 1.8 %lead.1 = (bf16[1168,128]{1,0:T(8,128)(2,1)S(1)}, f32[4,384]{1,0:T(4,128)S(1)}, bf16[4,384,384]{2,1,0:T(8,128)(2,1)S(1)}, bf16[4,384,384]{2,1,0:T(8,128)(2,1)S(1)}) custom-call(f32[12]{0:T(128)} %constant.2.clone.constants_hbm.constants_ref, s32[2]{0:T(128)} %contact_ref.4, f32[4,384]{1,0:T(4,128)} %onsite.4, f32[4,384]{1,0:T(4,128)} %hopping.4, ...), custom_call_target="tpu_custom_call" | custom-call | flops 1358954496 | bytes 2097152 | tf_op jit(solution)/shard_map/lead/pallas_call | solution.py:589
  7.4 2.8 %all-to-all-done = s32[8,1,1]{2,1,0:T(1,128)S(1)} async-done(((s32[8,1,1]{2,1,0:T(1,128)}), s32[8,1,1]{2,1,0:T(1,128)S(1)}, u32[]{:S(2)}, u32[]{:S(2)}) %all-to-all-start) | async-done | bytes 64 | tf_op jit(solution)/shard_map/all_to_all | solution.py:672
  10.2 0.2 reduce.counts_ref
  10.4 0.0 copy-done.1
  10.4 0.0 copy-done.2
  10.4 0.0 copy-done.3
  10.4 0.0 copy-done.4
  10.4 0.0 copy-done.5
  10.5 0.1 begin_0.1
  10.5 0.7 %collective-permute-start = (bf16[1168,128]{1,0:T(8,128)(2,1)S(1)}, bf16[1168,128]{1,0:T(8,128)(2,1)S(1)}, u32[]{:S(2)}, u32[]{:S(2)}) collective-permute-start(bf16[1168,128]{1,0:T(8,128)(2,1)S(1)} %get-tuple-element.61), channel_id=1, source_target_pairs={{0,1},{4,5},{8,9},{12,13},{16,17},{20,21},{24,25},{28,29}} | collective-permute-start | bytes 897032 | tf_op jit(solution)/shard_map/ppermute | solution.py:661
  11.3 0.7 %collective-permute-start.3 = (bf16[1168,128]{1,0:T(8,128)(2,1)S(1)}, bf16[1168,128]{1,0:T(8,128)(2,1)S(1)}, u32[]{:S(2)}, u32[]{:S(2)}) collective-permute-start(bf16[1168,128]{1,0:T(8,128)(2,1)S(1)} %get-tuple-element.47), channel_id=1, source_target_pairs={{0,1},{4,5},{8,9},{12,13},{16,17},{20,21},{24,25},{28,29}} | collective-permute-start | bytes 897032 | tf_op jit(solution)/shard_map/ppermute | solution.py:661
  11.9 1.5 %prepare.1 = (bf16[4,384,384]{2,1,0:T(8,128)(2,1)S(1)}, f32[9,8,384]{2,1,0:T(8,128)S(1)}, bf16[4,384,384]{2,1,0:T(8,128)(2,1)S(1)}, f32[9,8,384]{2,1,0:T(8,128)S(1)}) custom-call(f32[12]{0:T(128)S(1)} %copy-done.5, s32[2]{0:T(128)S(1)} %copy-done.4, s32[8]{0:T(128)S(1)} %reduce.counts_ref, f32[4,384]{1,0:T(4,128)S(1)} %copy-done.1, f32[4,384]{1,0:T(4,128)S(1)} %copy-done.2, ...), custom_call_target="tpu_custom_call" | custom-call | flops 28311552 | bytes 65536 | tf_op jit(solution)/shard_map/prepare/pallas_call | solution.py:589
  13.5 2.8 %local_0.1 = (f32[1536,128]{1,0:T(8,128)S(1)}, f32[4,384]{1,0:T(4,128)S(1)}) custom-call(bf16[4,384,384]{2,1,0:T(8,128)(2,1)S(1)} %get-tuple-element.56.refs_0_, f32[9,8,384]{2,1,0:T(8,128)S(1)} %get-tuple-element.57.refs_1_.refs_0_), custom_call_target="tpu_custom_call" | custom-call | flops 28311552 | bytes 65536 | tf_op jit(solution)/shard_map/local_0/pallas_call | solution.py:589
  16.3 2.3 %carriers_0.1 = (bf16[1536,768]{1,0:T(8,128)(2,1)S(1)}, bf16[768,768]{1,0:T(8,128)(2,1)S(1)}) custom-call(bf16[4,384,384]{2,1,0:T(8,128)(2,1)S(1)} %get-tuple-element.56.refs_0_, f32[9,8,384]{2,1,0:T(8,128)S(1)} %get-tuple-element.57.refs_1_.refs_0_), custom_call_target="tpu_custom_call" | custom-call | flops 28311552 | bytes 65536 | tf_op jit(solution)/shard_map/carriers_0/pallas_call | solution.py:589
  18.6 0.0 collective-permute-done.refs_3_
  18.6 0.7 %collective-permute-start.1 = (bf16[1168,128]{1,0:T(8,128)(2,1)S(1)}, bf16[1168,128]{1,0:T(8,128)(2,1)S(1)}, u32[]{:S(2)}, u32[]{:S(2)}) collective-permute-start(bf16[1168,128]{1,0:T(8,128)(2,1)S(1)} %pass_1_0.1), channel_id=1, source_target_pairs={{1,2},{5,6},{9,10},{13,14},{17,18},{21,22},{25,26},{29,30}} | collective-permute-start | bytes 897032 | tf_op jit(solution)/shard_map/ppermute | solution.py:661
  19.3 2.8 %local_1.1 = (f32[1536,128]{1,0:T(8,128)S(1)}, f32[4,384]{1,0:T(4,128)S(1)}) custom-call(bf16[4,384,384]{2,1,0:T(8,128)(2,1)S(1)} %get-tuple-element.62.refs_0_, f32[9,8,384]{2,1,0:T(8,128)S(1)} %get-tuple-element.63.refs_1_.refs_0_), custom_call_target="tpu_custom_call" | custom-call | flops 28311552 | bytes 65536 | tf_op jit(solution)/shard_map/local_1/pallas_call | solution.py:589
  22.1 2.1 %carriers_1.1 = (bf16[1536,768]{1,0:T(8,128)(2,1)S(1)}, bf16[768,768]{1,0:T(8,128)(2,1)S(1)}) custom-call(bf16[4,384,384]{2,1,0:T(8,128)(2,1)S(1)} %get-tuple-element.62.refs_0_, f32[9,8,384]{2,1,0:T(8,128)S(1)} %get-tuple-element.63.refs_1_.refs_0_), custom_call_target="tpu_custom_call" | custom-call | flops 28311552 | bytes 65536 | tf_op jit(solution)/shard_map/carriers_1/pallas_call | solution.py:589
  24.2 0.0 collective-permute-done.3.refs_3_
  24.2 0.7 %collective-permute-start.4 = (bf16[1168,128]{1,0:T(8,128)(2,1)S(1)}, bf16[1168,128]{1,0:T(8,128)(2,1)S(1)}, u32[]{:S(2)}, u32[]{:S(2)}) collective-permute-start(bf16[1168,128]{1,0:T(8,128)(2,1)S(1)} %pass_1_1.1), channel_id=1, source_target_pairs={{1,2},{5,6},{9,10},{13,14},{17,18},{21,22},{25,26},{29,30}} | collective-permute-start | bytes 897032 | tf_op jit(solution)/shard_map/ppermute | solution.py:661
  24.9 0.0 collective-permute-done.1.refs_3_.refs_4_
  24.9 0.0 copy-start.6
  24.9 1.4 %collective-permute-start.2 = (bf16[1168,128]{1,0:T(8,128)(2,1)S(1)}, bf16[1168,128]{1,0:T(8,128)(2,1)S(1)}, u32[]{:S(2)}, u32[]{:S(2)}) collective-permute-start(bf16[1168,128]{1,0:T(8,128)(2,1)S(1)} %pass_2_0.1), channel_id=1, source_target_pairs={{2,3},{6,7},{10,11},{14,15},{18,19},{22,23},{26,27},{30,31}} | collective-permute-start | bytes 897032 | tf_op jit(solution)/shard_map/ppermute | solution.py:661
  26.4 0.0 collective-permute-done.4.refs_3_.refs_4_
  26.4 1.3 %collective-permute-start.5 = (bf16[1168,128]{1,0:T(8,128)(2,1)S(1)}, bf16[1168,128]{1,0:T(8,128)(2,1)S(1)}, u32[]{:S(2)}, u32[]{:S(2)}) collective-permute-start(bf16[1168,128]{1,0:T(8,128)(2,1)S(1)} %pass_2_1.1), channel_id=1, source_target_pairs={{2,3},{6,7},{10,11},{14,15},{18,19},{22,23},{26,27},{30,31}} | collective-permute-start | bytes 897032 | tf_op jit(solution)/shard_map/ppermute | solution.py:661
  27.7 0.0 copy-done.6
  27.7 0.2 split_inverse.1
  28.0 10.8 %collective-permute-done.2.refs_5_ = bf16[1168,128]{1,0:T(8,128)(2,1)S(1)} collective-permute-done((bf16[1168,128]{1,0:T(8,128)(2,1)S(1)}, bf16[1168,128]{1,0:T(8,128)(2,1)S(1)}, u32[]{:S(2)}, u32[]{:S(2)}) %collective-permute-start.2) | collective-permute-done | bytes 299040 | tf_op jit(solution)/shard_map/ppermute | solution.py:661
  38.7 2.7 %density_0.1.refs_2_ = f32[4,384]{1,0:T(4,128)S(1)} custom-call(bf16[1536,768]{1,0:T(8,128)(2,1)S(1)} %get-tuple-element.59.refs_1_.carriers, f32[9,8,384]{2,1,0:T(8,128)S(1)} %get-tuple-element.57.refs_1_.refs_0_, f32[4,384]{1,0:T(4,128)S(1)} %get-tuple-element.66.refs_1_, f32[4,384]{1,0:T(4,128)S(1)} %get-tuple-element.67.refs_2_, ...), custom_call_target="tpu_custom_call", output_to_operand_aliasing={{}: (3, {})} | custom-call | flops 1811939328 | bytes 2097152 | tf_op jit(solution)/shard_map/density_0/pallas_call | solution.py:589
  41.4 4.5 %collective-permute-done.5.refs_5_ = bf16[1168,128]{1,0:T(8,128)(2,1)S(1)} collective-permute-done((bf16[1168,128]{1,0:T(8,128)(2,1)S(1)}, bf16[1168,128]{1,0:T(8,128)(2,1)S(1)}, u32[]{:S(2)}, u32[]{:S(2)}) %collective-permute-start.5) | collective-permute-done | bytes 299040 | tf_op jit(solution)/shard_map/ppermute | solution.py:661
  45.9 0.0 copy-start
  45.9 2.5 %density_1.1 = f32[4,384]{1,0:T(4,128)S(1)} custom-call(bf16[1536,768]{1,0:T(8,128)(2,1)S(1)} %get-tuple-element.64.refs_1_.carriers, f32[9,8,384]{2,1,0:T(8,128)S(1)} %get-tuple-element.63.refs_1_.refs_0_, f32[4,384]{1,0:T(4,128)S(1)} %get-tuple-element.65.refs_1_, f32[4,384]{1,0:T(4,128)S(1)} %density_0.1.refs_2_, ...), custom_call_target="tpu_custom_call", output_to_operand_aliasing={{}: (3, {})} | custom-call | flops 1811939328 | bytes 2097152 | tf_op jit(solution)/shard_map/density_1/pallas_call | solution.py:589
  48.3 7.3 %all_to_all.14.gathered = f32[8,4,384]{2,1,0:T(4,128)S(1)} all-to-all(f32[8,4,384]{2,1,0:T(4,128)S(1)} %broadcast_in_dim.2), channel_id=1, replica_groups=mesh['kt'=8,'en'=4] {'kt'}, dimensions={0} | all-to-all | bytes 98304 | tf_op jit(solution)/shard_map/all_to_all | solution.py:635
  55.6 0.0 copy-done
  55.6 0.9 %last.1 = (f32[4,384]{1,0:T(4,128)}, f32[4,384]{1,0:T(4,128)}) custom-call(f32[8,4,384]{2,1,0:T(4,128)S(1)} %all_to_all.14.gathered, f32[4,384]{1,0:T(4,128)S(1)} %copy-done, bf16[384,384]{1,0:T(8,128)(2,1)S(1)} %get-tuple-element.75.high, bf16[384,384]{1,0:T(8,128)(2,1)S(1)} %get-tuple-element.76.middle, bf16[384,384]{1,0:T(8,128)(2,1)S(1)} %get-tuple-element.77.low), custom_call_target="tpu_custom_call" | custom-call | flops 113246208 | bytes 2097152 | tf_op jit(solution)/shard_map/last/pallas_call | solution.py:589
  (6 shorter events, 0.1 us)
Async XLA Ops:
  1.9 8.3 %all-to-all-start = ((s32[8,1,1]{2,1,0:T(1,128)}), s32[8,1,1]{2,1,0:T(1,128)S(1)}, u32[]{:S(2)}, u32[]{:S(2)}) async-start(s32[8,1,1]{2,1,0:T(1,128)} %tile.10), calls=%async_computation | async-start | bytes 8192 | tf_op jit(solution)/shard_map/all_to_all | solution.py:672
  5.6 4.8 %copy-start.1 = (f32[4,384]{1,0:T(4,128)S(1)}, f32[4,384]{1,0:T(4,128)}, u32[]{:S(2)}) copy-start(f32[4,384]{1,0:T(4,128)} %onsite.4) | copy-start | bytes 18436
  5.6 4.8 %copy-start.2 = (f32[4,384]{1,0:T(4,128)S(1)}, f32[4,384]{1,0:T(4,128)}, u32[]{:S(2)}) copy-start(f32[4,384]{1,0:T(4,128)} %hopping.4) | copy-start | bytes 18436
  5.6 4.8 %copy-start.3 = (f32[4,384]{1,0:T(4,128)S(1)}, f32[4,384]{1,0:T(4,128)}, u32[]{:S(2)}) copy-start(f32[4,384]{1,0:T(4,128)} %potential.4) | copy-start | bytes 18436
  5.6 4.8 %copy-start.4 = (s32[2]{0:T(128)S(1)}, s32[2]{0:T(128)}, u32[]{:S(2)}) copy-start(s32[2]{0:T(128)} %contact_ref.4) | copy-start | bytes 28
  5.6 4.8 %copy-start.5 = (f32[12]{0:T(128)S(1)}, f32[12]{0:T(128)}, u32[]{:S(2)}) copy-start(f32[12]{0:T(128)} %constant.2.clone.constants_hbm.constants_ref) | copy-start | bytes 148
  10.5 8.1 %collective-permute-start = (bf16[1168,128]{1,0:T(8,128)(2,1)S(1)}, bf16[1168,128]{1,0:T(8,128)(2,1)S(1)}, u32[]{:S(2)}, u32[]{:S(2)}) collective-permute-start(bf16[1168,128]{1,0:T(8,128)(2,1)S(1)} %get-tuple-element.61), channel_id=1, source_target_pairs={{0,1},{4,5},{8,9},{12,13},{16,17},{20,21},{24,25},{28,29}} | collective-permute-start | bytes 897032 | tf_op jit(solution)/shard_map/ppermute | solution.py:661
  11.3 12.9 %collective-permute-start.3 = (bf16[1168,128]{1,0:T(8,128)(2,1)S(1)}, bf16[1168,128]{1,0:T(8,128)(2,1)S(1)}, u32[]{:S(2)}, u32[]{:S(2)}) collective-permute-start(bf16[1168,128]{1,0:T(8,128)(2,1)S(1)} %get-tuple-element.47), channel_id=1, source_target_pairs={{0,1},{4,5},{8,9},{12,13},{16,17},{20,21},{24,25},{28,29}} | collective-permute-start | bytes 897032 | tf_op jit(solution)/shard_map/ppermute | solution.py:661
  18.6 6.3 %collective-permute-start.1 = (bf16[1168,128]{1,0:T(8,128)(2,1)S(1)}, bf16[1168,128]{1,0:T(8,128)(2,1)S(1)}, u32[]{:S(2)}, u32[]{:S(2)}) collective-permute-start(bf16[1168,128]{1,0:T(8,128)(2,1)S(1)} %pass_1_0.1), channel_id=1, source_target_pairs={{1,2},{5,6},{9,10},{13,14},{17,18},{21,22},{25,26},{29,30}} | collective-permute-start | bytes 897032 | tf_op jit(solution)/shard_map/ppermute | solution.py:661
  24.2 2.2 %collective-permute-start.4 = (bf16[1168,128]{1,0:T(8,128)(2,1)S(1)}, bf16[1168,128]{1,0:T(8,128)(2,1)S(1)}, u32[]{:S(2)}, u32[]{:S(2)}) collective-permute-start(bf16[1168,128]{1,0:T(8,128)(2,1)S(1)} %pass_1_1.1), channel_id=1, source_target_pairs={{1,2},{5,6},{9,10},{13,14},{17,18},{21,22},{25,26},{29,30}} | collective-permute-start | bytes 897032 | tf_op jit(solution)/shard_map/ppermute | solution.py:661
  24.9 2.8 %copy-start.6 = (f32[384,384]{1,0:T(8,128)S(1)}, f32[384,384]{1,0:T(8,128)}, u32[]{:S(2)}) copy-start(f32[384,384]{1,0:T(8,128)} %inverse) | copy-start | bytes 1769476
  24.9 13.8 %collective-permute-start.2 = (bf16[1168,128]{1,0:T(8,128)(2,1)S(1)}, bf16[1168,128]{1,0:T(8,128)(2,1)S(1)}, u32[]{:S(2)}, u32[]{:S(2)}) collective-permute-start(bf16[1168,128]{1,0:T(8,128)(2,1)S(1)} %pass_2_0.1), channel_id=1, source_target_pairs={{2,3},{6,7},{10,11},{14,15},{18,19},{22,23},{26,27},{30,31}} | collective-permute-start | bytes 897032 | tf_op jit(solution)/shard_map/ppermute | solution.py:661
  26.4 19.4 %collective-permute-start.5 = (bf16[1168,128]{1,0:T(8,128)(2,1)S(1)}, bf16[1168,128]{1,0:T(8,128)(2,1)S(1)}, u32[]{:S(2)}, u32[]{:S(2)}) collective-permute-start(bf16[1168,128]{1,0:T(8,128)(2,1)S(1)} %pass_2_1.1), channel_id=1, source_target_pairs={{2,3},{6,7},{10,11},{14,15},{18,19},{22,23},{26,27},{30,31}} | collective-permute-start | bytes 897032 | tf_op jit(solution)/shard_map/ppermute | solution.py:661
  45.9 9.8 %copy-start = (f32[4,384]{1,0:T(4,128)S(1)}, f32[4,384]{1,0:T(4,128)}, u32[]{:S(2)}) copy-start(f32[4,384]{1,0:T(4,128)} %doping.1) | copy-start | bytes 18436

commit v10 on v9

--- a/solution.py
+++ b/solution.py
@@ -173,7 +173,11 @@
 
 
 def times_carried(coupled, g, left, parts):
-    product = jnp.dot(coupled, g[...], preferred_element_type=F32).astype(BF16)
+    product = jnp.dot(coupled, g[...], preferred_element_type=F32)
+    keep_product(product.astype(BF16), left, parts)
+
+
+def keep_product(product, left, parts):
     for column in range(2 * parts):
         half, c = (
             (0, column)
@@ -184,7 +188,7 @@
 
 
 def finish_slab(
-    s, times_turned, left, g, packed, columns, real_row, imag_row, note, parts, local=None
+    s, times_turned, left, g, packed, columns, real_row, imag_row, note, parts, local=None, offset=0
 ):
     last = (parts - 1) * LANE
     rows, cols = tile_indices()
@@ -215,9 +219,9 @@
             return
         for half, green in ((0, green_real), (1, green_imag)):
             rounded = green.astype(BF16)
-            g[span(r), span(place(parts, half, c))] = rounded
+            g[span(r), span(offset + place(parts, half, c))] = rounded
             if r != c:
-                g[span(c), span(place(parts, half, r))] = rounded.T
+                g[span(c), span(offset + place(parts, half, r))] = rounded.T
 
     turned = times_turned(left[...])
     far = turned[2 * last :, :]
@@ -456,31 +460,61 @@
     return inv_real, inv_imag, entry[2 * slabs, 0:1, 0:1]
 
 
-def carrier_kernel(calls, *refs):
-    couple, entry = Either(refs[:calls]), Either(refs[calls : 2 * calls])
-    carriers, cross = refs[2 * calls :]
+def operator_kernel(couple, entry, carriers, cross, local, densities, both, left):
     slabs, orbitals, _ = couple.shape
     parts = orbitals // LANE
 
     @pl.when(lax.axis_index("en") > 0)
     def _():
-        inv_real, inv_imag, _ = rows_of_entry(entry, slabs)
-        down = jnp.concatenate([inv_real, inv_imag], axis=0).T
+        inv_real, inv_imag, weight = rows_of_entry(entry, slabs)
+        down = columns_of(inv_real, inv_imag)
         for s in range(slabs):
-            here = slice(s * orbitals, (s + 1) * orbitals)
+            coupled = couple[s]
             real_col = down[:, s : s + 1]
             imag_col = down[:, slabs + s : slabs + s + 1]
+            real_row, imag_row = inv_real[s : s + 1, :], inv_imag[s : s + 1, :]
             if s == 0:
-                wide = couple[0].astype(F32)
+                wide = coupled.astype(F32)
                 real, imag = real_col * wide, imag_col * wide
+                densities[0:1, :] = -weight * imag_row
             else:
-                ahead = slice((s - 1) * orbitals, s * orbitals)
-                product = jnp.dot(couple[s], carriers[ahead, :], preferred_element_type=F32)
-                from_real, from_imag = product[:, :orbitals], product[:, orbitals:]
+                width = 2 * orbitals if s == 1 else 4 * orbitals
+                product = jnp.dot(coupled, both[:, :width], preferred_element_type=F32)
+                from_real, from_imag = product[:, :orbitals], product[:, orbitals : 2 * orbitals]
                 real = real_col * from_real - imag_col * from_imag
                 imag = real_col * from_imag + imag_col * from_real
-            carriers[here, :orbitals] = real.astype(BF16)
-            carriers[here, orbitals:] = imag.astype(BF16)
+                if s == 1:
+                    wide = coupled.astype(F32)
+                    for half, inv in ((0, inv_real), (1, inv_imag)):
+                        piece = (wide * inv[0:1, :].astype(BF16).astype(F32)).astype(BF16)
+                        for c in range(parts):
+                            store_left(left, piece[:, span(c)], half, c, parts)
+                else:
+                    keep_product(product[:, 2 * orbitals :].astype(BF16), left, parts)
+            real, imag = real.astype(BF16), imag.astype(BF16)
+            here = slice(s * orbitals, (s + 1) * orbitals)
+            carriers[here, :orbitals] = real
+            carriers[here, orbitals:] = imag
+            if s < slabs - 1:
+                both[:, :orbitals] = real
+                both[:, orbitals : 2 * orbitals] = imag
+            if s == 0:
+                continue
+
+            def times_turned(rows):
+                return lax.dot_general(
+                    rows, coupled, (((1,), (1,)), ((), ())), preferred_element_type=F32
+                )
+
+            def note(r, middle):
+                densities[s : s + 1, span(r)] = -weight * middle
+
+            final = s == slabs - 1
+            finish_slab(
+                s, times_turned, left, None if final else both, None,
+                (real_col, imag_col), real_row, imag_row, note, parts,
+                local if final else None, 2 * parts,
+            )
         top = (slabs - 1) * parts
         for r in range(parts):
             for c in range(parts):
@@ -490,20 +524,6 @@
                 cross[span(parts + c), span(parts + r)] = real
                 cross[span(c), span(parts + r)] = imag
                 cross[span(parts + c), span(r)] = -imag
-
-
-def local_kernel(calls, *refs):
-    couple, entry = Either(refs[:calls]), Either(refs[calls : 2 * calls])
-    local, densities, g, left = refs[2 * calls :]
-    slabs = couple.shape[0]
-
-    @pl.when(lax.axis_index("en") > 0)
-    def _():
-        inv_real, inv_imag, weight = rows_of_entry(entry, slabs)
-        densities[...] = jnp.zeros_like(densities)
-        first_segment(
-            lambda s: couple[s], inv_real, inv_imag, weight, g, left, None, densities, local
-        )
 
 
 def pass_kernel(stage, calls, *refs):
@@ -734,31 +754,28 @@
     carriers_shape = jax.ShapeDtypeStruct((slabs * orbitals, 2 * orbitals), BF16)
     double_shape = jax.ShapeDtypeStruct((2 * orbitals, 2 * orbitals), BF16)
 
-    def carriers_of(slot):
-        couple, entry = made[slot]
-        return vmem_call(
-            functools.partial(carrier_kernel, len(couple)),
-            (carriers_shape, double_shape),
-            (*couple, *entry),
-            [vmem] * (2 * len(couple)),
-            [],
-            f"carriers_{slot}",
+    def operator_of(slot):
+        (couple,), (entry,) = made[slot]
+        results = vmem_call(
+            operator_kernel,
+            (
+                carriers_shape,
+                double_shape,
+                jax.ShapeDtypeStruct((local_rows(parts), LANE), F32),
+                density_shape,
+            ),
+            (couple, entry),
+            [vmem] * 2,
+            [
+                pltpu.VMEM((orbitals, 4 * orbitals), BF16),
+                pltpu.VMEM((2 * orbitals, orbitals), BF16),
+            ],
+            f"operator_{slot}",
             flops // 16,
             2**16,
         )
-
-    def local_of(slot):
-        couple, entry = made[slot]
-        return vmem_call(
-            functools.partial(local_kernel, len(couple)),
-            (jax.ShapeDtypeStruct((local_rows(parts), LANE), F32), density_shape),
-            (*couple, *entry),
-            [vmem] * (2 * len(couple)),
-            work,
-            f"local_{slot}",
-            flops // 16,
-            2**16,
-        )
+        carried.append(results[:2])
+        local.append([results[2:]])
 
     def pass_on(stage, slot, block):
         calls = [one[0] for one in local[slot]]
@@ -794,13 +811,13 @@
         )[0]
 
     came = [[arrived[0]], [arrived[1]]]
-    carried, local = [carriers_of(0)], [[local_of(0)]]
+    carried, local = [], []
+    operator_of(0)
     for stage in range(1, en_size - 1):
         for slot in range(2):
             if stage == 1 and slot == 1:
                 made[1], _ = lax.optimization_barrier((made[1], block))
-                carried.append(carriers_of(1))
-                local.append([local_of(1)])
+                operator_of(1)
             block = pass_on(stage, slot, came[slot][-1])
             came[slot].append(forward(block, stage))
     for slot in range(2):

time: 56.8 us -> 55.9 us (0.984)
  Pallas kernels: 19.6 us -> 17.1 us
  waiting for transfers between devices: 18 us -> 19.4 us
    pallas_call x16 -> x14, Pallas kernels: 19.6 us -> 17.1 us  [vmem_call(): pl.pallas_call(kernel, out_shape=tuple(outs), in_specs=in_specs, out_spec...]
    ppermute x6, waiting for transfers between devices: 15.2 us -> 16.6 us  [forward(): return lax.ppermute(block, 'en', [(stage, stage + 1)])]
  transfers between devices with their start and end apart: 7 -> 7, of which waited for: 3 -> 3; matrix products, arithmetic and copies ran while one was open for 0% -> 0% of each run, Pallas kernels for 29% -> 25%
where the time goes in v10:
time: 55.9 us; the launch traced here: 55.6 us
  waiting for transfers between devices  19.4 us (35%)
  Pallas kernels  17.1 us (31%)
  starting transfers between devices  9.38 us (17%)
  blocking collectives  7.31 us (13%)
  between operations  1.53 us (3%)
  local copies, waits for them, and re-layouts  0.65 us (1%)
    pallas_call x14, Pallas kernels, vmem_call(): pl.pallas_call(kernel, out_shape=tuple(outs), in_specs=in_specs, out_spec...  17.1 us
    ppermute x6, waiting for transfers between devices, forward(): return lax.ppermute(block, 'en', [(stage, stage + 1)])  16.6 us
    all_to_all x1, blocking collectives, gather_over(): return lax.all_to_all(copies, axis, 0, 0)  7.31 us
    ppermute x6, starting transfers between devices, forward(): return lax.ppermute(block, 'en', [(stage, stage + 1)])  5.66 us
    all_to_all x1, starting transfers between devices, body(): lax.all_to_all(jnp.tile(counts, kt_size), 'kt', 0, 0, tiled=True)  3.72 us
    all_to_all x1, waiting for transfers between devices, body(): lax.all_to_all(jnp.tile(counts, kt_size), 'kt', 0, 0, tiled=True)  2.75 us
  transfers between devices with their start and end apart: 7, of which 3 were waited for; matrix products, arithmetic and copies ran while one was open for 0% of the time, Pallas kernels for 25%

profile of v10, /device:TPU:24, one launch (start us, length us, event | category | flops | bytes accessed | tf_op | source)
XLA Modules:
  0.0 55.6 jit_solution(2064364566962398820)
XLA Ops:
  1.3 0.6 %tile.10 = s32[8,1,1]{2,1,0:T(1,128)} broadcast(s32[]{:T(128)} %bitcast.1), dimensions={} | broadcast | bytes 36 | tf_op jit(solution)/shard_map/tile | solution.py:692
  1.9 3.7 %all-to-all-start = ((s32[8,1,1]{2,1,0:T(1,128)}), s32[8,1,1]{2,1,0:T(1,128)S(1)}, u32[]{:S(2)}, u32[]{:S(2)}) async-start(s32[8,1,1]{2,1,0:T(1,128)} %tile.10), calls=%async_computation | async-start | bytes 8192 | tf_op jit(solution)/shard_map/all_to_all | solution.py:692
  5.6 0.0 copy-start.1
  5.6 0.0 copy-start.2
  5.6 0.0 copy-start.3
  5.6 0.0 copy-start.4
  5.6 0.0 copy-start.5
  5.6 1.8 %lead.1 = (bf16[1168,128]{1,0:T(8,128)(2,1)S(1)}, f32[4,384]{1,0:T(4,128)S(1)}, bf16[4,384,384]{2,1,0:T(8,128)(2,1)S(1)}, bf16[4,384,384]{2,1,0:T(8,128)(2,1)S(1)}) custom-call(f32[12]{0:T(128)} %constant.2.clone.constants_hbm.constants_ref, s32[2]{0:T(128)} %contact_ref.4, f32[4,384]{1,0:T(4,128)} %onsite.4, f32[4,384]{1,0:T(4,128)} %hopping.4, ...), custom_call_target="tpu_custom_call" | custom-call | flops 1358954496 | bytes 2097152 | tf_op jit(solution)/shard_map/lead/pallas_call | solution.py:609
  7.4 2.8 %all-to-all-done = s32[8,1,1]{2,1,0:T(1,128)S(1)} async-done(((s32[8,1,1]{2,1,0:T(1,128)}), s32[8,1,1]{2,1,0:T(1,128)S(1)}, u32[]{:S(2)}, u32[]{:S(2)}) %all-to-all-start) | async-done | bytes 64 | tf_op jit(solution)/shard_map/all_to_all | solution.py:692
  10.2 0.2 reduce.counts_ref
  10.4 0.0 copy-done.1
  10.4 0.0 copy-done.2
  10.4 0.0 copy-done.3
  10.4 0.0 copy-done.4
  10.4 0.0 copy-done.5
  10.5 0.1 begin_0.1
  10.5 0.7 %collective-permute-start = (bf16[1168,128]{1,0:T(8,128)(2,1)S(1)}, bf16[1168,128]{1,0:T(8,128)(2,1)S(1)}, u32[]{:S(2)}, u32[]{:S(2)}) collective-permute-start(bf16[1168,128]{1,0:T(8,128)(2,1)S(1)} %get-tuple-element.61), channel_id=1, source_target_pairs={{0,1},{4,5},{8,9},{12,13},{16,17},{20,21},{24,25},{28,29}} | collective-permute-start | bytes 897032 | tf_op jit(solution)/shard_map/ppermute | solution.py:681
  11.3 0.7 %collective-permute-start.3 = (bf16[1168,128]{1,0:T(8,128)(2,1)S(1)}, bf16[1168,128]{1,0:T(8,128)(2,1)S(1)}, u32[]{:S(2)}, u32[]{:S(2)}) collective-permute-start(bf16[1168,128]{1,0:T(8,128)(2,1)S(1)} %get-tuple-element.47), channel_id=1, source_target_pairs={{0,1},{4,5},{8,9},{12,13},{16,17},{20,21},{24,25},{28,29}} | collective-permute-start | bytes 897032 | tf_op jit(solution)/shard_map/ppermute | solution.py:681
  11.9 1.5 %prepare.1 = (bf16[4,384,384]{2,1,0:T(8,128)(2,1)S(1)}, f32[9,8,384]{2,1,0:T(8,128)S(1)}, bf16[4,384,384]{2,1,0:T(8,128)(2,1)S(1)}, f32[9,8,384]{2,1,0:T(8,128)S(1)}) custom-call(f32[12]{0:T(128)S(1)} %copy-done.5, s32[2]{0:T(128)S(1)} %copy-done.4, s32[8]{0:T(128)S(1)} %reduce.counts_ref, f32[4,384]{1,0:T(4,128)S(1)} %copy-done.1, f32[4,384]{1,0:T(4,128)S(1)} %copy-done.2, ...), custom_call_target="tpu_custom_call" | custom-call | flops 28311552 | bytes 65536 | tf_op jit(solution)/shard_map/prepare/pallas_call | solution.py:609
  13.5 4.0 %operator_0.1 = (bf16[1536,768]{1,0:T(8,128)(2,1)S(1)}, bf16[768,768]{1,0:T(8,128)(2,1)S(1)}, f32[1536,128]{1,0:T(8,128)S(1)}, f32[4,384]{1,0:T(4,128)S(1)}) custom-call(bf16[4,384,384]{2,1,0:T(8,128)(2,1)S(1)} %get-tuple-element.56.couple, f32[9,8,384]{2,1,0:T(8,128)S(1)} %get-tuple-element.57.entry.refs_0_), custom_call_target="tpu_custom_call" | custom-call | flops 28311552 | bytes 65536 | tf_op jit(solution)/shard_map/operator_0/pallas_call | solution.py:609
  17.5 0.0 collective-permute-done.refs_3_
  17.5 0.7 %collective-permute-start.1 = (bf16[1168,128]{1,0:T(8,128)(2,1)S(1)}, bf16[1168,128]{1,0:T(8,128)(2,1)S(1)}, u32[]{:S(2)}, u32[]{:S(2)}) collective-permute-start(bf16[1168,128]{1,0:T(8,128)(2,1)S(1)} %pass_1_0.1), channel_id=1, source_target_pairs={{1,2},{5,6},{9,10},{13,14},{17,18},{21,22},{25,26},{29,30}} | collective-permute-start | bytes 897032 | tf_op jit(solution)/shard_map/ppermute | solution.py:681
  18.2 3.8 %operator_1.1 = (bf16[1536,768]{1,0:T(8,128)(2,1)S(1)}, bf16[768,768]{1,0:T(8,128)(2,1)S(1)}, f32[1536,128]{1,0:T(8,128)S(1)}, f32[4,384]{1,0:T(4,128)S(1)}) custom-call(bf16[4,384,384]{2,1,0:T(8,128)(2,1)S(1)} %get-tuple-element.62.couple, f32[9,8,384]{2,1,0:T(8,128)S(1)} %get-tuple-element.63.entry.refs_0_), custom_call_target="tpu_custom_call" | custom-call | flops 28311552 | bytes 65536 | tf_op jit(solution)/shard_map/operator_1/pallas_call | solution.py:609
  22.0 0.0 collective-permute-done.3.refs_3_
  22.0 0.7 %collective-permute-start.4 = (bf16[1168,128]{1,0:T(8,128)(2,1)S(1)}, bf16[1168,128]{1,0:T(8,128)(2,1)S(1)}, u32[]{:S(2)}, u32[]{:S(2)}) collective-permute-start(bf16[1168,128]{1,0:T(8,128)(2,1)S(1)} %pass_1_1.1), channel_id=1, source_target_pairs={{1,2},{5,6},{9,10},{13,14},{17,18},{21,22},{25,26},{29,30}} | collective-permute-start | bytes 897032 | tf_op jit(solution)/shard_map/ppermute | solution.py:681
  22.7 0.0 collective-permute-done.1.refs_3_.refs_4_
  22.7 0.0 copy-start.6
  22.7 1.4 %collective-permute-start.2 = (bf16[1168,128]{1,0:T(8,128)(2,1)S(1)}, bf16[1168,128]{1,0:T(8,128)(2,1)S(1)}, u32[]{:S(2)}, u32[]{:S(2)}) collective-permute-start(bf16[1168,128]{1,0:T(8,128)(2,1)S(1)} %pass_2_0.1), channel_id=1, source_target_pairs={{2,3},{6,7},{10,11},{14,15},{18,19},{22,23},{26,27},{30,31}} | collective-permute-start | bytes 897032 | tf_op jit(solution)/shard_map/ppermute | solution.py:681
  24.2 0.0 collective-permute-done.4.refs_3_.refs_4_
  24.2 1.5 %collective-permute-start.5 = (bf16[1168,128]{1,0:T(8,128)(2,1)S(1)}, bf16[1168,128]{1,0:T(8,128)(2,1)S(1)}, u32[]{:S(2)}, u32[]{:S(2)}) collective-permute-start(bf16[1168,128]{1,0:T(8,128)(2,1)S(1)} %pass_2_1.1), channel_id=1, source_target_pairs={{2,3},{6,7},{10,11},{14,15},{18,19},{22,23},{26,27},{30,31}} | collective-permute-start | bytes 897032 | tf_op jit(solution)/shard_map/ppermute | solution.py:681
  25.7 0.0 copy-done.6
  25.7 0.2 split_inverse.1
  26.0 13.7 %collective-permute-done.2.refs_5_ = bf16[1168,128]{1,0:T(8,128)(2,1)S(1)} collective-permute-done((bf16[1168,128]{1,0:T(8,128)(2,1)S(1)}, bf16[1168,128]{1,0:T(8,128)(2,1)S(1)}, u32[]{:S(2)}, u32[]{:S(2)}) %collective-permute-start.2) | collective-permute-done | bytes 299040 | tf_op jit(solution)/shard_map/ppermute | solution.py:681
  39.7 2.4 %density_0.1.refs_2_ = f32[4,384]{1,0:T(4,128)S(1)} custom-call(bf16[1536,768]{1,0:T(8,128)(2,1)S(1)} %get-tuple-element.59.refs_1_.carriers, f32[9,8,384]{2,1,0:T(8,128)S(1)} %get-tuple-element.57.entry.refs_0_, f32[4,384]{1,0:T(4,128)S(1)} %get-tuple-element.66.refs_1_, f32[4,384]{1,0:T(4,128)S(1)} %get-tuple-element.67.refs_2_, ...), custom_call_target="tpu_custom_call", output_to_operand_aliasing={{}: (3, {})} | custom-call | flops 1811939328 | bytes 2097152 | tf_op jit(solution)/shard_map/density_0/pallas_call | solution.py:609
  42.1 2.9 %collective-permute-done.5.refs_5_ = bf16[1168,128]{1,0:T(8,128)(2,1)S(1)} collective-permute-done((bf16[1168,128]{1,0:T(8,128)(2,1)S(1)}, bf16[1168,128]{1,0:T(8,128)(2,1)S(1)}, u32[]{:S(2)}, u32[]{:S(2)}) %collective-permute-start.5) | collective-permute-done | bytes 299040 | tf_op jit(solution)/shard_map/ppermute | solution.py:681
  45.0 0.0 copy-start
  45.0 2.4 %density_1.1 = f32[4,384]{1,0:T(4,128)S(1)} custom-call(bf16[1536,768]{1,0:T(8,128)(2,1)S(1)} %get-tuple-element.64.refs_1_.carriers, f32[9,8,384]{2,1,0:T(8,128)S(1)} %get-tuple-element.63.entry.refs_0_, f32[4,384]{1,0:T(4,128)S(1)} %get-tuple-element.65.refs_1_, f32[4,384]{1,0:T(4,128)S(1)} %density_0.1.refs_2_, ...), custom_call_target="tpu_custom_call", output_to_operand_aliasing={{}: (3, {})} | custom-call | flops 1811939328 | bytes 2097152 | tf_op jit(solution)/shard_map/density_1/pallas_call | solution.py:609
  47.4 7.3 %all_to_all.14.gathered = f32[8,4,384]{2,1,0:T(4,128)S(1)} all-to-all(f32[8,4,384]{2,1,0:T(4,128)S(1)} %broadcast_in_dim.2), channel_id=1, replica_groups=mesh['kt'=8,'en'=4] {'kt'}, dimensions={0} | all-to-all | bytes 98304 | tf_op jit(solution)/shard_map/all_to_all | solution.py:655
  54.7 0.0 copy-done
  54.7 0.9 %last.1 = (f32[4,384]{1,0:T(4,128)}, f32[4,384]{1,0:T(4,128)}) custom-call(f32[8,4,384]{2,1,0:T(4,128)S(1)} %all_to_all.14.gathered, f32[4,384]{1,0:T(4,128)S(1)} %copy-done, bf16[384,384]{1,0:T(8,128)(2,1)S(1)} %get-tuple-element.75.high, bf16[384,384]{1,0:T(8,128)(2,1)S(1)} %get-tuple-element.76.middle, bf16[384,384]{1,0:T(8,128)(2,1)S(1)} %get-tuple-element.77.low), custom_call_target="tpu_custom_call" | custom-call | flops 113246208 | bytes 2097152 | tf_op jit(solution)/shard_map/last/pallas_call | solution.py:609
  (6 shorter events, 0.1 us)
Async XLA Ops:
  1.9 8.3 %all-to-all-start = ((s32[8,1,1]{2,1,0:T(1,128)}), s32[8,1,1]{2,1,0:T(1,128)S(1)}, u32[]{:S(2)}, u32[]{:S(2)}) async-start(s32[8,1,1]{2,1,0:T(1,128)} %tile.10), calls=%async_computation | async-start | bytes 8192 | tf_op jit(solution)/shard_map/all_to_all | solution.py:692
  5.6 4.8 %copy-start.1 = (f32[4,384]{1,0:T(4,128)S(1)}, f32[4,384]{1,0:T(4,128)}, u32[]{:S(2)}) copy-start(f32[4,384]{1,0:T(4,128)} %onsite.4) | copy-start | bytes 18436
  5.6 4.8 %copy-start.2 = (f32[4,384]{1,0:T(4,128)S(1)}, f32[4,384]{1,0:T(4,128)}, u32[]{:S(2)}) copy-start(f32[4,384]{1,0:T(4,128)} %hopping.4) | copy-start | bytes 18436
  5.6 4.8 %copy-start.3 = (f32[4,384]{1,0:T(4,128)S(1)}, f32[4,384]{1,0:T(4,128)}, u32[]{:S(2)}) copy-start(f32[4,384]{1,0:T(4,128)} %potential.4) | copy-start | bytes 18436
  5.6 4.8 %copy-start.4 = (s32[2]{0:T(128)S(1)}, s32[2]{0:T(128)}, u32[]{:S(2)}) copy-start(s32[2]{0:T(128)} %contact_ref.4) | copy-start | bytes 28
  5.6 4.8 %copy-start.5 = (f32[12]{0:T(128)S(1)}, f32[12]{0:T(128)}, u32[]{:S(2)}) copy-start(f32[12]{0:T(128)} %constant.2.clone.constants_hbm.constants_ref) | copy-start | bytes 148
  10.5 6.9 %collective-permute-start = (bf16[1168,128]{1,0:T(8,128)(2,1)S(1)}, bf16[1168,128]{1,0:T(8,128)(2,1)S(1)}, u32[]{:S(2)}, u32[]{:S(2)}) collective-permute-start(bf16[1168,128]{1,0:T(8,128)(2,1)S(1)} %get-tuple-element.61), channel_id=1, source_target_pairs={{0,1},{4,5},{8,9},{12,13},{16,17},{20,21},{24,25},{28,29}} | collective-permute-start | bytes 897032 | tf_op jit(solution)/shard_map/ppermute | solution.py:681
  11.3 10.7 %collective-permute-start.3 = (bf16[1168,128]{1,0:T(8,128)(2,1)S(1)}, bf16[1168,128]{1,0:T(8,128)(2,1)S(1)}, u32[]{:S(2)}, u32[]{:S(2)}) collective-permute-start(bf16[1168,128]{1,0:T(8,128)(2,1)S(1)} %get-tuple-element.47), channel_id=1, source_target_pairs={{0,1},{4,5},{8,9},{12,13},{16,17},{20,21},{24,25},{28,29}} | collective-permute-start | bytes 897032 | tf_op jit(solution)/shard_map/ppermute | solution.py:681
  17.5 5.2 %collective-permute-start.1 = (bf16[1168,128]{1,0:T(8,128)(2,1)S(1)}, bf16[1168,128]{1,0:T(8,128)(2,1)S(1)}, u32[]{:S(2)}, u32[]{:S(2)}) collective-permute-start(bf16[1168,128]{1,0:T(8,128)(2,1)S(1)} %pass_1_0.1), channel_id=1, source_target_pairs={{1,2},{5,6},{9,10},{13,14},{17,18},{21,22},{25,26},{29,30}} | collective-permute-start | bytes 897032 | tf_op jit(solution)/shard_map/ppermute | solution.py:681
  22.0 2.2 %collective-permute-start.4 = (bf16[1168,128]{1,0:T(8,128)(2,1)S(1)}, bf16[1168,128]{1,0:T(8,128)(2,1)S(1)}, u32[]{:S(2)}, u32[]{:S(2)}) collective-permute-start(bf16[1168,128]{1,0:T(8,128)(2,1)S(1)} %pass_1_1.1), channel_id=1, source_target_pairs={{1,2},{5,6},{9,10},{13,14},{17,18},{21,22},{25,26},{29,30}} | collective-permute-start | bytes 897032 | tf_op jit(solution)/shard_map/ppermute | solution.py:681
  22.7 3.0 %copy-start.6 = (f32[384,384]{1,0:T(8,128)S(1)}, f32[384,384]{1,0:T(8,128)}, u32[]{:S(2)}) copy-start(f32[384,384]{1,0:T(8,128)} %inverse) | copy-start | bytes 1769476
  22.7 16.9 %collective-permute-start.2 = (bf16[1168,128]{1,0:T(8,128)(2,1)S(1)}, bf16[1168,128]{1,0:T(8,128)(2,1)S(1)}, u32[]{:S(2)}, u32[]{:S(2)}) collective-permute-start(bf16[1168,128]{1,0:T(8,128)(2,1)S(1)} %pass_2_0.1), channel_id=1, source_target_pairs={{2,3},{6,7},{10,11},{14,15},{18,19},{22,23},{26,27},{30,31}} | collective-permute-start | bytes 897032 | tf_op jit(solution)/shard_map/ppermute | solution.py:681
  24.2 20.8 %collective-permute-start.5 = (bf16[1168,128]{1,0:T(8,128)(2,1)S(1)}, bf16[1168,128]{1,0:T(8,128)(2,1)S(1)}, u32[]{:S(2)}, u32[]{:S(2)}) collective-permute-start(bf16[1168,128]{1,0:T(8,128)(2,1)S(1)} %pass_2_1.1), channel_id=1, source_target_pairs={{2,3},{6,7},{10,11},{14,15},{18,19},{22,23},{26,27},{30,31}} | collective-permute-start | bytes 897032 | tf_op jit(solution)/shard_map/ppermute | solution.py:681
  45.0 9.7 %copy-start = (f32[4,384]{1,0:T(4,128)S(1)}, f32[4,384]{1,0:T(4,128)}, u32[]{:S(2)}) copy-start(f32[4,384]{1,0:T(4,128)} %doping.1) | copy-start | bytes 18436

commit v11 on v10

--- a/solution.py
+++ b/solution.py
@@ -128,7 +128,7 @@
 
     def one(k, state):
         momentum, before = state
-        extra = counts[k] - 1
+        extra = counts[k, 0, 0] - 1
         take = jnp.logical_and(momentum == k, before + extra <= wanted)
         return (jnp.where(take, k + 1, momentum), jnp.where(take, before + extra, before))
 
@@ -689,7 +689,9 @@
         pltpu.VMEM((2 * orbitals, orbitals), BF16),
     ]
 
-    counts_all = lax.all_to_all(jnp.tile(counts, kt_size), "kt", 0, 0, tiled=True)
+    counts_all = gather_over(
+        jnp.broadcast_to(counts[:, None], (counts.shape[0], 128)), "kt"
+    )
     given = (constants, contact_slabs, onsite, hopping, potential_in, couple_base, couple_wave)
     pinned = [pltpu.with_memory_space_constraint(t, pltpu.HBM) for t in given]
     block, density, *loaded = vmem_call(

time: 55.9 us -> 55.5 us (level)
  no operation moved by 1% of the time
where the time goes in v11:
time: 55.5 us; the launch traced here: 55.1 us
  waiting for transfers between devices  19.1 us (34%)
  Pallas kernels  17.2 us (31%)
  starting transfers between devices  9.38 us (17%)
  blocking collectives  7.31 us (13%)
  between operations  1.52 us (3%)
  local copies, waits for them, and re-layouts  0.65 us (1%)
    pallas_call x14, Pallas kernels, vmem_call(): pl.pallas_call(kernel, out_shape=tuple(outs), in_specs=in_specs, out_spec...  17.2 us
    ppermute x6, waiting for transfers between devices, forward(): return lax.ppermute(block, 'en', [(stage, stage + 1)])  16.4 us
    all_to_all x1, blocking collectives, gather_over(): return lax.all_to_all(copies, axis, 0, 0)  7.31 us
    ppermute x6, starting transfers between devices, forward(): return lax.ppermute(block, 'en', [(stage, stage + 1)])  5.66 us
    all_to_all x1, starting transfers between devices, gather_over(): return lax.all_to_all(copies, axis, 0, 0)  3.72 us
    all_to_all x1, waiting for transfers between devices, gather_over(): return lax.all_to_all(copies, axis, 0, 0)  2.75 us
  transfers between devices with their start and end apart: 7, of which 3 were waited for; matrix products, arithmetic and copies ran while one was open for 0% of the time, Pallas kernels for 25%

profile of v11, /device:TPU:24, one launch (start us, length us, event | category | flops | bytes accessed | tf_op | source)
XLA Modules:
  0.0 55.1 jit_solution(6883468061560367712)
XLA Ops:
  1.3 0.6 %broadcast_in_dim_broadcast_in_dim_broadcast_in_dim.8 = s32[8,1,128]{2,1,0:T(1,128)} broadcast(s32[]{:T(128)} %bitcast.1), dimensions={} | broadcast | bytes 4100 | tf_op jit(solution)/shard_map/broadcast_in_dim;broadcast_in_dim;broadcast_in_dim | solution.py:654
  1.9 3.7 %all-to-all-start = ((s32[8,1,128]{2,1,0:T(1,128)}), s32[8,1,128]{2,1,0:T(1,128)S(1)}, u32[]{:S(2)}, u32[]{:S(2)}) async-start(s32[8,1,128]{2,1,0:T(1,128)} %broadcast_in_dim_broadcast_in_dim_broadcast_in_dim.8), calls=%async_computation | async-start | bytes 8192 | tf_op jit(solution)/shard_map/all_to_all | solution.py:655
  5.6 0.0 copy-start
  5.6 0.0 copy-start.1
  5.6 0.0 copy-start.2
  5.6 0.0 copy-start.4
  5.6 0.0 copy-start.5
  5.6 1.8 %lead.1 = (bf16[1168,128]{1,0:T(8,128)(2,1)S(1)}, f32[4,384]{1,0:T(4,128)S(1)}, bf16[4,384,384]{2,1,0:T(8,128)(2,1)S(1)}, bf16[4,384,384]{2,1,0:T(8,128)(2,1)S(1)}) custom-call(f32[12]{0:T(128)} %constant.2.clone.constants_hbm.constants_ref, s32[2]{0:T(128)} %contact_ref.4, f32[4,384]{1,0:T(4,128)} %onsite.4, f32[4,384]{1,0:T(4,128)} %hopping.4, ...), custom_call_target="tpu_custom_call" | custom-call | flops 1358954496 | bytes 2097152 | tf_op jit(solution)/shard_map/lead/pallas_call | solution.py:609
  7.4 2.8 %all-to-all-done.counts_ref = s32[8,1,128]{2,1,0:T(1,128)S(1)} async-done(((s32[8,1,128]{2,1,0:T(1,128)}), s32[8,1,128]{2,1,0:T(1,128)S(1)}, u32[]{:S(2)}, u32[]{:S(2)}) %all-to-all-start) | async-done | bytes 4128 | tf_op jit(solution)/shard_map/all_to_all | solution.py:655
  10.2 0.0 copy-done
  10.2 0.0 copy-done.1
  10.2 0.0 copy-done.2
  10.2 0.0 copy-done.4
  10.2 0.0 copy-done.5
  10.2 0.1 begin_0.1
  10.3 0.7 %collective-permute-start = (bf16[1168,128]{1,0:T(8,128)(2,1)S(1)}, bf16[1168,128]{1,0:T(8,128)(2,1)S(1)}, u32[]{:S(2)}, u32[]{:S(2)}) collective-permute-start(bf16[1168,128]{1,0:T(8,128)(2,1)S(1)} %get-tuple-element.61), channel_id=1, source_target_pairs={{0,1},{4,5},{8,9},{12,13},{16,17},{20,21},{24,25},{28,29}} | collective-permute-start | bytes 897032 | tf_op jit(solution)/shard_map/ppermute | solution.py:681
  11.0 0.7 %collective-permute-start.3 = (bf16[1168,128]{1,0:T(8,128)(2,1)S(1)}, bf16[1168,128]{1,0:T(8,128)(2,1)S(1)}, u32[]{:S(2)}, u32[]{:S(2)}) collective-permute-start(bf16[1168,128]{1,0:T(8,128)(2,1)S(1)} %get-tuple-element.47), channel_id=1, source_target_pairs={{0,1},{4,5},{8,9},{12,13},{16,17},{20,21},{24,25},{28,29}} | collective-permute-start | bytes 897032 | tf_op jit(solution)/shard_map/ppermute | solution.py:681
  11.7 1.6 %prepare.1 = (bf16[4,384,384]{2,1,0:T(8,128)(2,1)S(1)}, f32[9,8,384]{2,1,0:T(8,128)S(1)}, bf16[4,384,384]{2,1,0:T(8,128)(2,1)S(1)}, f32[9,8,384]{2,1,0:T(8,128)S(1)}) custom-call(f32[12]{0:T(128)S(1)} %copy-done.5, s32[2]{0:T(128)S(1)} %copy-done.4, s32[8,1,128]{2,1,0:T(1,128)S(1)} %all-to-all-done.counts_ref, f32[4,384]{1,0:T(4,128)S(1)} %copy-done, ...), custom_call_target="tpu_custom_call" | custom-call | flops 28311552 | bytes 65536 | tf_op jit(solution)/shard_map/prepare/pallas_call | solution.py:609
  13.3 4.0 %operator_0.1 = (bf16[1536,768]{1,0:T(8,128)(2,1)S(1)}, bf16[768,768]{1,0:T(8,128)(2,1)S(1)}, f32[1536,128]{1,0:T(8,128)S(1)}, f32[4,384]{1,0:T(4,128)S(1)}) custom-call(bf16[4,384,384]{2,1,0:T(8,128)(2,1)S(1)} %get-tuple-element.56.couple, f32[9,8,384]{2,1,0:T(8,128)S(1)} %get-tuple-element.57.entry.refs_0_), custom_call_target="tpu_custom_call" | custom-call | flops 28311552 | bytes 65536 | tf_op jit(solution)/shard_map/operator_0/pallas_call | solution.py:609
  17.3 0.0 collective-permute-done.refs_3_
  17.3 0.7 %collective-permute-start.1 = (bf16[1168,128]{1,0:T(8,128)(2,1)S(1)}, bf16[1168,128]{1,0:T(8,128)(2,1)S(1)}, u32[]{:S(2)}, u32[]{:S(2)}) collective-permute-start(bf16[1168,128]{1,0:T(8,128)(2,1)S(1)} %pass_1_0.1), channel_id=1, source_target_pairs={{1,2},{5,6},{9,10},{13,14},{17,18},{21,22},{25,26},{29,30}} | collective-permute-start | bytes 897032 | tf_op jit(solution)/shard_map/ppermute | solution.py:681
  18.0 3.8 %operator_1.1 = (bf16[1536,768]{1,0:T(8,128)(2,1)S(1)}, bf16[768,768]{1,0:T(8,128)(2,1)S(1)}, f32[1536,128]{1,0:T(8,128)S(1)}, f32[4,384]{1,0:T(4,128)S(1)}) custom-call(bf16[4,384,384]{2,1,0:T(8,128)(2,1)S(1)} %get-tuple-element.62.couple, f32[9,8,384]{2,1,0:T(8,128)S(1)} %get-tuple-element.63.entry.refs_0_), custom_call_target="tpu_custom_call" | custom-call | flops 28311552 | bytes 65536 | tf_op jit(solution)/shard_map/operator_1/pallas_call | solution.py:609
  21.8 0.0 collective-permute-done.3.refs_3_
  21.8 0.7 %collective-permute-start.4 = (bf16[1168,128]{1,0:T(8,128)(2,1)S(1)}, bf16[1168,128]{1,0:T(8,128)(2,1)S(1)}, u32[]{:S(2)}, u32[]{:S(2)}) collective-permute-start(bf16[1168,128]{1,0:T(8,128)(2,1)S(1)} %pass_1_1.1), channel_id=1, source_target_pairs={{1,2},{5,6},{9,10},{13,14},{17,18},{21,22},{25,26},{29,30}} | collective-permute-start | bytes 897032 | tf_op jit(solution)/shard_map/ppermute | solution.py:681
  22.5 0.0 collective-permute-done.1.refs_3_.refs_4_
  22.5 0.0 copy-start.6
  22.5 1.4 %collective-permute-start.2 = (bf16[1168,128]{1,0:T(8,128)(2,1)S(1)}, bf16[1168,128]{1,0:T(8,128)(2,1)S(1)}, u32[]{:S(2)}, u32[]{:S(2)}) collective-permute-start(bf16[1168,128]{1,0:T(8,128)(2,1)S(1)} %pass_2_0.1), channel_id=1, source_target_pairs={{2,3},{6,7},{10,11},{14,15},{18,19},{22,23},{26,27},{30,31}} | collective-permute-start | bytes 897032 | tf_op jit(solution)/shard_map/ppermute | solution.py:681
  24.0 0.0 collective-permute-done.4.refs_3_.refs_4_
  24.0 1.5 %collective-permute-start.5 = (bf16[1168,128]{1,0:T(8,128)(2,1)S(1)}, bf16[1168,128]{1,0:T(8,128)(2,1)S(1)}, u32[]{:S(2)}, u32[]{:S(2)}) collective-permute-start(bf16[1168,128]{1,0:T(8,128)(2,1)S(1)} %pass_2_1.1), channel_id=1, source_target_pairs={{2,3},{6,7},{10,11},{14,15},{18,19},{22,23},{26,27},{30,31}} | collective-permute-start | bytes 897032 | tf_op jit(solution)/shard_map/ppermute | solution.py:681
  25.5 0.0 copy-done.6
  25.5 0.2 split_inverse.1
  25.8 13.3 %collective-permute-done.2.refs_5_ = bf16[1168,128]{1,0:T(8,128)(2,1)S(1)} collective-permute-done((bf16[1168,128]{1,0:T(8,128)(2,1)S(1)}, bf16[1168,128]{1,0:T(8,128)(2,1)S(1)}, u32[]{:S(2)}, u32[]{:S(2)}) %collective-permute-start.2) | collective-permute-done | bytes 299040 | tf_op jit(solution)/shard_map/ppermute | solution.py:681
  39.1 2.4 %density_0.1.refs_2_ = f32[4,384]{1,0:T(4,128)S(1)} custom-call(bf16[1536,768]{1,0:T(8,128)(2,1)S(1)} %get-tuple-element.59.refs_1_.carriers, f32[9,8,384]{2,1,0:T(8,128)S(1)} %get-tuple-element.57.entry.refs_0_, f32[4,384]{1,0:T(4,128)S(1)} %get-tuple-element.66.refs_1_, f32[4,384]{1,0:T(4,128)S(1)} %get-tuple-element.67.refs_2_, ...), custom_call_target="tpu_custom_call", output_to_operand_aliasing={{}: (3, {})} | custom-call | flops 1811939328 | bytes 2097152 | tf_op jit(solution)/shard_map/density_0/pallas_call | solution.py:609
  41.5 3.0 %collective-permute-done.5.refs_5_ = bf16[1168,128]{1,0:T(8,128)(2,1)S(1)} collective-permute-done((bf16[1168,128]{1,0:T(8,128)(2,1)S(1)}, bf16[1168,128]{1,0:T(8,128)(2,1)S(1)}, u32[]{:S(2)}, u32[]{:S(2)}) %collective-permute-start.5) | collective-permute-done | bytes 299040 | tf_op jit(solution)/shard_map/ppermute | solution.py:681
  44.5 0.0 copy-start.3
  44.5 2.4 %density_1.1 = f32[4,384]{1,0:T(4,128)S(1)} custom-call(bf16[1536,768]{1,0:T(8,128)(2,1)S(1)} %get-tuple-element.64.refs_1_.carriers, f32[9,8,384]{2,1,0:T(8,128)S(1)} %get-tuple-element.63.entry.refs_0_, f32[4,384]{1,0:T(4,128)S(1)} %get-tuple-element.65.refs_1_, f32[4,384]{1,0:T(4,128)S(1)} %density_0.1.refs_2_, ...), custom_call_target="tpu_custom_call", output_to_operand_aliasing={{}: (3, {})} | custom-call | flops 1811939328 | bytes 2097152 | tf_op jit(solution)/shard_map/density_1/pallas_call | solution.py:609
  47.0 7.3 %all_to_all.10.gathered = f32[8,4,384]{2,1,0:T(4,128)S(1)} all-to-all(f32[8,4,384]{2,1,0:T(4,128)S(1)} %broadcast_in_dim.2), channel_id=1, replica_groups=mesh['kt'=8,'en'=4] {'kt'}, dimensions={0} | all-to-all | bytes 98304 | tf_op jit(solution)/shard_map/all_to_all | solution.py:655
  54.3 0.0 copy-done.3
  54.3 0.9 %last.1 = (f32[4,384]{1,0:T(4,128)}, f32[4,384]{1,0:T(4,128)}) custom-call(f32[8,4,384]{2,1,0:T(4,128)S(1)} %all_to_all.10.gathered, f32[4,384]{1,0:T(4,128)S(1)} %copy-done.3, bf16[384,384]{1,0:T(8,128)(2,1)S(1)} %get-tuple-element.75.high, bf16[384,384]{1,0:T(8,128)(2,1)S(1)} %get-tuple-element.76.middle, bf16[384,384]{1,0:T(8,128)(2,1)S(1)} %get-tuple-element.77.low), custom_call_target="tpu_custom_call" | custom-call | flops 113246208 | bytes 2097152 | tf_op jit(solution)/shard_map/last/pallas_call | solution.py:609
  (6 shorter events, 0.1 us)
Async XLA Ops:
  1.9 8.3 %all-to-all-start = ((s32[8,1,128]{2,1,0:T(1,128)}), s32[8,1,128]{2,1,0:T(1,128)S(1)}, u32[]{:S(2)}, u32[]{:S(2)}) async-start(s32[8,1,128]{2,1,0:T(1,128)} %broadcast_in_dim_broadcast_in_dim_broadcast_in_dim.8), calls=%async_computation | async-start | bytes 8192 | tf_op jit(solution)/shard_map/all_to_all | solution.py:655
  5.6 4.6 %copy-start = (f32[4,384]{1,0:T(4,128)S(1)}, f32[4,384]{1,0:T(4,128)}, u32[]{:S(2)}) copy-start(f32[4,384]{1,0:T(4,128)} %onsite.4) | copy-start | bytes 18436
  5.6 4.6 %copy-start.1 = (f32[4,384]{1,0:T(4,128)S(1)}, f32[4,384]{1,0:T(4,128)}, u32[]{:S(2)}) copy-start(f32[4,384]{1,0:T(4,128)} %hopping.4) | copy-start | bytes 18436
  5.6 4.6 %copy-start.2 = (f32[4,384]{1,0:T(4,128)S(1)}, f32[4,384]{1,0:T(4,128)}, u32[]{:S(2)}) copy-start(f32[4,384]{1,0:T(4,128)} %potential.4) | copy-start | bytes 18436
  5.6 4.6 %copy-start.4 = (s32[2]{0:T(128)S(1)}, s32[2]{0:T(128)}, u32[]{:S(2)}) copy-start(s32[2]{0:T(128)} %contact_ref.4) | copy-start | bytes 28
  5.6 4.6 %copy-start.5 = (f32[12]{0:T(128)S(1)}, f32[12]{0:T(128)}, u32[]{:S(2)}) copy-start(f32[12]{0:T(128)} %constant.2.clone.constants_hbm.constants_ref) | copy-start | bytes 148
  10.3 7.0 %collective-permute-start = (bf16[1168,128]{1,0:T(8,128)(2,1)S(1)}, bf16[1168,128]{1,0:T(8,128)(2,1)S(1)}, u32[]{:S(2)}, u32[]{:S(2)}) collective-permute-start(bf16[1168,128]{1,0:T(8,128)(2,1)S(1)} %get-tuple-element.61), channel_id=1, source_target_pairs={{0,1},{4,5},{8,9},{12,13},{16,17},{20,21},{24,25},{28,29}} | collective-permute-start | bytes 897032 | tf_op jit(solution)/shard_map/ppermute | solution.py:681
  11.0 10.8 %collective-permute-start.3 = (bf16[1168,128]{1,0:T(8,128)(2,1)S(1)}, bf16[1168,128]{1,0:T(8,128)(2,1)S(1)}, u32[]{:S(2)}, u32[]{:S(2)}) collective-permute-start(bf16[1168,128]{1,0:T(8,128)(2,1)S(1)} %get-tuple-element.47), channel_id=1, source_target_pairs={{0,1},{4,5},{8,9},{12,13},{16,17},{20,21},{24,25},{28,29}} | collective-permute-start | bytes 897032 | tf_op jit(solution)/shard_map/ppermute | solution.py:681
  17.3 5.2 %collective-permute-start.1 = (bf16[1168,128]{1,0:T(8,128)(2,1)S(1)}, bf16[1168,128]{1,0:T(8,128)(2,1)S(1)}, u32[]{:S(2)}, u32[]{:S(2)}) collective-permute-start(bf16[1168,128]{1,0:T(8,128)(2,1)S(1)} %pass_1_0.1), channel_id=1, source_target_pairs={{1,2},{5,6},{9,10},{13,14},{17,18},{21,22},{25,26},{29,30}} | collective-permute-start | bytes 897032 | tf_op jit(solution)/shard_map/ppermute | solution.py:681
  21.8 2.2 %collective-permute-start.4 = (bf16[1168,128]{1,0:T(8,128)(2,1)S(1)}, bf16[1168,128]{1,0:T(8,128)(2,1)S(1)}, u32[]{:S(2)}, u32[]{:S(2)}) collective-permute-start(bf16[1168,128]{1,0:T(8,128)(2,1)S(1)} %pass_1_1.1), channel_id=1, source_target_pairs={{1,2},{5,6},{9,10},{13,14},{17,18},{21,22},{25,26},{29,30}} | collective-permute-start | bytes 897032 | tf_op jit(solution)/shard_map/ppermute | solution.py:681
  22.5 3.0 %copy-start.6 = (f32[384,384]{1,0:T(8,128)S(1)}, f32[384,384]{1,0:T(8,128)}, u32[]{:S(2)}) copy-start(f32[384,384]{1,0:T(8,128)} %inverse) | copy-start | bytes 1769476
  22.5 16.6 %collective-permute-start.2 = (bf16[1168,128]{1,0:T(8,128)(2,1)S(1)}, bf16[1168,128]{1,0:T(8,128)(2,1)S(1)}, u32[]{:S(2)}, u32[]{:S(2)}) collective-permute-start(bf16[1168,128]{1,0:T(8,128)(2,1)S(1)} %pass_2_0.1), channel_id=1, source_target_pairs={{2,3},{6,7},{10,11},{14,15},{18,19},{22,23},{26,27},{30,31}} | collective-permute-start | bytes 897032 | tf_op jit(solution)/shard_map/ppermute | solution.py:681
  24.0 20.5 %collective-permute-start.5 = (bf16[1168,128]{1,0:T(8,128)(2,1)S(1)}, bf16[1168,128]{1,0:T(8,128)(2,1)S(1)}, u32[]{:S(2)}, u32[]{:S(2)}) collective-permute-start(bf16[1168,128]{1,0:T(8,128)(2,1)S(1)} %pass_2_1.1), channel_id=1, source_target_pairs={{2,3},{6,7},{10,11},{14,15},{18,19},{22,23},{26,27},{30,31}} | collective-permute-start | bytes 897032 | tf_op jit(solution)/shard_map/ppermute | solution.py:681
  44.5 9.7 %copy-start.3 = (f32[4,384]{1,0:T(4,128)S(1)}, f32[4,384]{1,0:T(4,128)}, u32[]{:S(2)}) copy-start(f32[4,384]{1,0:T(4,128)} %doping.1) | copy-start | bytes 18436

commit v12 on v11

--- a/solution.py
+++ b/solution.py
@@ -690,7 +690,7 @@
     ]
 
     counts_all = gather_over(
-        jnp.broadcast_to(counts[:, None], (counts.shape[0], 128)), "kt"
+        jnp.broadcast_to(counts[:, None], (counts.shape[0], 1)), "kt"
     )
     given = (constants, contact_slabs, onsite, hopping, potential_in, couple_base, couple_wave)
     pinned = [pltpu.with_memory_space_constraint(t, pltpu.HBM) for t in given]

time: 55.5 us -> 55.5 us (level)
    another operation x1 -> x0, local copies, waits for them, and re-layouts: 0.6 us -> none  [gather_over(): jnp.broadcast_to(values[None], (lax.axis_size(axis),) + values.shape)]
    broadcast_in_dim x1 -> x2, local copies, waits for them, and re-layouts: 0.01 us -> 0.61 us  [gather_over(): jnp.broadcast_to(values[None], (lax.axis_size(axis),) + values.shape)]
where the time goes in v12:
time: 55.5 us; the launch traced here: 55.1 us
  waiting for transfers between devices  19.1 us (34%)
  Pallas kernels  17.2 us (31%)
  starting transfers between devices  9.38 us (17%)
  blocking collectives  7.31 us (13%)
  between operations  1.52 us (3%)
  local copies, waits for them, and re-layouts  0.65 us (1%)
    pallas_call x14, Pallas kernels, vmem_call(): pl.pallas_call(kernel, out_shape=tuple(outs), in_specs=in_specs, out_spec...  17.2 us
    ppermute x6, waiting for transfers between devices, forward(): return lax.ppermute(block, 'en', [(stage, stage + 1)])  16.4 us
    all_to_all x1, blocking collectives, gather_over(): return lax.all_to_all(copies, axis, 0, 0)  7.31 us
    ppermute x6, starting transfers between devices, forward(): return lax.ppermute(block, 'en', [(stage, stage + 1)])  5.66 us
    all_to_all x1, starting transfers between devices, gather_over(): return lax.all_to_all(copies, axis, 0, 0)  3.72 us
    all_to_all x1, waiting for transfers between devices, gather_over(): return lax.all_to_all(copies, axis, 0, 0)  2.75 us
  transfers between devices with their start and end apart: 7, of which 3 were waited for; matrix products, arithmetic and copies ran while one was open for 0% of the time, Pallas kernels for 25%

profile of v12, /device:TPU:24, one launch (start us, length us, event | category | flops | bytes accessed | tf_op | source)
XLA Modules:
  0.0 55.1 jit_solution(6883468061560367712)
XLA Ops:
  1.3 0.6 %broadcast_in_dim.14 = s32[8,1,1]{2,1,0:T(1,128)} broadcast(s32[]{:T(128)} %bitcast.1), dimensions={} | broadcast | bytes 36 | tf_op jit(solution)/shard_map/broadcast_in_dim | solution.py:654
  1.9 3.7 %all-to-all-start = ((s32[8,1,1]{2,1,0:T(1,128)}), s32[8,1,1]{2,1,0:T(1,128)S(1)}, u32[]{:S(2)}, u32[]{:S(2)}) async-start(s32[8,1,1]{2,1,0:T(1,128)} %broadcast_in_dim.14), calls=%async_computation | async-start | bytes 8192 | tf_op jit(solution)/shard_map/all_to_all | solution.py:655
  5.6 0.0 copy-start
  5.6 0.0 copy-start.1
  5.6 0.0 copy-start.2
  5.6 0.0 copy-start.4
  5.6 0.0 copy-start.5
  5.6 1.8 %lead.1 = (bf16[1168,128]{1,0:T(8,128)(2,1)S(1)}, f32[4,384]{1,0:T(4,128)S(1)}, bf16[4,384,384]{2,1,0:T(8,128)(2,1)S(1)}, bf16[4,384,384]{2,1,0:T(8,128)(2,1)S(1)}) custom-call(f32[12]{0:T(128)} %constant.2.clone.constants_hbm.constants_ref, s32[2]{0:T(128)} %contact_ref.4, f32[4,384]{1,0:T(4,128)} %onsite.4, f32[4,384]{1,0:T(4,128)} %hopping.4, ...), custom_call_target="tpu_custom_call" | custom-call | flops 1358954496 | bytes 2097152 | tf_op jit(solution)/shard_map/lead/pallas_call | solution.py:609
  7.4 2.8 %all-to-all-done.counts_ref = s32[8,1,1]{2,1,0:T(1,128)S(1)} async-done(((s32[8,1,1]{2,1,0:T(1,128)}), s32[8,1,1]{2,1,0:T(1,128)S(1)}, u32[]{:S(2)}, u32[]{:S(2)}) %all-to-all-start) | async-done | bytes 64 | tf_op jit(solution)/shard_map/all_to_all | solution.py:655
  10.2 0.0 copy-done
  10.2 0.0 copy-done.1
  10.2 0.0 copy-done.2
  10.2 0.0 copy-done.4
  10.2 0.0 copy-done.5
  10.2 0.1 begin_0.1
  10.3 0.7 %collective-permute-start = (bf16[1168,128]{1,0:T(8,128)(2,1)S(1)}, bf16[1168,128]{1,0:T(8,128)(2,1)S(1)}, u32[]{:S(2)}, u32[]{:S(2)}) collective-permute-start(bf16[1168,128]{1,0:T(8,128)(2,1)S(1)} %get-tuple-element.61), channel_id=1, source_target_pairs={{0,1},{4,5},{8,9},{12,13},{16,17},{20,21},{24,25},{28,29}} | collective-permute-start | bytes 897032 | tf_op jit(solution)/shard_map/ppermute | solution.py:681
  11.0 0.7 %collective-permute-start.3 = (bf16[1168,128]{1,0:T(8,128)(2,1)S(1)}, bf16[1168,128]{1,0:T(8,128)(2,1)S(1)}, u32[]{:S(2)}, u32[]{:S(2)}) collective-permute-start(bf16[1168,128]{1,0:T(8,128)(2,1)S(1)} %get-tuple-element.47), channel_id=1, source_target_pairs={{0,1},{4,5},{8,9},{12,13},{16,17},{20,21},{24,25},{28,29}} | collective-permute-start | bytes 897032 | tf_op jit(solution)/shard_map/ppermute | solution.py:681
  11.7 1.6 %prepare.1 = (bf16[4,384,384]{2,1,0:T(8,128)(2,1)S(1)}, f32[9,8,384]{2,1,0:T(8,128)S(1)}, bf16[4,384,384]{2,1,0:T(8,128)(2,1)S(1)}, f32[9,8,384]{2,1,0:T(8,128)S(1)}) custom-call(f32[12]{0:T(128)S(1)} %copy-done.5, s32[2]{0:T(128)S(1)} %copy-done.4, s32[8,1,1]{2,1,0:T(1,128)S(1)} %all-to-all-done.counts_ref, f32[4,384]{1,0:T(4,128)S(1)} %copy-done, ...), custom_call_target="tpu_custom_call" | custom-call | flops 28311552 | bytes 65536 | tf_op jit(solution)/shard_map/prepare/pallas_call | solution.py:609
  13.3 4.0 %operator_0.1 = (bf16[1536,768]{1,0:T(8,128)(2,1)S(1)}, bf16[768,768]{1,0:T(8,128)(2,1)S(1)}, f32[1536,128]{1,0:T(8,128)S(1)}, f32[4,384]{1,0:T(4,128)S(1)}) custom-call(bf16[4,384,384]{2,1,0:T(8,128)(2,1)S(1)} %get-tuple-element.56.couple, f32[9,8,384]{2,1,0:T(8,128)S(1)} %get-tuple-element.57.entry.refs_0_), custom_call_target="tpu_custom_call" | custom-call | flops 28311552 | bytes 65536 | tf_op jit(solution)/shard_map/operator_0/pallas_call | solution.py:609
  17.3 0.0 collective-permute-done.refs_3_
  17.3 0.7 %collective-permute-start.1 = (bf16[1168,128]{1,0:T(8,128)(2,1)S(1)}, bf16[1168,128]{1,0:T(8,128)(2,1)S(1)}, u32[]{:S(2)}, u32[]{:S(2)}) collective-permute-start(bf16[1168,128]{1,0:T(8,128)(2,1)S(1)} %pass_1_0.1), channel_id=1, source_target_pairs={{1,2},{5,6},{9,10},{13,14},{17,18},{21,22},{25,26},{29,30}} | collective-permute-start | bytes 897032 | tf_op jit(solution)/shard_map/ppermute | solution.py:681
  18.0 3.8 %operator_1.1 = (bf16[1536,768]{1,0:T(8,128)(2,1)S(1)}, bf16[768,768]{1,0:T(8,128)(2,1)S(1)}, f32[1536,128]{1,0:T(8,128)S(1)}, f32[4,384]{1,0:T(4,128)S(1)}) custom-call(bf16[4,384,384]{2,1,0:T(8,128)(2,1)S(1)} %get-tuple-element.62.couple, f32[9,8,384]{2,1,0:T(8,128)S(1)} %get-tuple-element.63.entry.refs_0_), custom_call_target="tpu_custom_call" | custom-call | flops 28311552 | bytes 65536 | tf_op jit(solution)/shard_map/operator_1/pallas_call | solution.py:609
  21.8 0.0 collective-permute-done.3.refs_3_
  21.8 0.7 %collective-permute-start.4 = (bf16[1168,128]{1,0:T(8,128)(2,1)S(1)}, bf16[1168,128]{1,0:T(8,128)(2,1)S(1)}, u32[]{:S(2)}, u32[]{:S(2)}) collective-permute-start(bf16[1168,128]{1,0:T(8,128)(2,1)S(1)} %pass_1_1.1), channel_id=1, source_target_pairs={{1,2},{5,6},{9,10},{13,14},{17,18},{21,22},{25,26},{29,30}} | collective-permute-start | bytes 897032 | tf_op jit(solution)/shard_map/ppermute | solution.py:681
  22.5 0.0 collective-permute-done.1.refs_3_.refs_4_
  22.5 0.0 copy-start.6
  22.5 1.4 %collective-permute-start.2 = (bf16[1168,128]{1,0:T(8,128)(2,1)S(1)}, bf16[1168,128]{1,0:T(8,128)(2,1)S(1)}, u32[]{:S(2)}, u32[]{:S(2)}) collective-permute-start(bf16[1168,128]{1,0:T(8,128)(2,1)S(1)} %pass_2_0.1), channel_id=1, source_target_pairs={{2,3},{6,7},{10,11},{14,15},{18,19},{22,23},{26,27},{30,31}} | collective-permute-start | bytes 897032 | tf_op jit(solution)/shard_map/ppermute | solution.py:681
  24.0 0.0 collective-permute-done.4.refs_3_.refs_4_
  24.0 1.5 %collective-permute-start.5 = (bf16[1168,128]{1,0:T(8,128)(2,1)S(1)}, bf16[1168,128]{1,0:T(8,128)(2,1)S(1)}, u32[]{:S(2)}, u32[]{:S(2)}) collective-permute-start(bf16[1168,128]{1,0:T(8,128)(2,1)S(1)} %pass_2_1.1), channel_id=1, source_target_pairs={{2,3},{6,7},{10,11},{14,15},{18,19},{22,23},{26,27},{30,31}} | collective-permute-start | bytes 897032 | tf_op jit(solution)/shard_map/ppermute | solution.py:681
  25.5 0.0 copy-done.6
  25.5 0.2 split_inverse.1
  25.8 13.3 %collective-permute-done.2.refs_5_ = bf16[1168,128]{1,0:T(8,128)(2,1)S(1)} collective-permute-done((bf16[1168,128]{1,0:T(8,128)(2,1)S(1)}, bf16[1168,128]{1,0:T(8,128)(2,1)S(1)}, u32[]{:S(2)}, u32[]{:S(2)}) %collective-permute-start.2) | collective-permute-done | bytes 299040 | tf_op jit(solution)/shard_map/ppermute | solution.py:681
  39.1 2.4 %density_0.1.refs_2_ = f32[4,384]{1,0:T(4,128)S(1)} custom-call(bf16[1536,768]{1,0:T(8,128)(2,1)S(1)} %get-tuple-element.59.refs_1_.carriers, f32[9,8,384]{2,1,0:T(8,128)S(1)} %get-tuple-element.57.entry.refs_0_, f32[4,384]{1,0:T(4,128)S(1)} %get-tuple-element.66.refs_1_, f32[4,384]{1,0:T(4,128)S(1)} %get-tuple-element.67.refs_2_, ...), custom_call_target="tpu_custom_call", output_to_operand_aliasing={{}: (3, {})} | custom-call | flops 1811939328 | bytes 2097152 | tf_op jit(solution)/shard_map/density_0/pallas_call | solution.py:609
  41.5 3.0 %collective-permute-done.5.refs_5_ = bf16[1168,128]{1,0:T(8,128)(2,1)S(1)} collective-permute-done((bf16[1168,128]{1,0:T(8,128)(2,1)S(1)}, bf16[1168,128]{1,0:T(8,128)(2,1)S(1)}, u32[]{:S(2)}, u32[]{:S(2)}) %collective-permute-start.5) | collective-permute-done | bytes 299040 | tf_op jit(solution)/shard_map/ppermute | solution.py:681
  44.5 0.0 copy-start.3
  44.5 2.4 %density_1.1 = f32[4,384]{1,0:T(4,128)S(1)} custom-call(bf16[1536,768]{1,0:T(8,128)(2,1)S(1)} %get-tuple-element.64.refs_1_.carriers, f32[9,8,384]{2,1,0:T(8,128)S(1)} %get-tuple-element.63.entry.refs_0_, f32[4,384]{1,0:T(4,128)S(1)} %get-tuple-element.65.refs_1_, f32[4,384]{1,0:T(4,128)S(1)} %density_0.1.refs_2_, ...), custom_call_target="tpu_custom_call", output_to_operand_aliasing={{}: (3, {})} | custom-call | flops 1811939328 | bytes 2097152 | tf_op jit(solution)/shard_map/density_1/pallas_call | solution.py:609
  47.0 7.3 %all_to_all.10.gathered = f32[8,4,384]{2,1,0:T(4,128)S(1)} all-to-all(f32[8,4,384]{2,1,0:T(4,128)S(1)} %broadcast_in_dim.15), channel_id=1, replica_groups=mesh['kt'=8,'en'=4] {'kt'}, dimensions={0} | all-to-all | bytes 98304 | tf_op jit(solution)/shard_map/all_to_all | solution.py:655
  54.3 0.0 copy-done.3
  54.3 0.9 %last.1 = (f32[4,384]{1,0:T(4,128)}, f32[4,384]{1,0:T(4,128)}) custom-call(f32[8,4,384]{2,1,0:T(4,128)S(1)} %all_to_all.10.gathered, f32[4,384]{1,0:T(4,128)S(1)} %copy-done.3, bf16[384,384]{1,0:T(8,128)(2,1)S(1)} %get-tuple-element.75.high, bf16[384,384]{1,0:T(8,128)(2,1)S(1)} %get-tuple-element.76.middle, bf16[384,384]{1,0:T(8,128)(2,1)S(1)} %get-tuple-element.77.low), custom_call_target="tpu_custom_call" | custom-call | flops 113246208 | bytes 2097152 | tf_op jit(solution)/shard_map/last/pallas_call | solution.py:609
  (6 shorter events, 0.1 us)
Async XLA Ops:
  1.9 8.3 %all-to-all-start = ((s32[8,1,1]{2,1,0:T(1,128)}), s32[8,1,1]{2,1,0:T(1,128)S(1)}, u32[]{:S(2)}, u32[]{:S(2)}) async-start(s32[8,1,1]{2,1,0:T(1,128)} %broadcast_in_dim.14), calls=%async_computation | async-start | bytes 8192 | tf_op jit(solution)/shard_map/all_to_all | solution.py:655
  5.6 4.6 %copy-start = (f32[4,384]{1,0:T(4,128)S(1)}, f32[4,384]{1,0:T(4,128)}, u32[]{:S(2)}) copy-start(f32[4,384]{1,0:T(4,128)} %onsite.4) | copy-start | bytes 18436
  5.6 4.6 %copy-start.1 = (f32[4,384]{1,0:T(4,128)S(1)}, f32[4,384]{1,0:T(4,128)}, u32[]{:S(2)}) copy-start(f32[4,384]{1,0:T(4,128)} %hopping.4) | copy-start | bytes 18436
  5.6 4.6 %copy-start.2 = (f32[4,384]{1,0:T(4,128)S(1)}, f32[4,384]{1,0:T(4,128)}, u32[]{:S(2)}) copy-start(f32[4,384]{1,0:T(4,128)} %potential.4) | copy-start | bytes 18436
  5.6 4.6 %copy-start.4 = (s32[2]{0:T(128)S(1)}, s32[2]{0:T(128)}, u32[]{:S(2)}) copy-start(s32[2]{0:T(128)} %contact_ref.4) | copy-start | bytes 28
  5.6 4.6 %copy-start.5 = (f32[12]{0:T(128)S(1)}, f32[12]{0:T(128)}, u32[]{:S(2)}) copy-start(f32[12]{0:T(128)} %constant.2.clone.constants_hbm.constants_ref) | copy-start | bytes 148
  10.3 7.0 %collective-permute-start = (bf16[1168,128]{1,0:T(8,128)(2,1)S(1)}, bf16[1168,128]{1,0:T(8,128)(2,1)S(1)}, u32[]{:S(2)}, u32[]{:S(2)}) collective-permute-start(bf16[1168,128]{1,0:T(8,128)(2,1)S(1)} %get-tuple-element.61), channel_id=1, source_target_pairs={{0,1},{4,5},{8,9},{12,13},{16,17},{20,21},{24,25},{28,29}} | collective-permute-start | bytes 897032 | tf_op jit(solution)/shard_map/ppermute | solution.py:681
  11.0 10.8 %collective-permute-start.3 = (bf16[1168,128]{1,0:T(8,128)(2,1)S(1)}, bf16[1168,128]{1,0:T(8,128)(2,1)S(1)}, u32[]{:S(2)}, u32[]{:S(2)}) collective-permute-start(bf16[1168,128]{1,0:T(8,128)(2,1)S(1)} %get-tuple-element.47), channel_id=1, source_target_pairs={{0,1},{4,5},{8,9},{12,13},{16,17},{20,21},{24,25},{28,29}} | collective-permute-start | bytes 897032 | tf_op jit(solution)/shard_map/ppermute | solution.py:681
  17.3 5.2 %collective-permute-start.1 = (bf16[1168,128]{1,0:T(8,128)(2,1)S(1)}, bf16[1168,128]{1,0:T(8,128)(2,1)S(1)}, u32[]{:S(2)}, u32[]{:S(2)}) collective-permute-start(bf16[1168,128]{1,0:T(8,128)(2,1)S(1)} %pass_1_0.1), channel_id=1, source_target_pairs={{1,2},{5,6},{9,10},{13,14},{17,18},{21,22},{25,26},{29,30}} | collective-permute-start | bytes 897032 | tf_op jit(solution)/shard_map/ppermute | solution.py:681
  21.8 2.2 %collective-permute-start.4 = (bf16[1168,128]{1,0:T(8,128)(2,1)S(1)}, bf16[1168,128]{1,0:T(8,128)(2,1)S(1)}, u32[]{:S(2)}, u32[]{:S(2)}) collective-permute-start(bf16[1168,128]{1,0:T(8,128)(2,1)S(1)} %pass_1_1.1), channel_id=1, source_target_pairs={{1,2},{5,6},{9,10},{13,14},{17,18},{21,22},{25,26},{29,30}} | collective-permute-start | bytes 897032 | tf_op jit(solution)/shard_map/ppermute | solution.py:681
  22.5 3.0 %copy-start.6 = (f32[384,384]{1,0:T(8,128)S(1)}, f32[384,384]{1,0:T(8,128)}, u32[]{:S(2)}) copy-start(f32[384,384]{1,0:T(8,128)} %inverse) | copy-start | bytes 1769476
  22.5 16.6 %collective-permute-start.2 = (bf16[1168,128]{1,0:T(8,128)(2,1)S(1)}, bf16[1168,128]{1,0:T(8,128)(2,1)S(1)}, u32[]{:S(2)}, u32[]{:S(2)}) collective-permute-start(bf16[1168,128]{1,0:T(8,128)(2,1)S(1)} %pass_2_0.1), channel_id=1, source_target_pairs={{2,3},{6,7},{10,11},{14,15},{18,19},{22,23},{26,27},{30,31}} | collective-permute-start | bytes 897032 | tf_op jit(solution)/shard_map/ppermute | solution.py:681
  24.0 20.5 %collective-permute-start.5 = (bf16[1168,128]{1,0:T(8,128)(2,1)S(1)}, bf16[1168,128]{1,0:T(8,128)(2,1)S(1)}, u32[]{:S(2)}, u32[]{:S(2)}) collective-permute-start(bf16[1168,128]{1,0:T(8,128)(2,1)S(1)} %pass_2_1.1), channel_id=1, source_target_pairs={{2,3},{6,7},{10,11},{14,15},{18,19},{22,23},{26,27},{30,31}} | collective-permute-start | bytes 897032 | tf_op jit(solution)/shard_map/ppermute | solution.py:681
  44.5 9.7 %copy-start.3 = (f32[4,384]{1,0:T(4,128)S(1)}, f32[4,384]{1,0:T(4,128)}, u32[]{:S(2)}) copy-start(f32[4,384]{1,0:T(4,128)} %doping.1) | copy-start | bytes 18436
